TPU v7x, 32 devices: a whole 2x2x4 slice. The times are simulated.
32 devices in a mesh: dp: 4 (over x, core), seq: 4 (over z), tensor: 2 (over y).
Axes of the slice: x: 2, y: 2, z: 4, core: 2. Of those that a mesh axis runs over, the one named last changes fastest.
Arguments:
- hidden: bfloat16 [8192, 1536], P(('dp', 'seq')), may hold values from -6 to 6
- cotangent: bfloat16 [8192, 1536], P(('dp', 'seq')), may hold values from -6 to 6
- segments: int32 [8192], P('dp'), may hold values from 0 to 2, as said below
- positions: int32 [8192], P('dp'), may hold values from 0 to 2047, as said below
- first_gain: bfloat16 [1536], replicated, may hold values from 0.5 to 1.5
- query_weight: bfloat16 [1536, 1536], P(('dp', 'seq'), 'tensor'), may hold values from -0.21875 to 0.21875
- query_bias: bfloat16 [1536], P('tensor'), may hold values from -3 to 3
- key_weight: bfloat16 [1536, 256], P(('dp', 'seq'), 'tensor'), may hold values from -0.15625 to 0.15625
- key_bias: bfloat16 [256], P('tensor'), may hold values from -3 to 3
- value_weight: bfloat16 [1536, 256], P(('dp', 'seq'), 'tensor'), may hold values from -0.15625 to 0.15625
- value_bias: bfloat16 [256], P('tensor'), may hold values from -3 to 3
- out_weight: bfloat16 [1536, 1536], P('tensor', ('dp', 'seq')), may hold values from -1.25 to 1.25
- second_gain: bfloat16 [1536], replicated, may hold values from 0.5 to 1.5
- gate_weight: bfloat16 [1536, 8960], P(('dp', 'seq'), 'tensor'), may hold values from -0.15625 to 0.15625
- up_weight: bfloat16 [1536, 8960], P(('dp', 'seq'), 'tensor'), may hold values from -0.15625 to 0.15625
- down_weight: bfloat16 [8960, 1536], P('tensor', ('dp', 'seq')), may hold values from -0.125 to 0.125
Outputs:
- output: bfloat16 [8192, 1536], P(('dp', 'seq'))
- input_gradient: bfloat16 [8192, 1536], P(('dp', 'seq'))
- first_gain_gradient: float32 [1536], replicated
- query_weight_gradient: float32 [1536, 1536], P(('dp', 'seq'), 'tensor')
- query_bias_gradient: float32 [1536], P('tensor')
- key_weight_gradient: float32 [1536, 256], P(('dp', 'seq'), 'tensor')
- key_bias_gradient: float32 [256], P('tensor')
- value_weight_gradient: float32 [1536, 256], P(('dp', 'seq'), 'tensor')
- value_bias_gradient: float32 [256], P('tensor')
- out_weight_gradient: float32 [1536, 1536], P('tensor', ('dp', 'seq'))
- second_gain_gradient: float32 [1536], replicated
- gate_weight_gradient: float32 [1536, 8960], P(('dp', 'seq'), 'tensor')
- up_weight_gradient: float32 [1536, 8960], P(('dp', 'seq'), 'tensor')
- down_weight_gradient: float32 [8960, 1536], P('tensor', ('dp', 'seq'))
Inputs may be any that keep to these rules, and one draw needn't show every extreme that they name: `segments`: in each group of 2048 tokens (one index of dp), every aligned block of 512 tokens holds one member: the prompt (segment 0) fills 2 blocks, its blocks in order; each continuation 1 to 2 fills one block. `positions`: prompt tokens hold 0 to 1023 in order; a continuation's tokens hold a start to that start + 511 in order, with the start between 1024 and 1536.
All inputs are finite; a program needn't handle non-finite values.
Results may differ from a plain program's by a relative error of at most 0.018.
Values may be sent and summed in bfloat16 or wider, within the bound.
No kernel may reach another device: no remote copies, remote signals or barrier semaphores. Data moves between devices by JAX's collectives and lax.ppermute only.
A program may use at most 256 MiB of HBM per device.

v0:
```python
import math

import jax
import jax.numpy as jnp
from jax import lax
from jax.sharding import PartitionSpec as P

HEAD_DIM = 128


EPS = 1e-06
LOG_BASE = math.log(1000000.0)
NEG_FILL = -1e30


def product(left, right):
    return jnp.dot(left, right, preferred_element_type=jnp.float32)


def left_product(left, right):
    return lax.dot_general(
        left, right, (((0,), (0,)), ((), ())), preferred_element_type=jnp.float32
    )


def right_product(left, right):
    return lax.dot_general(
        left, right, (((1,), (1,)), ((), ())), preferred_element_type=jnp.float32
    )


def rope_tables(places, width):
    half = width // 2
    freq = jnp.exp(jnp.arange(half, dtype=jnp.float32) * (-2.0 * LOG_BASE / width))
    angle = places.astype(jnp.float32)[:, None] * freq[None, :]
    return (jnp.cos(angle), jnp.sin(angle))


def rotate(values, cosine, sine):
    half = values.shape[-1] // 2
    first = values[..., :half]
    second = values[..., half:]
    cosine = cosine[:, None, :]
    sine = sine[:, None, :]
    return jnp.concatenate(
        [first * cosine - second * sine, second * cosine + first * sine], axis=-1
    )


def unrotate(values, cosine, sine):
    half = values.shape[-1] // 2
    first = values[..., :half]
    second = values[..., half:]
    cosine = cosine[:, None, :]
    sine = sine[:, None, :]
    return jnp.concatenate(
        [first * cosine + second * sine, second * cosine - first * sine], axis=-1
    )


def visible(segment_rows, place_rows, segment_keys, place_keys):
    same = (segment_keys[None, :] == 0) | (segment_keys[None, :] == segment_rows[:, None])
    return same & (place_keys[None, :] <= place_rows[:, None])


def norm_forward(values, gain):
    inverse = lax.rsqrt(jnp.mean(values * values, axis=-1, keepdims=True) + EPS)
    normed = values * inverse
    return (normed, inverse, (normed * gain).astype(jnp.bfloat16))


def norm_backward(upstream, normed, inverse, gain):
    scaled = upstream * gain
    inner = inverse * (scaled - normed * jnp.mean(scaled * normed, axis=-1, keepdims=True))
    return (inner, jnp.sum(upstream * normed, axis=0))


def on_device(
    hidden,
    cotangent,
    segments,
    positions,
    first_gain,
    query_weight,
    query_bias,
    key_weight,
    key_bias,
    value_weight,
    value_bias,
    out_weight,
    second_gain,
    gate_weight,
    up_weight,
    down_weight,
):
    rows = hidden.shape[0]
    group = segments.shape[0]
    blocks = group // rows
    local_heads = query_weight.shape[1] // HEAD_DIM
    local_pairs = key_weight.shape[1] // HEAD_DIM
    repeat = local_heads // local_pairs
    scale = HEAD_DIM ** (-0.5)
    start = lax.axis_index("seq") * rows
    own_segment = lax.dynamic_slice_in_dim(segments, start, rows)
    own_place = lax.dynamic_slice_in_dim(positions, start, rows)
    segment_blocks = segments.reshape(blocks, rows)
    place_blocks = positions.reshape(blocks, rows)
    gain_first = first_gain.astype(jnp.float32)
    gain_second = second_gain.astype(jnp.float32)
    query_full, key_full, value_full, out_full = (
        lax.all_gather(query_weight, ("dp", "seq"), axis=0, tiled=True),
        lax.all_gather(key_weight, ("dp", "seq"), axis=0, tiled=True),
        lax.all_gather(value_weight, ("dp", "seq"), axis=0, tiled=True),
        lax.all_gather(out_weight, ("dp", "seq"), axis=1, tiled=True),
    )
    inputs = hidden.astype(jnp.float32)
    first_normed, first_inverse, first_rounded = norm_forward(inputs, gain_first)
    query_linear = product(first_rounded, query_full) + query_bias.astype(jnp.float32)
    key_linear = product(first_rounded, key_full) + key_bias.astype(jnp.float32)
    value_rounded = (product(first_rounded, value_full) + value_bias.astype(jnp.float32)).astype(
        jnp.bfloat16
    )
    cosine, sine = rope_tables(own_place, HEAD_DIM)
    queries = rotate(query_linear.reshape(rows, local_heads, HEAD_DIM), cosine, sine).astype(
        jnp.bfloat16
    )
    keys = rotate(key_linear.reshape(rows, local_pairs, HEAD_DIM), cosine, sine).astype(
        jnp.bfloat16
    )
    values = value_rounded.reshape(rows, local_pairs, HEAD_DIM)
    group_keys, group_values = (
        lax.all_gather(keys, "seq", axis=0, tiled=True),
        lax.all_gather(values, "seq", axis=0, tiled=True),
    )
    key_blocks = group_keys.reshape(blocks, rows, local_pairs, HEAD_DIM)
    value_blocks = group_values.reshape(blocks, rows, local_pairs, HEAD_DIM)
    grouped = queries.reshape(rows, local_pairs, repeat, HEAD_DIM)
    stacked = (key_blocks, value_blocks, segment_blocks, place_blocks)

    def scores_of(key_block):
        return (
            jnp.einsum("tgrd,kgd->grtk", grouped, key_block, preferred_element_type=jnp.float32)
            * scale
        )

    def logsum_step(carry, block):
        key_block, value_block, segment_block, place_block = block
        mask = visible(own_segment, own_place, segment_block, place_block)

        def logsum_work(state):
            top, total = state
            masked = jnp.where(mask, scores_of(key_block), NEG_FILL)
            new_top = jnp.maximum(top, jnp.max(masked, axis=-1))
            weights = jnp.where(mask, jnp.exp(masked - new_top[..., None]), 0.0)
            return (new_top, total * jnp.exp(top - new_top) + jnp.sum(weights, axis=-1))

        return (lax.cond(jnp.any(mask), logsum_work, lambda state: state, carry), None)

    start_top = jnp.full((local_pairs, repeat, rows), NEG_FILL, jnp.float32)
    start_total = jnp.zeros((local_pairs, repeat, rows), jnp.float32)
    (top_final, total_final), _ = lax.scan(logsum_step, (start_top, start_total), stacked)
    log_total = top_final + jnp.log(total_final)

    def weights_of(key_block, mask):
        return jnp.where(mask, jnp.exp(scores_of(key_block) - log_total[..., None]), 0.0)

    def output_step(summed, block):
        key_block, value_block, segment_block, place_block = block
        mask = visible(own_segment, own_place, segment_block, place_block)

        def output_work(summed):
            chances = weights_of(key_block, mask).astype(jnp.bfloat16)
            return summed + jnp.einsum(
                "grtk,kgd->tgrd", chances, value_block, preferred_element_type=jnp.float32
            )

        return (lax.cond(jnp.any(mask), output_work, lambda summed: summed, summed), None)

    attended, _ = lax.scan(
        output_step, jnp.zeros((rows, local_pairs, repeat, HEAD_DIM), jnp.float32), stacked
    )
    attended = attended.reshape(rows, local_heads * HEAD_DIM).astype(jnp.bfloat16)
    attention_out = lax.psum(product(attended, out_full), "tensor")
    residual = inputs + attention_out
    second_normed, second_inverse, second_rounded = norm_forward(residual, gain_second)
    gate_full, up_full, down_full = (
        lax.all_gather(gate_weight, ("dp", "seq"), axis=0, tiled=True),
        lax.all_gather(up_weight, ("dp", "seq"), axis=0, tiled=True),
        lax.all_gather(down_weight, ("dp", "seq"), axis=1, tiled=True),
    )
    gate = product(second_rounded, gate_full)
    upper = product(second_rounded, up_full)
    sigma = jax.nn.sigmoid(gate)
    swish = gate * sigma
    activated = (swish * upper).astype(jnp.bfloat16)
    down_out = lax.psum(product(activated, down_full).astype(jnp.bfloat16), "tensor").astype(
        jnp.float32
    )
    output = (residual + down_out).astype(jnp.bfloat16)
    down_gradient = left_product(activated, cotangent)
    activated_back = right_product(cotangent, down_full)
    gate_back = (activated_back * upper * sigma * (1.0 + gate * (1.0 - sigma))).astype(jnp.bfloat16)
    upper_back = (activated_back * swish).astype(jnp.bfloat16)
    gate_gradient = left_product(second_rounded, gate_back)
    up_gradient = left_product(second_rounded, upper_back)
    feed_shares = (
        lax.psum_scatter(gate_gradient, ("dp", "seq"), scatter_dimension=0, tiled=True),
        lax.psum_scatter(up_gradient, ("dp", "seq"), scatter_dimension=0, tiled=True),
        lax.psum_scatter(down_gradient, ("dp", "seq"), scatter_dimension=1, tiled=True),
    )
    second_back = lax.psum(
        right_product(gate_back, gate_full) + right_product(upper_back, up_full), "tensor"
    )
    residual_inner, second_gain_term = norm_backward(
        second_back, second_normed, second_inverse, gain_second
    )
    residual_back = cotangent.astype(jnp.float32) + residual_inner
    attention_back = residual_back.astype(jnp.bfloat16)
    out_gradient = left_product(attended, attention_back)
    attended_back = (
        right_product(attention_back, out_full)
        .astype(jnp.bfloat16)
        .reshape(rows, local_pairs, repeat, HEAD_DIM)
    )

    def delta_step(summed, block):
        key_block, value_block, segment_block, place_block = block
        mask = visible(own_segment, own_place, segment_block, place_block)

        def delta_work(summed):
            chances = weights_of(key_block, mask)
            chance_back = jnp.einsum(
                "tgrd,kgd->grtk", attended_back, value_block, preferred_element_type=jnp.float32
            )
            return summed + jnp.sum(chances * chance_back, axis=-1)

        return (lax.cond(jnp.any(mask), delta_work, lambda summed: summed, summed), None)

    delta, _ = lax.scan(delta_step, jnp.zeros((local_pairs, repeat, rows), jnp.float32), stacked)
    empty_part = jnp.zeros((rows, local_pairs, HEAD_DIM), jnp.float32)

    def gradient_step(summed, block):
        key_block, value_block, segment_block, place_block = block
        mask = visible(own_segment, own_place, segment_block, place_block)

        def gradient_work(summed):
            chances = weights_of(key_block, mask)
            chance_back = jnp.einsum(
                "tgrd,kgd->grtk", attended_back, value_block, preferred_element_type=jnp.float32
            )
            score_back = (chances * (chance_back - delta[..., None])).astype(jnp.bfloat16)
            summed = (
                summed
                + jnp.einsum(
                    "grtk,kgd->tgrd", score_back, key_block, preferred_element_type=jnp.float32
                )
                * scale
            )
            key_part = (
                jnp.einsum(
                    "grtk,tgrd->kgd", score_back, grouped, preferred_element_type=jnp.float32
                )
                * scale
            )
            value_part = jnp.einsum(
                "grtk,tgrd->kgd",
                chances.astype(jnp.bfloat16),
                attended_back,
                preferred_element_type=jnp.float32,
            )
            return (summed, (key_part, value_part))

        def skip(summed):
            return (summed, (empty_part, empty_part))

        return lax.cond(jnp.any(mask), gradient_work, skip, summed)

    query_rotated_back, (key_parts, value_parts) = lax.scan(
        gradient_step, jnp.zeros((rows, local_pairs, repeat, HEAD_DIM), jnp.float32), stacked
    )
    key_back, value_back = (
        lax.psum_scatter(
            key_parts.reshape(group, local_pairs * HEAD_DIM), "seq", scatter_dimension=0, tiled=True
        ),
        lax.psum_scatter(
            value_parts.reshape(group, local_pairs * HEAD_DIM),
            "seq",
            scatter_dimension=0,
            tiled=True,
        ),
    )
    query_linear_back = (
        unrotate(query_rotated_back.reshape(rows, local_heads, HEAD_DIM), cosine, sine)
        .reshape(rows, local_heads * HEAD_DIM)
        .astype(jnp.bfloat16)
    )
    key_linear_back = (
        unrotate(key_back.reshape(rows, local_pairs, HEAD_DIM), cosine, sine)
        .reshape(rows, local_pairs * HEAD_DIM)
        .astype(jnp.bfloat16)
    )
    value_linear_back = value_back.astype(jnp.bfloat16)
    query_gradient = left_product(first_rounded, query_linear_back)
    key_gradient = left_product(first_rounded, key_linear_back)
    value_gradient = left_product(first_rounded, value_linear_back)
    attention_shares = (
        lax.psum_scatter(query_gradient, ("dp", "seq"), scatter_dimension=0, tiled=True),
        lax.psum_scatter(key_gradient, ("dp", "seq"), scatter_dimension=0, tiled=True),
        lax.psum_scatter(value_gradient, ("dp", "seq"), scatter_dimension=0, tiled=True),
        lax.psum_scatter(out_gradient, ("dp", "seq"), scatter_dimension=1, tiled=True),
    )
    first_back = (
        right_product(query_linear_back, query_full)
        + right_product(key_linear_back, key_full)
        + right_product(value_linear_back, value_full)
    )
    first_back = lax.psum(first_back.astype(jnp.bfloat16), "tensor").astype(jnp.float32)
    input_inner, first_gain_term = norm_backward(
        first_back, first_normed, first_inverse, gain_first
    )
    input_gradient = (residual_back + input_inner).astype(jnp.bfloat16)
    query_bias_term = jnp.sum(query_linear_back.astype(jnp.float32), axis=0)
    key_bias_term = jnp.sum(key_linear_back.astype(jnp.float32), axis=0)
    value_bias_term = jnp.sum(value_linear_back.astype(jnp.float32), axis=0)
    small_sums = lax.psum(
        (first_gain_term, query_bias_term, key_bias_term, value_bias_term, second_gain_term),
        ("dp", "seq"),
    )
    return (
        output,
        input_gradient,
        small_sums[0],
        attention_shares[0],
        small_sums[1],
        attention_shares[1],
        small_sums[2],
        attention_shares[2],
        small_sums[3],
        attention_shares[3],
        small_sums[4],
        feed_shares[0],
        feed_shares[1],
        feed_shares[2],
    )


def solution(mesh):
    in_specs = (
        P(("dp", "seq"), None),
        P(("dp", "seq"), None),
        P("dp"),
        P("dp"),
        P(),
        P(("dp", "seq"), "tensor"),
        P("tensor"),
        P(("dp", "seq"), "tensor"),
        P("tensor"),
        P(("dp", "seq"), "tensor"),
        P("tensor"),
        P("tensor", ("dp", "seq")),
        P(),
        P(("dp", "seq"), "tensor"),
        P(("dp", "seq"), "tensor"),
        P("tensor", ("dp", "seq")),
    )
    out_specs = (
        P(("dp", "seq"), None),
        P(("dp", "seq"), None),
        P(),
        P(("dp", "seq"), "tensor"),
        P("tensor"),
        P(("dp", "seq"), "tensor"),
        P("tensor"),
        P(("dp", "seq"), "tensor"),
        P("tensor"),
        P("tensor", ("dp", "seq")),
        P(),
        P(("dp", "seq"), "tensor"),
        P(("dp", "seq"), "tensor"),
        P("tensor", ("dp", "seq")),
    )
    return jax.shard_map(
        on_device, mesh=mesh, in_specs=in_specs, out_specs=out_specs, check_vma=False
    )
```

profile of v0, /device:TPU:0, one launch (start us, length us, event | category | flops | bytes accessed | tf_op | source)
XLA Modules:
  0.0 2013.0 jit_solution(262134826872539722)
XLA Ops:
  14.2 41.4 %all_gather.27 = bf16[1536,128]{1,0:T(8,128)(2,1)S(1)} all-gather(bf16[96,128]{1,0:T(8,128)(2,1)} %param.41), channel_id=1, replica_groups=mesh['dp'=4,'seq'=4,'tensor'=2] {'dp','seq'}, dimensions={0}, use_global_device_ids=true | all-gather | bytes 417792 | tf_op jit(solution)/shard_map/all_gather | solution.py:113
  58.7 17.1 all-gather
  77.6 34.2 %all_gather.29 = bf16[1536,128]{1,0:T(8,128)(2,1)S(1)} all-gather(bf16[96,128]{1,0:T(8,128)(2,1)S(1)} %copy-done.35), channel_id=1, replica_groups=mesh['dp'=4,'seq'=4,'tensor'=2] {'dp','seq'}, dimensions={0}, use_global_device_ids=true | all-gather | bytes 417792 | tf_op jit(solution)/shard_map/all_gather | solution.py:112
  113.7 15.0 all_gather.30
  129.1 4.2 convolution_add_fusion.3
  135.9 15.3 while.55
  151.3 15.7 while.56
  168.1 5.1 fusion.120
  175.1 81.7 %all-reduce.6.cloned.1.call-done = f32[512,1536]{1,0:T(8,128)} async-done(((f32[512,1536]{1,0:T(8,128)}), f32[512,1536]{1,0:T(8,128)}) %all-reduce.6.cloned.1.call-update) | async-done | bytes 3145744 | tf_op jit(solution)/shard_map/psum | solution.py:183
  261.1 106.3 %all-gather.11.cloned.1.call-done = bf16[1536,4480]{1,0:T(8,128)(2,1)} async-done(((bf16[96,4480]{1,0:T(8,128)(2,1)}), bf16[1536,4480]{1,0:T(8,128)(2,1)}) %all-gather.11.cloned.1.call-update) | async-done | bytes 13762576 | tf_op jit(solution)/shard_map/all_gather | solution.py:187
  367.4 13.2 fusion.121
  380.6 95.6 %all-gather.13.cloned.1.call-done = bf16[1536,4480]{1,0:T(8,128)(2,1)} async-done(((bf16[96,4480]{1,0:T(8,128)(2,1)}), bf16[1536,4480]{1,0:T(8,128)(2,1)}) %all-gather.13.cloned.1.call-update) | async-done | bytes 13762576 | tf_op jit(solution)/shard_map/all_gather | solution.py:188
  476.2 12.8 fusion.122
  489.0 96.0 %all-gather.15.cloned.1.call-done = bf16[4480,1536]{0,1:T(8,128)(2,1)} async-done(((bf16[4480,96]{0,1:T(8,128)(2,1)}), bf16[4480,1536]{0,1:T(8,128)(2,1)}) %all-gather.15.cloned.1.call-update) | async-done | bytes 13762576 | tf_op jit(solution)/shard_map/all_gather | solution.py:189
  585.0 21.8 %multiply_convert_fusion = (bf16[512,4480]{1,0:T(8,128)(2,1)}, bf16[512,4480]{1,0:T(8,128)(2,1)}, bf16[512,4480]{1,0:T(8,128)(2,1)}) fusion(f32[512,4480]{1,0:T(8,128)} %fusion.121, f32[512,4480]{1,0:T(8,128)} %fusion.122, bf16[512,1536]{1,0:T(8,128)(2,1)} %param.33, bf16[4480,1536]{0,1:T(8,128)(2,1)} %all-gather.15.cloned.1.call-done), kind=kOutput, calls=%fused_computation.92 | convolution fusion | flops 7080837120 | bytes 47448064 | tf_op jit(solution)/shard_map/dot_general | solution.py:27
  606.9 11.8 fusion.123
  618.6 12.2 convolution_add_fusion.2
  631.0 84.0 %all-reduce.8.cloned.1.call-done = f32[512,1536]{1,0:T(8,128)} async-done(((f32[512,1536]{1,0:T(8,128)}), f32[512,1536]{1,0:T(8,128)}) %all-reduce.8.cloned.1.call-update) | async-done | bytes 3145744 | tf_op jit(solution)/shard_map/psum | solution.py:211
  715.0 4.4 multiply_reduce_fusion
  724.3 18.8 while.57
  726.0 4.0 conditional.10
  733.5 4.0 conditional.10
  739.2 4.0 conditional.10
  744.2 35.2 %while.58 = (s32[]{:T(128)}, f32[512,1,6,128]{0,3,2,1:T(8,128)S(1)}, f32[4,512,1,128]{3,1,2,0:T(8,128)}, f32[4,512,1,128]{3,1,2,0:T(8,128)}, s32[4,512]{1,0:T(4,...) while((s32[]{:T(128)}, ...), condition=%wide.region_28.29_spmd, body=%wide.region_24.28_spmd.sunk | while | flops 2031157760 | bytes 41605440 | solution.py:278
  746.6 7.4 conditional.11
  747.9 3.1 fusion.47
  760.6 7.4 conditional.11
  771.2 7.4 conditional.11
  782.8 13.1 convolution_convert_fusion
  797.8 3.1 fusion.124
  800.9 7.8 reduce-scatter.10.cloned.1.call-done
  810.3 4.2 convolution_add_fusion.1
  814.5 23.0 %reduce-scatter.12.cloned.1.call-done = f32[512,128]{1,0:T(8,128)} async-done(((f32[2048,128]{1,0:T(8,128)}), f32[512,128]{1,0:T(8,128)}) %reduce-scatter.12.cloned.1.call-update) | async-done | bytes 262160 | tf_op jit(solution)/shard_map/reduce_scatter | solution.py:285
  837.5 3.7 fusion.85
  844.5 3.5 fusion.125
  849.2 5.5 fusion.88
  856.0 14.9 fusion.126
  871.0 14.9 fusion.127
  887.4 15.2 fusion.128
  902.8 23.3 %all-reduce.10.cloned.1.call-done = (bf16[512,1536]{1,0:T(8,128)(2,1)}, bf16[512,1536]{1,0:T(8,128)(2,1)}) async-done(((bf16[512,1536]{1,0:T(8,128)(2,1)}, bf16[512,1536]{1,0:T(8,128)(2,1)}), (bf16[512,1536]{1,0:T(8,128)(2,1)}, bf16[512,1536]{1,0:T(8,128)(2,1)})) %all-reduce.10.cloned.1.call-update) | async-done | bytes 3145744 | tf_op jit(solution)/shard_map/psum | solution.py:196
  928.5 61.7 %all-reduce = (f32[1536]{0:T(1024)}, f32[768]{0:T(1024)}, f32[128]{0:T(128)}, f32[128]{0:T(128)}, f32[1536]{0:T(1024)}) all-reduce(f32[1536]{0:T(1024)S(1)} %get-tuple-element.596, f32[768]{0:T(1024)S(1)} %bitcast.300, f32[128]{0:T(128)S(1)} %convert_reduce_fusion.2, ...), channel_id=1, replica_groups=mesh['dp'=4,'seq'=4,'tensor'=2] {'dp','seq'}, use_global_device_ids=true, to_apply=%region_34.35 | all-reduce | flops 4096 | bytes 32768 | tf_op jit(solution)/shard_map/psum | solution.py:325
  990.1 6.3 fusion.80
  996.5 50.3 %reduce-scatter.18.cloned.1.call-done = f32[96,128]{1,0:T(8,128)} async-done(((f32[1536,128]{1,0:T(8,128)}), f32[96,128]{1,0:T(8,128)}) %reduce-scatter.18.cloned.1.call-update) | async-done | bytes 49168 | tf_op jit(solution)/shard_map/reduce_scatter | solution.py:309
  1046.8 79.6 %reduce-scatter.14.cloned.1.call-done = f32[96,768]{1,0:T(8,128)} async-done(((f32[1536,768]{1,0:T(8,128)}), f32[96,768]{1,0:T(8,128)}) %reduce-scatter.14.cloned.1.call-update) | async-done | bytes 294928 | tf_op jit(solution)/shard_map/reduce_scatter | solution.py:307
  1126.3 78.9 %reduce-scatter.20.cloned.1.call-done = f32[768,96]{0,1:T(8,128)} async-done(((f32[768,1536]{0,1:T(8,128)}), f32[768,96]{0,1:T(8,128)}) %reduce-scatter.20.cloned.1.call-update) | async-done | bytes 294928 | tf_op jit(solution)/shard_map/reduce_scatter | solution.py:310
  1205.2 267.0 %reduce-scatter.22.cloned.1.call-done = f32[96,4480]{1,0:T(8,128)} async-done(((f32[1536,4480]{1,0:T(8,128)}), f32[96,4480]{1,0:T(8,128)}) %reduce-scatter.22.cloned.1.call-update) | async-done | bytes 1720336 | tf_op jit(solution)/shard_map/reduce_scatter | solution.py:207
  1472.2 266.6 %reduce-scatter.24.cloned.1.call-done = f32[96,4480]{1,0:T(8,128)} async-done(((f32[1536,4480]{1,0:T(8,128)}), f32[96,4480]{1,0:T(8,128)}) %reduce-scatter.24.cloned.1.call-update) | async-done | bytes 1720336 | tf_op jit(solution)/shard_map/reduce_scatter | solution.py:208
  1738.9 267.2 %reduce-scatter.26.cloned.1.call-done = f32[4480,96]{0,1:T(8,128)} async-done(((f32[4480,1536]{0,1:T(8,128)}), f32[4480,96]{0,1:T(8,128)}) %reduce-scatter.26.cloned.1.call-update) | async-done | bytes 1720336 | tf_op jit(solution)/shard_map/reduce_scatter | solution.py:209
  (289 shorter events, 134.1 us)
Async XLA Ops:
  7.2 121.9 %all-gather.7.cloned.1.call-start = ((), (), s32[]{:S(2)}) async-start(), calls=%async_computation.9 | async-start | bytes 2506752 | tf_op jit(solution)/shard_map/all_gather | solution.py:111
  7.9 160.2 %all-gather.9.cloned.1.call-start = ((), (), s32[]{:S(2)}) async-start(), calls=%async_computation.10 | async-start | bytes 2506752 | tf_op jit(solution)/shard_map/all_gather | solution.py:114
  8.7 248.1 %all-reduce.6.cloned.1.call-start = ((), (), s32[]{:S(2)}) async-start(), calls=%async_computation.11 | async-start | bytes 6291456 | tf_op jit(solution)/shard_map/psum | solution.py:183
  11.6 101.4 %copy-start.30 = (f32[512]{0:T(512)}, f32[512]{0:T(512)S(1)}, u32[]{:S(2)}) copy-start(f32[512]{0:T(512)S(1)} %get-tuple-element.713) | copy-start | bytes 6148
  11.7 101.4 %copy-start.36 = (f32[64]{0:T(128)}, f32[64]{0:T(128)S(1)}, u32[]{:S(2)}) copy-start(f32[64]{0:T(128)S(1)} %multiply_exponential_fusion) | copy-start | bytes 772
  12.4 46.3 %copy-start.28 = (f32[1536]{0:T(1024)}, f32[1536]{0:T(1024)S(1)}, u32[]{:S(2)}) copy-start(f32[1536]{0:T(1024)S(1)} %convert_element_type.141) | copy-start | bytes 18436
  14.2 61.7 %copy-start.33 = (f32[512]{0:T(512)}, f32[512]{0:T(512)S(1)}, u32[]{:S(2)}) copy-start(f32[512]{0:T(512)S(1)} %add_rsqrt_fusion.1) | copy-start | bytes 6148
  55.6 22.1 %copy-start.10 = (bf16[1536,128]{1,0:T(8,128)(2,1)}, bf16[1536,128]{1,0:T(8,128)(2,1)S(1)}, u32[]{:S(2)}) copy-start(bf16[1536,128]{1,0:T(8,128)(2,1)S(1)} %all_gather.27) | copy-start | bytes 1179652
  56.2 21.4 %copy-start.35 = (bf16[96,128]{1,0:T(8,128)(2,1)S(1)}, bf16[96,128]{1,0:T(8,128)(2,1)}, u32[]{:S(2)}) copy-start(bf16[96,128]{1,0:T(8,128)(2,1)} %param.39) | copy-start | bytes 73732
  56.2 55.6 %copy-start.42 = (bf16[128]{0:T(256)(128)(2,1)S(1)}, bf16[128]{0:T(256)(128)(2,1)}, u32[]{:S(2)}) copy-start(bf16[128]{0:T(256)(128)(2,1)} %param.40) | copy-start | bytes 772
  58.1 70.9 %copy-start.2 = (bf16[512,1536]{1,0:T(8,128)(2,1)}, bf16[512,1536]{1,0:T(8,128)(2,1)S(1)}, u32[]{:S(2)}) copy-start(bf16[512,1536]{1,0:T(8,128)(2,1)S(1)} %fusion.81) | copy-start | bytes 4718596
  76.6 52.4 %copy-start.39 = (bf16[768]{0:T(1024)(128)(2,1)S(1)}, bf16[768]{0:T(1024)(128)(2,1)}, u32[]{:S(2)}) copy-start(bf16[768]{0:T(1024)(128)(2,1)} %param.38) | copy-start | bytes 4612
  113.1 22.0 %copy-start.22 = (f32[512,64]{0,1:T(8,128)}, f32[512,64]{0,1:T(8,128)S(1)}, u32[]{:S(2)}) copy-start(f32[512,64]{0,1:T(8,128)S(1)} %get-tuple-element.730) | copy-start | bytes 393220
  113.1 22.0 %copy-start.24 = (f32[512,64]{0,1:T(8,128)}, f32[512,64]{0,1:T(8,128)S(1)}, u32[]{:S(2)}) copy-start(f32[512,64]{0,1:T(8,128)S(1)} %get-tuple-element.731) | copy-start | bytes 393220
  173.2 83.6 %copy-start.4 = (bf16[512,1536]{1,0:T(8,128)(2,1)S(1)}, bf16[512,1536]{1,0:T(8,128)(2,1)}, u32[]{:S(2)}) copy-start(bf16[512,1536]{1,0:T(8,128)(2,1)} %param.32) | copy-start | bytes 4718596
  173.2 194.2 %all-gather.11.cloned.1.call-start = ((), (), s32[]{:S(2)}) async-start(), calls=%async_computation.12 | async-start | bytes 14622720 | tf_op jit(solution)/shard_map/all_gather | solution.py:187
  173.8 302.4 %all-gather.13.cloned.1.call-start = ((), (), s32[]{:S(2)}) async-start(), calls=%async_computation.13 | async-start | bytes 14622720 | tf_op jit(solution)/shard_map/all_gather | solution.py:188
  174.4 410.6 %all-gather.15.cloned.1.call-start = ((), (), s32[]{:S(2)}) async-start(), calls=%async_computation.14 | async-start | bytes 14622720 | tf_op jit(solution)/shard_map/all_gather | solution.py:189
  175.0 540.0 %all-reduce.8.cloned.1.call-start = ((), (), s32[]{:S(2)}) async-start(), calls=%async_computation.15 | async-start | bytes 6291456 | tf_op jit(solution)/shard_map/psum | solution.py:211
  261.1 215.1 %copy-start.18 = (bf16[512,1536]{1,0:T(8,128)(2,1)}, bf16[512,1536]{1,0:T(8,128)(2,1)S(1)}, u32[]{:S(2)}) copy-start(bf16[512,1536]{1,0:T(8,128)(2,1)S(1)} %multiply_convert_fusion.3) | copy-start | bytes 4718596
  606.9 11.8 copy-start.43
  618.6 100.7 %copy-start.20 = (bf16[512,1536]{1,0:T(8,128)(2,1)S(1)}, bf16[512,1536]{1,0:T(8,128)(2,1)}, u32[]{:S(2)}) copy-start(bf16[512,1536]{1,0:T(8,128)(2,1)} %param.33) | copy-start | bytes 4718596
  630.9 177.8 %reduce-scatter.10.cloned.1.call-start = ((), (), s32[]{:S(2)}) async-start(), calls=%async_computation.16 | async-start | bytes 1310720 | tf_op jit(solution)/shard_map/reduce_scatter | solution.py:282
  715.0 4.4 copy-start.1
  715.0 4.7 copy-start.7
  719.7 2.6 copy-start.41
  782.0 55.6 %reduce-scatter.12.cloned.1.call-start = ((), (), s32[]{:S(2)}) async-start(), calls=%async_computation.17 | async-start | bytes 1310720 | tf_op jit(solution)/shard_map/reduce_scatter | solution.py:285
  782.7 143.3 %all-reduce.10.cloned.1.call-start = ((), (), s32[]{:S(2)}) async-start(), calls=%async_computation.25 | async-start | bytes 6291456 | tf_op jit(solution)/shard_map/psum | solution.py:196
  782.7 13.1 copy-start.23
  782.8 13.1 copy-start.25
  795.8 2.0 copy-start.40
  797.8 10.9 copy-start.31
  797.8 10.9 copy-start.37
  797.8 12.5 copy-start.13
  810.3 27.3 %copy-start.11 = (bf16[1536,128]{1,0:T(8,128)(2,1)S(1)}, bf16[1536,128]{1,0:T(8,128)(2,1)}, u32[]{:S(2)}) copy-start(bf16[1536,128]{1,0:T(8,128)(2,1)} %copy-done.10) | copy-start | bytes 1179652
  814.5 26.8 %copy-start.3 = (bf16[512,1536]{1,0:T(8,128)(2,1)S(1)}, bf16[512,1536]{1,0:T(8,128)(2,1)}, u32[]{:S(2)}) copy-start(bf16[512,1536]{1,0:T(8,128)(2,1)} %copy-done.2) | copy-start | bytes 4718596
  841.3 3.2 copy-start.15
  841.3 155.2 %reduce-scatter.16.cloned.1.call-start = ((), (), s32[]{:S(2)}) async-start(), calls=%async_computation.19 | async-start | bytes 835584 | tf_op jit(solution)/shard_map/reduce_scatter | solution.py:308
  842.9 203.9 %reduce-scatter.18.cloned.1.call-start = ((), (), s32[]{:S(2)}) async-start(), calls=%async_computation.20 | async-start | bytes 835584 | tf_op jit(solution)/shard_map/reduce_scatter | solution.py:309
  844.4 281.9 %reduce-scatter.14.cloned.1.call-start = ((), (), s32[]{:S(2)}) async-start(), calls=%async_computation.18 | async-start | bytes 5013504 | tf_op jit(solution)/shard_map/reduce_scatter | solution.py:307
  848.1 357.1 %reduce-scatter.20.cloned.1.call-start = ((), (), s32[]{:S(2)}) async-start(), calls=%async_computation.21 | async-start | bytes 5013504 | tf_op jit(solution)/shard_map/reduce_scatter | solution.py:310
  854.7 617.6 %reduce-scatter.22.cloned.1.call-start = ((), (), s32[]{:S(2)}) async-start(), calls=%async_computation.22 | async-start | bytes 29245440 | tf_op jit(solution)/shard_map/reduce_scatter | solution.py:207
  871.0 867.9 %reduce-scatter.24.cloned.1.call-start = ((), (), s32[]{:S(2)}) async-start(), calls=%async_computation.23 | async-start | bytes 29245440 | tf_op jit(solution)/shard_map/reduce_scatter | solution.py:208
  886.0 1120.1 %reduce-scatter.26.cloned.1.call-start = ((), (), s32[]{:S(2)}) async-start(), calls=%async_computation.24 | async-start | bytes 29245440 | tf_op jit(solution)/shard_map/reduce_scatter | solution.py:209
  902.5 23.5 %copy-start.5 = (bf16[512,1536]{1,0:T(8,128)(2,1)S(1)}, bf16[512,1536]{1,0:T(8,128)(2,1)}, u32[]{:S(2)}) copy-start(bf16[512,1536]{1,0:T(8,128)(2,1)} %param.32) | copy-start | bytes 4718596
  902.5 23.5 %copy-start.29 = (f32[1536]{0:T(1024)S(1)}, f32[1536]{0:T(1024)}, u32[]{:S(2)}) copy-start(f32[1536]{0:T(1024)} %copy-done.28) | copy-start | bytes 18436
  902.5 23.5 %copy-start.34 = (f32[512]{0:T(512)S(1)}, f32[512]{0:T(512)}, u32[]{:S(2)}) copy-start(f32[512]{0:T(512)} %copy-done.33) | copy-start | bytes 6148
  902.6 25.9 %copy-start.32 = (f32[1536]{0:T(1024)S(1)}, f32[1536]{0:T(1024)}, u32[]{:S(2)}) copy-start(f32[1536]{0:T(1024)} %get-tuple-element.594) | copy-start | bytes 18436
  (17 other events, 21.8 us)
Sparse Core Ops, SparseCore 0:
  10.3 46.5 all-gather.6
  59.2 41.8 all-gather.8
  173.4 83.3 all-reduce.5
  259.2 108.1 all-gather.10
  369.8 106.3 all-gather.12
  478.6 106.3 all-gather.14
  631.0 83.9 all-reduce.7
  782.1 26.5 reduce-scatter.9
  811.7 25.7 reduce-scatter.11
  841.4 84.5 all-reduce.9
  930.6 56.5 reduce-scatter.15
  991.1 55.5 reduce-scatter.17
  1051.7 74.5 reduce-scatter.13
  1130.6 74.5 reduce-scatter.19
  1210.3 261.8 reduce-scatter.21
  1476.8 262.0 reduce-scatter.23
  1743.9 262.0 reduce-scatter.25
where the time goes:
time: 2020 us; the launch traced here: 2010 us
  waiting for transfers between devices  1530 us (76%)
  matrix products  210 us (10%)
  blocking collectives  169 us (8%)
  other arithmetic  51.2 us (3%)
  local copies, waits for them, and re-layouts  24 us (1%)
    reduce_scatter x1, waiting for transfers between devices, on_device(): lax.psum_scatter(down_gradient, ('dp', 'seq'), scatter_dimension=1, tiled...  267 us
    reduce_scatter x1, waiting for transfers between devices, on_device(): lax.psum_scatter(gate_gradient, ('dp', 'seq'), scatter_dimension=0, tiled...  267 us
    reduce_scatter x1, waiting for transfers between devices, on_device(): lax.psum_scatter(up_gradient, ('dp', 'seq'), scatter_dimension=0, tiled=T...  267 us
    all_gather x1, waiting for transfers between devices, on_device(): lax.all_gather(gate_weight, ('dp', 'seq'), axis=0, tiled=True)  106 us
    all_gather x1, waiting for transfers between devices, on_device(): lax.all_gather(down_weight, ('dp', 'seq'), axis=1, tiled=True)  96 us
    all_gather x1, waiting for transfers between devices, on_device(): lax.all_gather(up_weight, ('dp', 'seq'), axis=0, tiled=True)  95.6 us
    psum x1, waiting for transfers between devices, on_device(): lax.psum(right_product(gate_back, gate_full) + right_product(upper_back,...  84 us
    psum x1, waiting for transfers between devices, on_device(): attention_out = lax.psum(product(attended, out_full), 'tensor')  81.7 us
  transfers between devices with their start and end apart: 17, of which 14 were waited for; matrix products, arithmetic and copies ran while one was open for 8% of the time, Pallas kernels for 0%

commit v1 on v0

v1 whole, which is shorter than its diff:
```python
import functools
import math

import jax
import jax.numpy as jnp
from jax import lax
from jax.experimental import pallas as pl
from jax.experimental.pallas import tpu as pltpu
from jax.sharding import PartitionSpec as P

HEAD_DIM = 128
EPS = 1e-06
LOG_BASE = math.log(1000000.0)
NEG_FILL = -1e30
LOG2E = 1.0 / math.log(2.0)
MIB = 1024 * 1024
F32 = jnp.float32
BF16 = jnp.bfloat16
FREE = pl.CostEstimate(flops=0, bytes_accessed=0, transcendentals=0)


def product(left, right):
    return jnp.dot(left, right, preferred_element_type=F32)


def left_product(left, right):
    return lax.dot_general(left, right, (((0,), (0,)), ((), ())), preferred_element_type=F32)


def right_product(left, right):
    return lax.dot_general(left, right, (((1,), (1,)), ((), ())), preferred_element_type=F32)


def after(value, *others):
    return lax.optimization_barrier((value,) + others)[0]


def together(*values):
    return lax.optimization_barrier(values)


def dp_swap(value, flip):
    size = lax.axis_size("dp")
    return lax.ppermute(value, "dp", [(i, i ^ flip) for i in range(size)])


def y_swap(value):
    return lax.ppermute(value, "tensor", [(0, 1), (1, 0)])


def z_shift(value, step):
    size = lax.axis_size("seq")
    return lax.ppermute(value, "seq", [(i, (i + step) % size) for i in range(size)])


def assemble_kernel(count, place_ref, *refs):
    pieces, out_ref, sems = refs[:count], refs[count], refs[count + 1]
    copies = [
        pltpu.make_async_copy(piece, out_ref.at[place_ref[i]], sems.at[i])
        for i, piece in enumerate(pieces)
    ]
    for copy in copies:
        copy.start()
    for copy in copies:
        copy.wait()


def assemble(pieces, places):
    count = len(pieces)
    return pl.pallas_call(
        functools.partial(assemble_kernel, count),
        out_shape=jax.ShapeDtypeStruct((count,) + pieces[0].shape, pieces[0].dtype),
        in_specs=[pl.BlockSpec(memory_space=pltpu.SMEM)]
        + [pl.BlockSpec(memory_space=pl.ANY)] * count,
        out_specs=pl.BlockSpec(memory_space=pltpu.VMEM),
        scratch_shapes=[pltpu.SemaphoreType.DMA((count,))],
        compiler_params=pltpu.CompilerParams(vmem_limit_bytes=24 * MIB),
        cost_estimate=FREE,
    )(places, *pieces)


def pair_mask(seg_q, pos_q, seg_k, pos_k):
    return ((seg_k == 0) | (seg_k == seg_q)) & (pos_k <= pos_q)


def attend_kernel(
    rows, factor, flag_ref, q_ref, k_ref, v_ref, sq_ref, pq_ref, sk_ref, pk_ref,
    o_ref, lse_ref, top_ref, sum_ref, acc_ref,
):
    blocks = k_ref.shape[0] // rows
    top_ref[...] = jnp.full_like(top_ref, NEG_FILL)
    sum_ref[...] = jnp.zeros_like(sum_ref)
    acc_ref[...] = jnp.zeros_like(acc_ref)
    q = q_ref[...]

    def block_step(j, masked):
        span = pl.ds(pl.multiple_of(j * rows, rows), rows)
        s = right_product(q, k_ref[span, :]) * factor
        if masked:
            mask = pair_mask(sq_ref[...], pq_ref[...], sk_ref[j], pk_ref[j])
            s = jnp.where(mask, s, NEG_FILL)
        top = top_ref[...]
        new_top = jnp.maximum(top, jnp.max(s, axis=1, keepdims=True))
        e = jnp.exp2(s - new_top)
        if masked:
            e = jnp.where(mask, e, 0.0)
        shrink = jnp.exp2(top - new_top)
        top_ref[...] = new_top
        sum_ref[...] = sum_ref[...] * shrink + jnp.sum(e, axis=1, keepdims=True)
        acc_ref[...] = acc_ref[...] * shrink + product(e.astype(BF16), v_ref[span, :])

    def step(j, carry):
        @pl.when(flag_ref[j] == 2)
        def _():
            block_step(j, False)

        @pl.when(flag_ref[j] == 1)
        def _():
            block_step(j, True)

        return carry

    lax.fori_loop(0, blocks, step, 0)
    total = sum_ref[...]
    o_ref[...] = (acc_ref[...] / total).astype(o_ref.dtype)
    lse_ref[...] = (top_ref[...] + jnp.log2(total))[None]


def attend(q, keys, values, seg_q, pos_q, seg_k, pos_k, flags):
    rows, width = q.shape
    heads = width // HEAD_DIM
    kv_heads = keys.shape[1] // HEAD_DIM
    repeat = heads // kv_heads
    length = keys.shape[0]
    blocks = length // rows
    whole = lambda *shape: pl.BlockSpec(shape, lambda h: (0,) * len(shape))
    return pl.pallas_call(
        functools.partial(attend_kernel, rows, HEAD_DIM ** (-0.5) * LOG2E),
        grid=(heads,),
        in_specs=[
            pl.BlockSpec(memory_space=pltpu.SMEM),
            pl.BlockSpec((rows, HEAD_DIM), lambda h: (0, h)),
            pl.BlockSpec((length, HEAD_DIM), lambda h: (0, h // repeat)),
            pl.BlockSpec((length, HEAD_DIM), lambda h: (0, h // repeat)),
            whole(rows, 1),
            whole(rows, 1),
            whole(blocks, 1, rows),
            whole(blocks, 1, rows),
        ],
        out_specs=[
            pl.BlockSpec((rows, HEAD_DIM), lambda h: (0, h)),
            pl.BlockSpec((1, rows, 1), lambda h: (h, 0, 0)),
        ],
        out_shape=[
            jax.ShapeDtypeStruct((rows, width), BF16),
            jax.ShapeDtypeStruct((heads, rows, 1), F32),
        ],
        scratch_shapes=[
            pltpu.VMEM((rows, 1), F32),
            pltpu.VMEM((rows, 1), F32),
            pltpu.VMEM((rows, HEAD_DIM), F32),
        ],
        compiler_params=pltpu.CompilerParams(vmem_limit_bytes=40 * MIB),
        cost_estimate=FREE,
    )(flags, q, keys, values, seg_q, pos_q, seg_k, pos_k)


def attend_back_kernel(
    rows, factor, scale, repeat, flag_ref, q_ref, k_ref, v_ref, do_ref, lse_ref, cos_ref, sin_ref,
    sq_ref, pq_ref, sk_ref, pk_ref, dq_ref, dk_ref, dv_ref, dk_acc, dv_acc, dq_acc,
    p_keep, dp_keep, delta_ref,
):
    head = pl.program_id(0)
    blocks = k_ref.shape[0] // rows

    @pl.when(lax.rem(head, repeat) == 0)
    def _():
        dk_acc[...] = jnp.zeros_like(dk_acc)
        dv_acc[...] = jnp.zeros_like(dv_acc)

    dq_acc[...] = jnp.zeros_like(dq_acc)
    delta_ref[...] = jnp.zeros_like(delta_ref)
    q = q_ref[...]
    d_o = do_ref[...]
    lse = lse_ref[0]

    def span_of(j):
        return pl.ds(pl.multiple_of(j * rows, rows), rows)

    def first_pass(j, masked):
        p = jnp.exp2(right_product(q, k_ref[span_of(j), :]) * factor - lse)
        if masked:
            mask = pair_mask(sq_ref[...], pq_ref[...], sk_ref[j], pk_ref[j])
            p = jnp.where(mask, p, 0.0)
        dp = right_product(d_o, v_ref[span_of(j), :])
        p_keep[j] = p
        dp_keep[j] = dp
        delta_ref[...] += jnp.sum(p * dp, axis=1, keepdims=True)

    def first_step(j, carry):
        @pl.when(flag_ref[j] == 2)
        def _():
            first_pass(j, False)

        @pl.when(flag_ref[j] == 1)
        def _():
            first_pass(j, True)

        return carry

    lax.fori_loop(0, blocks, first_step, 0)

    def second_step(j, carry):
        @pl.when(flag_ref[j] > 0)
        def _():
            p = p_keep[j]
            ds = (p * (dp_keep[j] - delta_ref[...])).astype(BF16)
            span = span_of(j)
            dv_acc[span, :] += left_product(p.astype(BF16), d_o)
            dk_acc[span, :] += left_product(ds, q)
            dq_acc[...] += product(ds, k_ref[span, :])

        return carry

    lax.fori_loop(0, blocks, second_step, 0)
    (turned,) = rope_lanes(dq_acc[...] * scale, cos_ref[...], -sin_ref[...])
    dq_ref[...] = turned.astype(dq_ref.dtype)

    @pl.when(lax.rem(head, repeat) == repeat - 1)
    def _():
        dk_ref[...] = (dk_acc[...] * scale).astype(dk_ref.dtype)
        dv_ref[...] = dv_acc[...].astype(dv_ref.dtype)


def attend_back(q, keys, values, d_o, lse, cosine, sine, seg_q, pos_q, seg_k, pos_k, flags):
    rows, width = q.shape
    heads = width // HEAD_DIM
    kv_heads = keys.shape[1] // HEAD_DIM
    repeat = heads // kv_heads
    length = keys.shape[0]
    blocks = length // rows
    whole = lambda *shape: pl.BlockSpec(shape, lambda h: (0,) * len(shape))
    per_head = pl.BlockSpec((rows, HEAD_DIM), lambda h: (0, h))
    per_pair = pl.BlockSpec((length, HEAD_DIM), lambda h: (0, h // repeat))
    held = pl.BlockSpec(
        (length, HEAD_DIM), lambda h: (0, h // repeat), pipeline_mode=pl.Buffered(1)
    )
    return pl.pallas_call(
        functools.partial(
            attend_back_kernel, rows, HEAD_DIM ** (-0.5) * LOG2E, HEAD_DIM ** (-0.5), repeat
        ),
        grid=(heads,),
        in_specs=[
            pl.BlockSpec(memory_space=pltpu.SMEM),
            per_head,
            held,
            held,
            per_head,
            pl.BlockSpec((1, rows, 1), lambda h: (h, 0, 0)),
            whole(rows, HEAD_DIM),
            whole(rows, HEAD_DIM),
            whole(rows, 1),
            whole(rows, 1),
            whole(blocks, 1, rows),
            whole(blocks, 1, rows),
        ],
        out_specs=[per_head, per_pair, per_pair],
        out_shape=[
            jax.ShapeDtypeStruct((rows, width), BF16),
            jax.ShapeDtypeStruct(keys.shape, BF16),
            jax.ShapeDtypeStruct(values.shape, BF16),
        ],
        scratch_shapes=[
            pltpu.VMEM((length, HEAD_DIM), F32),
            pltpu.VMEM((length, HEAD_DIM), F32),
            pltpu.VMEM((rows, HEAD_DIM), F32),
            pltpu.VMEM((blocks, rows, rows), F32),
            pltpu.VMEM((blocks, rows, rows), F32),
            pltpu.VMEM((rows, 1), F32),
        ],
        compiler_params=pltpu.CompilerParams(vmem_limit_bytes=58 * MIB),
        cost_estimate=FREE,
    )(flags, q, keys, values, d_o, lse, cosine, sine, seg_q, pos_q, seg_k, pos_k)


def rope_tables(places, width):
    half = width // 2
    freq = jnp.exp(jnp.arange(half, dtype=F32) * (-2.0 * LOG_BASE / width))
    angle = places.astype(F32)[:, None] * freq[None, :]
    return (jnp.cos(angle), jnp.sin(angle))


def rotate(values, cosine, sine):
    half = HEAD_DIM // 2
    parts = []
    for at in range(0, values.shape[1], HEAD_DIM):
        first = values[:, at : at + half]
        second = values[:, at + half : at + HEAD_DIM]
        parts += [first * cosine - second * sine, second * cosine + first * sine]
    return jnp.concatenate(parts, axis=1)


def inverse_rms(values):
    return lax.rsqrt(jnp.mean(values * values, axis=-1, keepdims=True) + EPS)


def norm_backward(upstream, normed, inverse, gain):
    scaled = upstream * gain
    inner = inverse * (scaled - normed * jnp.mean(scaled * normed, axis=-1, keepdims=True))
    return (inner, jnp.sum(upstream * normed, axis=0))


def rope_lanes(values, cosine, sine):
    parts = []
    for at in range(0, values.shape[1], HEAD_DIM):
        head = values[:, at : at + HEAD_DIM]
        parts.append(head * cosine + pltpu.roll(head, HEAD_DIM // 2, 1) * sine)
    return parts


def project_kernel(
    count, q_width, kv_width, place_ref, mine_ref, theirs_ref,
    x_ref, gain_ref, bias_ref, cos_ref, sin_ref, q_ref, kv_ref, h_ref, w_ref, sems,
):
    copies = [
        pltpu.make_async_copy(stack.at[i], w_ref.at[place_ref[at + i]], sems.at[at + i])
        for at, stack in ((0, mine_ref), (count, theirs_ref))
        for i in range(count)
    ]
    for copy in copies:
        copy.start()
    x = x_ref[...].astype(F32)
    normed = x * lax.rsqrt(jnp.mean(x * x, axis=1, keepdims=True) + EPS)
    h = (normed * gain_ref[...]).astype(BF16)
    h_ref[...] = h
    for copy in copies:
        copy.wait()
    depth, columns = x.shape[1], bias_ref.shape[1]
    weights = w_ref[...].reshape(depth, w_ref.shape[2])
    linear = product(h, weights[:, :columns]) + bias_ref[...]
    turned = rope_lanes(linear[:, : q_width + kv_width], cos_ref[...], sin_ref[...])
    heads = q_width // HEAD_DIM
    for i, part in enumerate(turned):
        if i < heads:
            q_ref[:, i * HEAD_DIM : (i + 1) * HEAD_DIM] = part.astype(BF16)
        else:
            at = (i - heads) * HEAD_DIM
            kv_ref[:, at : at + HEAD_DIM] = part.astype(BF16)
    kv_ref[:, kv_width:] = linear[:, q_width + kv_width :].astype(BF16)


def project(mine, theirs, places, inputs, gain, bias, cosine, sine, q_width, kv_width):
    count = mine.shape[0]
    rows, depth = inputs.shape
    columns = bias.shape[0]
    vmem = pl.BlockSpec(memory_space=pltpu.VMEM)
    return pl.pallas_call(
        functools.partial(project_kernel, count, q_width, kv_width),
        out_shape=[
            jax.ShapeDtypeStruct((rows, q_width), BF16),
            jax.ShapeDtypeStruct((rows, 2 * kv_width), BF16),
            jax.ShapeDtypeStruct((rows, depth), BF16),
            jax.ShapeDtypeStruct((2 * count,) + mine.shape[1:], BF16),
        ],
        in_specs=[pl.BlockSpec(memory_space=pltpu.SMEM)]
        + [pl.BlockSpec(memory_space=pl.ANY)] * 2
        + [vmem] * 5,
        out_specs=[vmem] * 4,
        scratch_shapes=[pltpu.SemaphoreType.DMA((2 * count,))],
        compiler_params=pltpu.CompilerParams(vmem_limit_bytes=40 * MIB),
        cost_estimate=FREE,
    )(places, mine, theirs, inputs, gain[None, :], bias[None, :], cosine, sine)


class Cut:
    def __init__(self, total, n_dp):
        tiles = total // n_dp // 128
        first = max(tiles * 3 // 8, 1)
        self.total = total
        self.n_dp = n_dp
        self.main = (first * 128, (tiles - first) * 128)
        self.start = (0, n_dp * self.main[0])
        self.rest_at = n_dp * (self.main[0] + self.main[1])
        self.rest = (total - self.rest_at) // n_dp
        pad = -(-self.rest // 128) * 128
        self.width = (self.main[0], self.main[1] + pad)


def pick(values, index):
    result = values[0]
    for i in range(1, len(values)):
        result = jnp.where(index == i, values[i], result)
    return result


def cut_kernel(cut, place_ref, *refs):
    weights, outs = refs[:3], refs[3:]
    n_dp = cut.n_dp
    for part in range(2):
        main, width = cut.main[part], cut.width[part]
        for k in range(n_dp):
            owner = place_ref[k]
            out = outs[part * n_dp + k]
            for i, w in enumerate(weights):
                at = i * width
                low = pl.multiple_of(cut.start[part] + owner * main, 128)
                out[:, at : at + main] = w[:, pl.ds(low, main)]
                if part == 1 and cut.rest:
                    tail = w[:, cut.rest_at :]
                    rest = pick(
                        [tail[:, b * cut.rest : (b + 1) * cut.rest] for b in range(n_dp)], owner
                    )
                    fill = jnp.zeros((rest.shape[0], width - main - cut.rest), rest.dtype)
                    out[:, at + main : at + width] = jnp.concatenate([rest, fill], axis=1)


def cut_units(cut, weights, owners):
    rows = weights[0].shape[0]
    vmem = pl.BlockSpec(memory_space=pltpu.VMEM)
    outs = pl.pallas_call(
        functools.partial(cut_kernel, cut),
        out_shape=[
            jax.ShapeDtypeStruct((rows, 3 * cut.width[part]), BF16)
            for part in range(2)
            for _ in range(cut.n_dp)
        ],
        in_specs=[pl.BlockSpec(memory_space=pltpu.SMEM)] + [vmem] * 3,
        out_specs=[vmem] * (2 * cut.n_dp),
        compiler_params=pltpu.CompilerParams(vmem_limit_bytes=24 * MIB),
        cost_estimate=FREE,
    )(owners, *weights)
    return outs[: cut.n_dp], outs[cut.n_dp :]


def lay_kernel(cut, place_ref, *refs):
    n_dp = cut.n_dp
    firsts, pairs, downs = (refs[i * n_dp : (i + 1) * n_dp] for i in range(3))
    outs = refs[3 * n_dp :]
    for i, out in enumerate(outs):
        for part in range(2):
            main, width = cut.main[part], cut.width[part]
            for k in range(n_dp):
                if part == 0:
                    piece = firsts[k].at[:, i * width : (i + 1) * width]
                elif i < 2:
                    piece = pairs[k].at[:, i * width : (i + 1) * width]
                else:
                    piece = downs[k]
                owner = place_ref[k]
                low = pl.multiple_of(cut.start[part] + owner * main, 128)
                out[:, pl.ds(low, main)] = piece[:, :main].astype(F32)
        if cut.rest:
            main, width = cut.main[1], cut.width[1]
            tails = []
            for k in range(n_dp):
                piece = pairs[k].at[:, i * width : (i + 1) * width] if i < 2 else downs[k]
                tails.append(piece[:, main:].astype(F32)[:, : cut.rest])
            laid = []
            for b in range(n_dp):
                laid.append(
                    functools.reduce(
                        lambda got, k: jnp.where(place_ref[k] == b, tails[k], got),
                        range(1, n_dp),
                        tails[0],
                    )
                )
            out[:, cut.rest_at :] = jnp.concatenate(laid, axis=1)


def lay_units(cut, pieces, owners):
    rows = pieces[0].shape[0]
    vmem = pl.BlockSpec(memory_space=pltpu.VMEM)
    return pl.pallas_call(
        functools.partial(lay_kernel, cut),
        out_shape=[jax.ShapeDtypeStruct((rows, cut.total), F32)] * 3,
        in_specs=[pl.BlockSpec(memory_space=pltpu.SMEM)] + [vmem] * len(pieces),
        out_specs=[vmem] * 3,
        compiler_params=pltpu.CompilerParams(vmem_limit_bytes=32 * MIB),
        cost_estimate=FREE,
    )(owners, *pieces)


def feed_kernel(count, sums, *refs):
    t_ref, c_ref, w_ref = refs[:3]
    p_ref, back_ref, out_ref = refs[-3:]
    gate_weight, up_weight, down_weight = (
        w_ref.at[:, i * count : (i + 1) * count] for i in range(3)
    )
    tokens = t_ref[...]
    gate = product(tokens, gate_weight[...])
    upper = product(tokens, up_weight[...])
    act_back = product(c_ref[...], down_weight[...])
    sigma = 1.0 / (1.0 + jnp.exp(-gate))
    swish = gate * sigma
    activated = (swish * upper).astype(BF16)
    gate_back = (act_back * upper * sigma * (1.0 + gate * (1.0 - sigma))).astype(BF16)
    upper_back = (act_back * swish).astype(BF16)
    for i, value in enumerate((gate_back, upper_back, activated)):
        p_ref[:, i * count : (i + 1) * count] = value
    back = right_product(gate_back, gate_weight[...]) + right_product(upper_back, up_weight[...])
    out = right_product(activated, down_weight[...])
    if sums:
        back = back + refs[3][...]
        out = out + refs[4][...]
    back_ref[...] = back.astype(back_ref.dtype)
    out_ref[...] = out.astype(out_ref.dtype)


def feed(tokens, cots, weights, side, kept, earlier, dtype):
    rows, width = tokens.shape
    columns = weights.shape[1]
    span = rows // 2
    tall = min(256, span)
    steps = span // tall
    block = lambda w: pl.BlockSpec((tall, w), lambda i: (side * steps + i, 0))
    near = pl.BlockSpec((tall, width), lambda i: (i, 0))
    operands = [tokens, cots, weights]
    in_specs = [
        block(width),
        block(width),
        pl.BlockSpec((width, columns), lambda i: (0, 0), pipeline_mode=pl.Buffered(1)),
    ]
    if earlier is not None:
        operands += list(earlier)
        in_specs += [near, near]
    aliases = {}
    if kept is not None:
        aliases = {len(operands): 0}
        operands.append(kept)
        in_specs.append(pl.BlockSpec(memory_space=pl.ANY))
    return pl.pallas_call(
        functools.partial(feed_kernel, columns // 3, earlier is not None),
        grid=(steps,),
        in_specs=in_specs,
        out_specs=[block(columns), near, near],
        out_shape=[
            jax.ShapeDtypeStruct((rows, columns), BF16),
            jax.ShapeDtypeStruct((span, width), dtype),
            jax.ShapeDtypeStruct((span, width), dtype),
        ],
        input_output_aliases=aliases,
        compiler_params=pltpu.CompilerParams(vmem_limit_bytes=56 * MIB),
        cost_estimate=FREE,
    )(*operands)


def grads_kernel(split, t_ref, c_ref, p_ref, o_ref):
    step = pl.program_id(0)

    @pl.when(step < split)
    def _():
        o_ref[...] = left_product(t_ref[...], p_ref[...]).astype(BF16)

    @pl.when(step >= split)
    def _():
        o_ref[...] = left_product(c_ref[...], p_ref[...]).astype(BF16)


def unit_gradients(tokens, cots, kept, which=(0, 1, 2), cost=FREE):
    rows, width = tokens.shape
    count = kept.shape[1] // 3
    wide = 384 if count % 384 == 0 else 128
    each = count // wide
    split = each * sum(i < 2 for i in which)
    first = which[0] * each
    held = pl.BlockSpec((rows, width), lambda i: (0, 0), pipeline_mode=pl.Buffered(1))
    return pl.pallas_call(
        functools.partial(grads_kernel, split),
        grid=(each * len(which),),
        in_specs=[held, held, pl.BlockSpec((rows, wide), lambda i: (0, first + i))],
        out_specs=pl.BlockSpec((width, wide), lambda i: (0, i)),
        out_shape=jax.ShapeDtypeStruct((width, len(which) * count), BF16),
        compiler_params=pltpu.CompilerParams(vmem_limit_bytes=56 * MIB),
        cost_estimate=cost,
    )(tokens, cots, kept)


def plane_gather(own, *others):
    cut = own.shape[0] // 2
    over_x, over_y, *others = together(dp_swap(own, 2), y_swap(own), *others)
    far_x = y_swap(over_x[:cut])
    far_y = dp_swap(over_y[cut:], 2)
    near = [own, over_y, over_x]
    across = [dp_swap(piece, 1) for piece in near]
    far_x, far_y, *across = together(far_x, far_y, *across)
    far = jnp.concatenate([far_x, far_y], axis=0)
    return near + [far] + across + [dp_swap(far, 1)], others


def plane_scatter(near, over_core, beside):
    t = near.shape[0] // 4
    cut = t // 2

    def summed(low, high):
        return near[low:high] + over_core[low:high].astype(F32)

    corner = summed(3 * t, 4 * t).astype(BF16)
    corner_x, corner_y = beside[0](corner, dp_swap(corner[:cut], 2), y_swap(corner[cut:]))
    to_y = jnp.concatenate(
        [summed(t, t + cut) + corner_x.astype(F32), summed(t + cut, 2 * t)], axis=0
    ).astype(BF16)
    to_x = jnp.concatenate(
        [summed(2 * t, 2 * t + cut), summed(2 * t + cut, 3 * t) + corner_y.astype(F32)], axis=0
    ).astype(BF16)
    over_x, over_y = beside[1](to_x, dp_swap(to_x, 2), y_swap(to_y))
    return summed(0, t) + over_x.astype(F32) + over_y.astype(F32)


def sum_over(values, axes):
    for axis in axes:
        size = lax.axis_size(axis)
        flip = 1
        while flip < size:
            values = values + lax.ppermute(values, axis, [(i, i ^ flip) for i in range(size)])
            flip *= 2
    return values


def on_device(
    hidden, cotangent, segments, positions, first_gain,
    query_weight, query_bias, key_weight, key_bias, value_weight, value_bias,
    out_weight, second_gain, gate_weight, up_weight, down_weight,
):
    n_dp, n_seq = lax.axis_size("dp"), lax.axis_size("seq")
    dp, seq, tensor = (lax.axis_index(a) for a in ("dp", "seq", "tensor"))
    rows, width = hidden.shape
    half = rows // 2
    share = query_weight.shape[0]
    group = segments.shape[0]
    blocks = group // rows
    q_width, kv_width = query_weight.shape[1], key_weight.shape[1]
    kv_end = q_width + kv_width
    dp_owners = jnp.stack([dp ^ k for k in range(n_dp)]).astype(jnp.int32)
    dp_slots = (dp_owners % 2) * (n_dp // 2) + dp_owners // 2
    seq_places = jnp.stack([(seq - s) % n_seq for s in range(n_seq)]).astype(jnp.int32)

    def vector_in(vector):
        parts = vector.reshape(n_dp // 2, 2, n_seq, share)
        return parts.transpose(2, 1, 0, 3).reshape(width).astype(F32)

    def vector_out(vector):
        parts = vector.reshape(n_seq, 2, n_dp // 2, share)
        return parts.transpose(2, 1, 0, 3).reshape(width)

    index = jnp.arange(width, dtype=jnp.int32)
    owner, place = index // (share * n_seq), index // share % n_seq
    slot = owner % 2 * (n_dp // 2) + owner // 2
    inner_of = (place * n_dp + slot) * share + index % share
    shuffle = (inner_of[:, None] == index[None, :]).astype(BF16)

    def relative(values):
        turned = jnp.concatenate([values[half:], values[:half]], axis=0)
        return jnp.where(tensor == 0, values, turned)

    def to_inner(values):
        return product(relative(values), shuffle).astype(BF16)

    def from_inner(values):
        return right_product(values, shuffle).astype(BF16)

    gain_first, gain_second = vector_in(first_gain), vector_in(second_gain)

    def slots_of(flips):
        return jnp.stack(
            [seq_places[s] * n_dp + dp_slots[k] for k in flips for s in range(n_seq)]
        ).astype(jnp.int32)

    cut = Cut(gate_weight.shape[1], n_dp)

    def spread(pieces):
        return [dp_swap(piece, k) if k else piece for k, piece in enumerate(pieces)]

    def stack_units(pieces):
        return assemble(pieces, dp_slots).reshape(n_dp * share, pieces[0].shape[1])

    line = [jnp.concatenate([query_weight, key_weight, value_weight, out_weight.T], axis=1)]
    over_x = []
    for s in range(n_seq):
        over_x.append(dp_swap(line[s], 2))
        if s + 1 == n_seq:
            cot_own = to_inner(cotangent)
            over_x[s], cot_own = together(over_x[s], cot_own)
            break
        moved = z_shift(line[s], 1)
        if s == 0:
            first_parts, second_parts = cut_units(
                cut, (gate_weight, up_weight, down_weight.T), dp_owners
            )
            moved, over_x[s], *parts = together(moved, over_x[s], *first_parts, *second_parts)
            first_parts, second_parts = parts[:n_dp], parts[n_dp:]
        elif s == 1:
            first_parts = spread(first_parts)
            inputs = to_inner(hidden)
            moved, over_x[s], inputs, *first_parts = together(
                moved, over_x[s], inputs, *first_parts
            )
        elif s == 2:
            first_stacked = stack_units(first_parts)
            first_units = lax.all_gather(first_stacked, "seq", axis=0, tiled=True)
            moved, over_x[s], first_stacked = together(moved, over_x[s], first_stacked)
        else:
            moved, over_x[s] = together(moved, over_x[s])
        line.append(moved)
    mine = assemble(line + over_x, jnp.arange(2 * n_seq, dtype=jnp.int32))
    mine, *second_parts = together(mine, *second_parts)
    theirs = dp_swap(mine, 1)
    second_parts = spread(second_parts)
    all_places = slots_of((0, 2, 1, 3))

    own_place = relative(lax.dynamic_slice_in_dim(positions, seq * rows, rows))
    own_segment = relative(lax.dynamic_slice_in_dim(segments, seq * rows, rows))
    cosine, sine = rope_tables(own_place, HEAD_DIM)
    cosine = jnp.concatenate([cosine, cosine], axis=1)
    sine = jnp.concatenate([-sine, sine], axis=1)
    bias = jnp.concatenate([query_bias, key_bias, value_bias]).astype(F32)
    queries, own_kv, first_rounded, attention_weights = project(
        mine, theirs, all_places, inputs, gain_first, bias, cosine, sine, q_width, kv_width
    )
    qkv_end = q_width + 2 * kv_width
    attention_weights = attention_weights.reshape(width, qkv_end + q_width)
    qkv_full, out_full = attention_weights[:, :qkv_end], attention_weights[:, qkv_end:]
    own_kv, cot_own = together(own_kv, cot_own)
    cot_x = dp_swap(cot_own, 2)
    group_kv = [own_kv] + [z_shift(own_kv, s) for s in range(1, n_seq)]
    second_stacked = stack_units(second_parts)
    second_units = lax.all_gather(second_stacked, "seq", axis=0, tiled=True)
    *group_kv, second_stacked = together(*group_kv, second_stacked)
    group_kv = jnp.concatenate(group_kv, axis=0)
    keys, values = group_kv[:, :kv_width], group_kv[:, kv_width:]

    def key_rows(vector):
        taken = jnp.take(vector.reshape(blocks, rows), seq_places, axis=0)
        return relative(taken.T).T

    seg_k, pos_k = key_rows(segments), key_rows(positions)
    seen = pair_mask(
        own_segment[None, :, None], own_place[None, :, None], seg_k[:, None, :], pos_k[:, None, :]
    )
    flags = (jnp.any(seen, axis=(1, 2)).astype(jnp.int32) + jnp.all(seen, axis=(1, 2))).astype(
        jnp.int32
    )
    pairs = (
        own_segment[:, None], own_place[:, None], seg_k[:, None, :], pos_k[:, None, :], flags,
    )
    attended, lse = attend(queries, keys, values, *pairs)
    attended, cot_x = together(attended, cot_x)
    cot_pieces = [cot_own, cot_x, dp_swap(cot_own, 1), dp_swap(cot_x, 1)]

    def reduce_halves(part):
        return part[:half] + y_swap(part[half:].astype(BF16)).astype(F32)

    inputs_half = inputs[:half].astype(F32)
    out_theirs = y_swap(right_product(attended[half:], out_full).astype(BF16))
    out_mine = right_product(attended[:half], out_full)
    out_theirs, out_mine, *cot_pieces = together(out_theirs, out_mine, *cot_pieces)
    cots = assemble(cot_pieces, jnp.arange(4, dtype=jnp.int32)).reshape(-1, width)
    residual = inputs_half + out_mine + out_theirs.astype(F32)
    second_inverse = inverse_rms(residual)
    second_normed = residual * second_inverse
    second_rounded = (second_normed * gain_second).astype(BF16)

    gathered, (cots,) = plane_gather(second_rounded, cots)
    tokens = assemble(gathered, jnp.arange(len(gathered), dtype=jnp.int32)).reshape(-1, width)

    kept, *far = feed(tokens, cots, first_units, 1, None, None, F32)
    kept, *near = feed(tokens, cots, first_units, 0, kept, None, F32)
    first_gradient = unit_gradients(tokens, cots, kept)
    second_weights = after(second_units, first_gradient)
    second_kept, back_far, out_far = feed(tokens, cots, second_weights, 1, None, far, BF16)
    second_kept, back_near, out_near = feed(
        tokens, cots, second_weights, 0, second_kept, near, F32
    )
    second_gradients = []

    def cost_of(count):
        flops = 2 * count * tokens.size * cut.width[1]
        return pl.CostEstimate(flops=flops, bytes_accessed=0, transcendentals=0)

    def gradients_beside(which):
        def run(operand, *moved):
            gradient = unit_gradients(
                tokens, cots, after(second_kept, operand), which, cost_of(len(which))
            )
            *moved, gradient = together(*moved, gradient)
            second_gradients.append(gradient)
            return moved

        return run

    back_core, back_near = together(dp_swap(back_far, 1), back_near)
    second_back = plane_scatter(
        back_near, back_core, (gradients_beside((2,)), gradients_beside((0, 1)))
    )

    def scatter_units(gradient):
        return lax.psum_scatter(gradient, "seq", scatter_dimension=0, tiled=True)

    def exchange_units(mine):
        mine = mine.reshape(n_dp, share, mine.shape[1])
        pieces = []
        for k in range(n_dp):
            piece = lax.dynamic_index_in_dim(mine, dp_slots[k], 0, keepdims=False)
            pieces.append(dp_swap(piece, k) if k else piece)
        return pieces

    first_share = scatter_units(first_gradient)
    second_shares = [scatter_units(g) for g in second_gradients]

    residual_inner, second_gain_term = norm_backward(
        second_back, second_normed, second_inverse, gain_second
    )
    residual_back = cot_own[:half].astype(F32) + residual_inner
    back_half = residual_back.astype(BF16)
    back_other, out_core = together(y_swap(back_half), dp_swap(after(out_far, back_half), 1))
    attention_back = jnp.concatenate([back_half, back_other], axis=0)

    take = lax.dynamic_index_in_dim
    core, x = dp % 2, dp // 2

    def core_halves(gradient):
        parts = gradient.reshape(n_seq, 2, (n_dp // 2) * share, gradient.shape[1])
        return take(parts, core, 1, keepdims=False), take(parts, 1 - core, 1, keepdims=False)

    def x_halves(own, over_core):
        parts = own.astype(F32) + over_core.astype(F32)
        parts = parts.reshape(n_seq, n_dp // 2, share, own.shape[2])
        return take(parts, x, 1, keepdims=False), take(parts, 1 - x, 1, keepdims=False).astype(BF16)

    def place_of(parts, s):
        return take(parts, seq_places[s % n_seq], 0, keepdims=False)

    attended_back = product(attention_back, out_full).astype(BF16)
    out_own, out_sent = core_halves(
        left_product(attention_back, attended).astype(BF16)
    )
    attended_back, first_share, out_sent = together(attended_back, first_share, out_sent)

    over_core = dp_swap(out_sent, 1)
    query_linear_back, key_parts, value_parts = attend_back(
        queries, keys, values, attended_back, lse, cosine, sine, *pairs
    )

    def plain(operand, *moved):
        *moved, operand = together(*moved, operand)
        return moved

    kv_parts = jnp.concatenate([key_parts, value_parts], axis=1)
    kv_parts, over_core, query_linear_back = together(kv_parts, over_core, query_linear_back)

    kv_moved = [z_shift(kv_parts[s * rows : (s + 1) * rows], -s) for s in range(1, n_seq)]
    out_parts, out_sent = x_halves(out_own, over_core)
    out_over_x = dp_swap(out_sent, 2)
    query_own, query_sent = core_halves(
        left_product(first_rounded, query_linear_back).astype(BF16)
    )
    over_core = dp_swap(query_sent, 1)
    *kv_moved, out_over_x, over_core = together(*kv_moved, out_over_x, over_core)
    out_parts = out_parts + out_over_x.astype(F32)
    kv_back = kv_parts[:rows].astype(F32)
    for moved in kv_moved:
        kv_back = kv_back + moved.astype(F32)
    key_linear_back = rotate(
        kv_back[:, :kv_width], cosine[:, : HEAD_DIM // 2], -sine[:, HEAD_DIM // 2 :]
    )
    kv_linear_back = jnp.concatenate([key_linear_back, kv_back[:, kv_width:]], axis=1).astype(BF16)
    linear_back = jnp.concatenate([query_linear_back, kv_linear_back], axis=1)

    query_parts, query_sent = x_halves(query_own, over_core)
    query_over_x = dp_swap(query_sent, 2)
    kv_own, kv_sent = core_halves(left_product(first_rounded, kv_linear_back).astype(BF16))
    over_core = dp_swap(kv_sent, 1)
    first_theirs = y_swap(right_product(linear_back[half:], qkv_full).astype(BF16))
    first_mine = right_product(linear_back[:half], qkv_full)
    query_over_x, over_core, first_theirs, first_mine = together(
        query_over_x, over_core, first_theirs, first_mine
    )
    first_back = first_mine + first_theirs.astype(F32)
    query_parts = query_parts + query_over_x.astype(F32)
    large = jnp.concatenate([query_parts, out_parts], axis=2)

    kv_own, kv_sent = x_halves(kv_own, over_core)
    kv_over_x = dp_swap(kv_sent, 2)
    total = z_shift(place_of(large, 1).astype(BF16), 1)
    first_inverse = inverse_rms(inputs_half)
    input_inner, first_gain_term = norm_backward(
        first_back, inputs_half * first_inverse, first_inverse, gain_first
    )
    input_half = from_inner((residual_back + input_inner).astype(BF16))
    input_other = y_swap(input_half)
    total, kv_over_x, input_other = together(total, kv_over_x, input_other)
    input_gradient = relative(jnp.concatenate([input_half, input_other], axis=0))
    kv_rows = kv_own + kv_over_x.astype(F32)
    kv_total = place_of(kv_rows, 1).astype(BF16)
    first_received = exchange_units(first_share)
    for s in range(1, n_seq):
        total = place_of(large, s + 1) + total.astype(F32)
        kv_total = place_of(kv_rows, s + 1) + z_shift(kv_total, 1).astype(F32)
        if s + 1 < n_seq:
            total, kv_total = together(z_shift(total.astype(BF16), 1), kv_total.astype(BF16))
    large_share, kv_share = total, kv_total
    out_gradient = large_share[:, q_width:].T
    down_out = plane_scatter(out_near, out_core, (plain, plain))
    out_half = from_inner((residual + down_out).astype(BF16))
    output = relative(jnp.concatenate([out_half, y_swap(out_half)], axis=0))
    second_pieces = [exchange_units(share_of) for share_of in second_shares]
    gate_gradient, up_gradient, down_gradient = lay_units(
        cut, first_received + second_pieces[1] + second_pieces[0], dp_owners
    )
    down_gradient = down_gradient.T

    bias_terms = jnp.sum(linear_back.astype(F32), axis=0)
    sums = sum_over(
        jnp.concatenate([first_gain_term, second_gain_term, bias_terms]), ("dp", "seq")
    )
    gain_terms = sum_over(sums[: 2 * width], ("tensor",))
    bias_terms = sums[2 * width :]
    return (
        output,
        input_gradient,
        vector_out(gain_terms[:width]),
        large_share[:, :q_width],
        bias_terms[:q_width],
        kv_share[:, :kv_width],
        bias_terms[q_width:kv_end],
        kv_share[:, kv_width:],
        bias_terms[kv_end:],
        out_gradient,
        vector_out(gain_terms[width:]),
        gate_gradient,
        up_gradient,
        down_gradient,
    )


def solution(mesh):
    tokens = P(("dp", "seq"), None)
    by_row = P(("dp", "seq"), "tensor")
    by_column = P("tensor", ("dp", "seq"))
    heads = P("tensor")
    in_specs = (
        tokens, tokens, P("dp"), P("dp"), P(), by_row, heads, by_row, heads, by_row, heads,
        by_column, P(), by_row, by_row, by_column,
    )
    out_specs = (
        tokens, tokens, P(), by_row, heads, by_row, heads, by_row, heads, by_column, P(),
        by_row, by_row, by_column,
    )
    return jax.shard_map(
        on_device, mesh=mesh, in_specs=in_specs, out_specs=out_specs, check_vma=False
    )
```

time: 2020 us -> 682 us (0.34)
  waiting for transfers between devices: 1530 us -> 228 us
  Pallas kernels: 0 us -> 209 us
  matrix products: 210 us -> 39.8 us
  blocking collectives: 169 us -> 0 us
  starting transfers between devices: 0.68 us -> 86.7 us
    reduce_scatter x9 -> x3, waiting for transfers between devices: 1040 us -> 0.01 us  [scatter_units(): return lax.psum_scatter(gradient, 'seq', scatter_dimension=0, tiled=True)]
    all_gather x5 -> x2, waiting for transfers between devices: 298 us -> 0.01 us  [the longest x1 0.01 us: on_device(): first_units = lax.all_gather(first_stacked, 'seq', axis=0, tiled=True)]
    ppermute x0 -> x72, waiting for transfers between devices: none -> 228 us  [the longest x15 92 us: z_shift(): lax.ppermute(value, 'seq', [(i, (i + step) % size) for i in range(size)])]
    pallas_call x0 -> x17, Pallas kernels: none -> 209 us  [the longest x4 76.9 us: feed(): pl.pallas_call(functools.partial(feed_kernel, columns // 3, earlier is no...]
    psum x3 -> x0, waiting for transfers between devices: 189 us -> none  [the longest x1 84 us: on_device(): lax.psum(right_product(gate_back, gate_full) + right_product(upper_back,...]
    all_gather x4 -> x0, blocking collectives: 108 us -> none  [the longest x1 41.4 us: on_device(): lax.all_gather(value_weight, ('dp', 'seq'), axis=0, tiled=True)]
    ppermute x0 -> x72, starting transfers between devices: none -> 86.3 us  [the longest x15 34.3 us: z_shift(): lax.ppermute(value, 'seq', [(i, (i + step) % size) for i in range(size)])]
    dot_general x34 -> x3, matrix products: 94.9 us -> 12.6 us  [product(): return jnp.dot(left, right, preferred_element_type=F32)]
  transfers between devices with their start and end apart: 17 -> 77, of which waited for: 14 -> 33; matrix products, arithmetic and copies ran while one was open for 8% -> 15% of each run, Pallas kernels for 0% -> 27%
where the time goes in v1:
time: 682 us; the launch traced here: 675 us
  waiting for transfers between devices  228 us (33%)
  Pallas kernels  209 us (31%)
  starting transfers between devices  86.7 us (13%)
  other arithmetic  40.1 us (6%)
  matrix products  39.8 us (6%)
  local copies, waits for them, and re-layouts  38.9 us (6%)
  between operations  32.5 us (5%)
    ppermute x15, waiting for transfers between devices, z_shift(): lax.ppermute(value, 'seq', [(i, (i + step) % size) for i in range(size)])  92 us
    pallas_call x4, Pallas kernels, feed(): pl.pallas_call(functools.partial(feed_kernel, columns // 3, earlier is no...  76.9 us
    ppermute x41, waiting for transfers between devices, dp_swap(): return lax.ppermute(value, 'dp', [(i, i ^ flip) for i in range(size)])  73.3 us
    ppermute x11, waiting for transfers between devices, y_swap(): return lax.ppermute(value, 'tensor', [(0, 1), (1, 0)])  57.9 us
    pallas_call x3, Pallas kernels, unit_gradients(): pl.pallas_call(functools.partial(grads_kernel, split), grid=(each * len(w...  50.8 us
    ppermute x15, starting transfers between devices, z_shift(): lax.ppermute(value, 'seq', [(i, (i + step) % size) for i in range(size)])  34.3 us
    pallas_call x1, Pallas kernels, attend_back(): pl.pallas_call(functools.partial(attend_back_kernel, rows, HEAD_DIM ** (-...  29.9 us
    pallas_call x1, Pallas kernels, attend(): pl.pallas_call(functools.partial(attend_kernel, rows, HEAD_DIM ** (-0.5)...  28.7 us
  transfers between devices with their start and end apart: 77, of which 33 were waited for; matrix products, arithmetic and copies ran while one was open for 15% of the time, Pallas kernels for 27%

profile of v1, /device:TPU:0, one launch (start us, length us, event | category | flops | bytes accessed | tf_op | source)
XLA Modules:
  0.0 674.7 jit_solution(15923741013946735891)
XLA Ops:
  8.3 3.0 collective-permute-start.1
  25.1 4.2 fusion.8.x_ref
  29.2 9.2 %collective-permute-done.5.refs_2_ = bf16[96,1152]{1,0:T(8,128)(2,1)S(1)} collective-permute-done((bf16[96,1152]{1,0:T(8,128)(2,1)S(1)}, bf16[96,1152]{1,0:T(8,128)(2,1)S(1)}, u32[]{:S(2)}, u32[]{:S(2)}) %collective-permute-start.5) | collective-permute-done | bytes 221216 | tf_op jit(solution)/shard_map/ppermute | solution.py:44
  44.7 7.7 %collective-permute-done.8.refs_6_ = bf16[96,1792]{1,0:T(8,128)(2,1)S(1)} collective-permute-done((bf16[96,1792]{1,0:T(8,128)(2,1)S(1)}, bf16[96,1792]{1,0:T(8,128)(2,1)S(1)}, u32[]{:S(2)}, u32[]{:S(2)}) %collective-permute-start.8) | collective-permute-done | bytes 344096 | tf_op jit(solution)/shard_map/ppermute | solution.py:44
  52.4 5.0 collective-permute-done.7.refs_3_
  57.4 4.2 fusion.9.refs_0_
  61.6 5.3 collective-permute-done.9.refs_7_
  70.5 11.2 %collective-permute-done.15.refs_2_ = bf16[96,2304]{1,0:T(8,128)(2,1)S(1)} collective-permute-done((bf16[96,2304]{1,0:T(8,128)(2,1)S(1)}, bf16[96,2304]{1,0:T(8,128)(2,1)S(1)}, u32[]{:S(2)}, u32[]{:S(2)}) %collective-permute-start.15) | collective-permute-done | bytes 442400 | tf_op jit(solution)/shard_map/ppermute | solution.py:44
  81.7 8.6 %collective-permute-done.16.refs_3_ = bf16[96,2304]{1,0:T(8,128)(2,1)S(1)} collective-permute-done((bf16[96,2304]{1,0:T(8,128)(2,1)S(1)}, bf16[96,2304]{1,0:T(8,128)(2,1)S(1)}, u32[]{:S(2)}, u32[]{:S(2)}) %collective-permute-start.16) | collective-permute-done | bytes 442400 | tf_op jit(solution)/shard_map/ppermute | solution.py:44
  109.7 6.1 shard_map.266
  123.3 7.0 %collective-permute-done.13 = bf16[512,256]{1,0:T(8,128)(2,1)S(1)} collective-permute-done((bf16[512,256]{1,0:T(8,128)(2,1)}, bf16[512,256]{1,0:T(8,128)(2,1)S(1)}, u32[]{:S(2)}, u32[]{:S(2)}) %collective-permute-start.13) | collective-permute-done | bytes 262176 | tf_op jit(solution)/shard_map/ppermute | solution.py:53
  130.3 30.2 %collective-permute-done.12 = bf16[512,256]{1,0:T(8,128)(2,1)S(1)} collective-permute-done((bf16[512,256]{1,0:T(8,128)(2,1)}, bf16[512,256]{1,0:T(8,128)(2,1)S(1)}, u32[]{:S(2)}, u32[]{:S(2)}) %collective-permute-start.12) | collective-permute-done | bytes 262176 | tf_op jit(solution)/shard_map/ppermute | solution.py:53
  161.7 28.7 %shard_map.268 = (bf16[512,768]{1,0:T(8,128)(2,1)S(1)}, f32[6,512,1]{2,1,0:T(8,128)S(1)}) custom-call(s32[4]{0:T(128)S(1)} %convert_add_fusion.8.flag_ref, bf16[512,768]{1,0:T(8,128)(2,1)S(1)} %get-tuple-element.164.q_ref, bf16[2048,128]{1,0:T(8,128)(2,1)S(1)} %get-tuple-element.295.k_ref, bf16[2048,128]{1,0:T(8,128)(2,1)S(1)} %get-tuple-element.294.v_ref, ...), custom_call_target="tpu_custom_call" | custom-call | tf_op jit(solution)/shard_map/pallas_call | solution.py:137
  190.6 3.9 convolution_convert_fusion.2
  197.3 16.8 %collective-permute-done.18 = bf16[256,1536]{1,0:T(8,128)(2,1)S(1)} collective-permute-done((bf16[256,1536]{1,0:T(8,128)(2,1)}, bf16[256,1536]{1,0:T(8,128)(2,1)S(1)}, u32[]{:S(2)}, u32[]{:S(2)}) %collective-permute-start.18) | collective-permute-done | bytes 786464 | tf_op jit(solution)/shard_map/ppermute | solution.py:48
  216.4 3.5 shard_map.269
  222.7 11.6 %collective-permute-done.22.refs_1_ = bf16[256,1536]{1,0:T(8,128)(2,1)S(1)} collective-permute-done((bf16[256,1536]{1,0:T(8,128)(2,1)S(1)}, bf16[256,1536]{1,0:T(8,128)(2,1)S(1)}, u32[]{:S(2)}, u32[]{:S(2)}) %collective-permute-start.22) | collective-permute-done | bytes 786464 | tf_op jit(solution)/shard_map/ppermute | solution.py:48
  236.9 9.3 %collective-permute-done.23 = bf16[128,1536]{1,0:T(8,128)(2,1)S(1)} collective-permute-done((bf16[128,1536]{1,0:T(8,128)(2,1)S(1)}, bf16[128,1536]{1,0:T(8,128)(2,1)S(1)}, u32[]{:S(2)}, u32[]{:S(2)}) %collective-permute-start.23) | collective-permute-done | bytes 393248 | tf_op jit(solution)/shard_map/ppermute | solution.py:48
  253.6 14.9 %shard_map.271 = (bf16[2048,1152]{1,0:T(8,128)(2,1)}, f32[1024,1536]{1,0:T(8,128)}, f32[1024,1536]{1,0:T(8,128)}) custom-call(bf16[2048,1536]{1,0:T(8,128)(2,1)} %bitcast.167, bf16[2048,1536]{1,0:T(8,128)(2,1)} %bitcast.160, bf16[1536,1152]{1,0:T(8,128)(2,1)} %all-gather.5.cloned.1.call-done.refs_2_), custom_call_target="tpu_custom_call" | custom-call | tf_op jit(solution)/shard_map/pallas_call | solution.py:531
  268.5 14.9 %shard_map.272 = (bf16[2048,1152]{1,0:T(8,128)(2,1)}, f32[1024,1536]{1,0:T(8,128)}, f32[1024,1536]{1,0:T(8,128)}) custom-call(bf16[2048,1536]{1,0:T(8,128)(2,1)} %bitcast.168, bf16[2048,1536]{1,0:T(8,128)(2,1)} %bitcast.161, bf16[1536,1152]{1,0:T(8,128)(2,1)} %all-gather.5.cloned.1.call-done.refs_2_, ...), custom_call_target="tpu_custom_call", output_to_operand_aliasing={{0}: (3, {})} | custom-call | tf_op jit(solution)/shard_map/pallas_call | solution.py:531
  283.4 17.1 %shard_map.273 = bf16[1536,1152]{1,0:T(8,128)(2,1)} custom-call(bf16[2048,1536]{1,0:T(8,128)(2,1)} %bitcast.169, bf16[2048,1536]{1,0:T(8,128)(2,1)} %bitcast.162, bf16[2048,1152]{1,0:T(8,128)(2,1)} %get-tuple-element.196.p_ref), custom_call_target="tpu_custom_call" | custom-call | tf_op jit(solution)/shard_map/pallas_call | solution.py:567
  300.5 23.1 %shard_map.274 = (bf16[2048,2304]{1,0:T(8,128)(2,1)}, bf16[1024,1536]{1,0:T(8,128)(2,1)}, bf16[1024,1536]{1,0:T(8,128)(2,1)}) custom-call(bf16[2048,1536]{1,0:T(8,128)(2,1)} %bitcast.170, bf16[2048,1536]{1,0:T(8,128)(2,1)} %bitcast.163, bf16[1536,2304]{1,0:T(8,128)(2,1)} %all-gather.3.cloned.1.call-done.refs_2_, f32[1024,1536]{1,0:T(8,128)} %get-tuple-element.200.refs_3_, ...), custom_call_target="tpu_custom_call" | custom-call | tf_op jit(solution)/shard_map/pallas_call | solution.py:531
  323.8 24.0 %shard_map.275 = (bf16[2048,2304]{1,0:T(8,128)(2,1)}, f32[1024,1536]{1,0:T(8,128)}, f32[1024,1536]{1,0:T(8,128)}) custom-call(bf16[2048,1536]{1,0:T(8,128)(2,1)} %bitcast.171, bf16[2048,1536]{1,0:T(8,128)(2,1)} %bitcast.164, bf16[1536,2304]{1,0:T(8,128)(2,1)} %all-gather.3.cloned.1.call-done.refs_2_, ...), custom_call_target="tpu_custom_call", output_to_operand_aliasing={{0}: (5, {})} | custom-call | tf_op jit(solution)/shard_map/pallas_call | solution.py:531
  351.3 13.2 %shard_map.276 = bf16[1536,768]{1,0:T(8,128)(2,1)} custom-call(bf16[2048,1536]{1,0:T(8,128)(2,1)} %bitcast.172, bf16[2048,1536]{1,0:T(8,128)(2,1)} %bitcast.165, bf16[2048,2304]{1,0:T(8,128)(2,1)} %get-tuple-element.212.p_ref), custom_call_target="tpu_custom_call" | custom-call | flops 4831838208 | tf_op jit(solution)/shard_map/pallas_call | solution.py:567
  371.8 20.5 %shard_map.277 = bf16[1536,1536]{1,0:T(8,128)(2,1)} custom-call(bf16[2048,1536]{1,0:T(8,128)(2,1)} %bitcast.173, bf16[2048,1536]{1,0:T(8,128)(2,1)} %bitcast.166, bf16[2048,2304]{1,0:T(8,128)(2,1)} %get-tuple-element.212.p_ref), custom_call_target="tpu_custom_call" | custom-call | flops 9663676416 | tf_op jit(solution)/shard_map/pallas_call | solution.py:567
  392.3 4.1 multiply_reduce_fusion
  399.4 19.5 %collective-permute-done.34 = bf16[256,1536]{1,0:T(8,128)(2,1)} collective-permute-done((bf16[256,1536]{1,0:T(8,128)(2,1)S(1)}, bf16[256,1536]{1,0:T(8,128)(2,1)}, u32[]{:S(2)}, u32[]{:S(2)}) %collective-permute-start.34) | collective-permute-done | bytes 786464 | tf_op jit(solution)/shard_map/ppermute | solution.py:48
  427.7 4.2 fusion.43.do_ref
  447.5 29.9 %shard_map.278 = (bf16[512,768]{1,0:T(8,128)(2,1)}, bf16[2048,128]{1,0:T(8,128)(2,1)}, bf16[2048,128]{1,0:T(8,128)(2,1)}) custom-call(s32[4]{0:T(128)} %copy-done.26, bf16[512,768]{1,0:T(8,128)(2,1)} %copy-done.7, bf16[2048,128]{1,0:T(8,128)(2,1)} %copy-done.6, bf16[2048,128]{1,0:T(8,128)(2,1)} %copy-done.5, bf16[512,768]{1,0:T(8,128)(2,1)} %fusion.43.do_ref, ...), custom_call_target="tpu_custom_call" | custom-call | tf_op jit(solution)/shard_map/pallas_call | solution.py:248
  483.8 5.6 fusion.17
  495.9 14.4 %collective-permute-start.44 = (bf16[512,256]{1,0:T(8,128)(2,1)S(1)}, bf16[512,256]{1,0:T(8,128)(2,1)S(1)}, u32[]{:S(2)}, u32[]{:S(2)}) collective-permute-start(bf16[512,256]{1,0:T(8,128)(2,1)S(1)} %get-tuple-element.291), channel_id=1, source_target_pairs={{0,2},{2,4},{4,6},{6,0},{1,3},{3,5},{5,7},{7,1},{8,10},{10,12},{12... | collective-permute-start | bytes 786440 | tf_op jit(solution)/shard_map/ppermute | solution.py:53
  515.0 3.5 maximum_select_fusion.4
  518.5 4.0 collective-permute-done.44
  522.5 14.5 %collective-permute-done.43 = bf16[512,256]{1,0:T(8,128)(2,1)S(1)} collective-permute-done((bf16[512,256]{1,0:T(8,128)(2,1)S(1)}, bf16[512,256]{1,0:T(8,128)(2,1)S(1)}, u32[]{:S(2)}, u32[]{:S(2)}) %collective-permute-start.43) | collective-permute-done | bytes 262176 | tf_op jit(solution)/shard_map/ppermute | solution.py:53
  537.7 9.8 %collective-permute-done.42 = bf16[512,256]{1,0:T(8,128)(2,1)S(1)} collective-permute-done((bf16[512,256]{1,0:T(8,128)(2,1)S(1)}, bf16[512,256]{1,0:T(8,128)(2,1)S(1)}, u32[]{:S(2)}, u32[]{:S(2)}) %collective-permute-start.42) | collective-permute-done | bytes 262176 | tf_op jit(solution)/shard_map/ppermute | solution.py:53
  549.5 3.0 fusion.14
  559.6 3.4 fusion.10
  563.0 9.4 %collective-permute-done.47 = bf16[4,96,768]{2,1,0:T(8,128)(2,1)S(1)} collective-permute-done((bf16[4,96,768]{2,1,0:T(8,128)(2,1)S(1)}, bf16[4,96,768]{2,1,0:T(8,128)(2,1)S(1)}, u32[]{:S(2)}, u32[]{:S(2)}) %collective-permute-start.47) | collective-permute-done | bytes 589856 | tf_op jit(solution)/shard_map/ppermute | solution.py:44
  573.2 4.1 fusion.18
  581.3 15.8 %collective-permute-start.55 = (f32[4096]{0:T(1024)S(1)}, f32[4096]{0:T(1024)S(1)}, u32[]{:S(2)}, u32[]{:S(2)}) collective-permute-start(f32[4096]{0:T(1024)S(1)} %add.490), channel_id=1, source_target_pairs={{0,2},{2,0},{4,6},{6,4},{1,3},{3,1},{5,7},{7,5},{8,10},{10,8},{12,... | collective-permute-start | bytes 49160 | tf_op jit(solution)/shard_map/ppermute | solution.py:614
  598.8 3.3 collective-permute-start.56
  609.1 4.5 collective-permute-done.51
  613.8 7.1 %collective-permute-start.59 = (bf16[96,256]{1,0:T(8,128)(2,1)S(1)}, bf16[96,256]{1,0:T(8,128)(2,1)S(1)}, u32[]{:S(2)}, u32[]{:S(2)}) collective-permute-start(bf16[96,256]{1,0:T(8,128)(2,1)S(1)} %fusion.81), channel_id=1, source_target_pairs={{0,2},{2,4},{4,6},{6,0},{1,3},{3,5},{5,7},{7,1},{8,10},{10,12},{12... | collective-permute-start | bytes 147464 | tf_op jit(solution)/shard_map/ppermute | solution.py:53
  623.1 3.1 collective-permute-done.59
  626.2 6.1 collective-permute-done.58
  638.8 5.7 collective-permute-done.60
  652.2 12.7 %collective-permute-done.70.refs_10_ = bf16[96,768]{1,0:T(8,128)(2,1)S(1)} collective-permute-done((bf16[96,768]{1,0:T(8,128)(2,1)S(1)}, bf16[96,768]{1,0:T(8,128)(2,1)S(1)}, u32[]{:S(2)}, u32[]{:S(2)}) %collective-permute-start.70) | collective-permute-done | bytes 147488 | tf_op jit(solution)/shard_map/ppermute | solution.py:44
  664.9 3.2 shard_map.279
  (437 shorter events, 148.3 us)
Async XLA Ops:
  7.2 246.4 %all-gather.5.cloned.1.call-start = ((), (), s32[]{:S(2)}) async-start(), calls=%async_computation.4 | async-start | bytes 4423680 | tf_op jit(solution)/shard_map/all_gather | solution.py:699
  22.7 16.5 %collective-permute-start.3 = (bf16[96,1792]{1,0:T(8,128)(2,1)S(1)}, bf16[96,1792]{1,0:T(8,128)(2,1)S(1)}, u32[]{:S(2)}, u32[]{:S(2)}) collective-permute-start(bf16[96,1792]{1,0:T(8,128)(2,1)S(1)} %collective-permute-done.refs_1_), channel_id=1, source_target_pairs={{0,16},{8,24},{16,0},{24,8},{1,17},{9,25},{17,1},{25,9},{2,18},{10... | collective-permute-start | bytes 1032200 | tf_op jit(solution)/shard_map/ppermute | solution.py:44
  23.2 15.9 %collective-permute-start.2 = (bf16[96,1792]{1,0:T(8,128)(2,1)S(1)}, bf16[96,1792]{1,0:T(8,128)(2,1)S(1)}, u32[]{:S(2)}, u32[]{:S(2)}) collective-permute-start(bf16[96,1792]{1,0:T(8,128)(2,1)S(1)} %collective-permute-done.refs_1_), channel_id=1, source_target_pairs={{0,2},{2,4},{4,6},{6,0},{1,3},{3,5},{5,7},{7,1},{8,10},{10,12},{12... | collective-permute-start | bytes 1032200 | tf_op jit(solution)/shard_map/ppermute | solution.py:53
  23.2 15.2 %collective-permute-start.5 = (bf16[96,1152]{1,0:T(8,128)(2,1)S(1)}, bf16[96,1152]{1,0:T(8,128)(2,1)S(1)}, u32[]{:S(2)}, u32[]{:S(2)}) collective-permute-start(bf16[96,1152]{1,0:T(8,128)(2,1)S(1)} %get-tuple-element.146), channel_id=1, source_target_pairs={{0,16},{8,24},{16,0},{24,8},{1,17},{9,25},{17,1},{25,9},{2,18},{10... | collective-permute-start | bytes 663560 | tf_op jit(solution)/shard_map/ppermute | solution.py:44
  24.7 14.4 %collective-permute-start.6 = (bf16[96,1152]{1,0:T(8,128)(2,1)S(1)}, bf16[96,1152]{1,0:T(8,128)(2,1)S(1)}, u32[]{:S(2)}, u32[]{:S(2)}) collective-permute-start(bf16[96,1152]{1,0:T(8,128)(2,1)S(1)} %get-tuple-element.147), channel_id=1, source_target_pairs={{0,24},{8,16},{16,8},{24,0},{1,25},{9,17},{17,9},{25,1},{2,26},{10... | collective-permute-start | bytes 663560 | tf_op jit(solution)/shard_map/ppermute | solution.py:44
  41.8 258.7 %all-gather.3.cloned.1.call-start = ((), (), s32[]{:S(2)}) async-start(), calls=%async_computation.3 | async-start | bytes 8847360 | tf_op jit(solution)/shard_map/all_gather | solution.py:726
  43.2 14.2 %collective-permute-start.7 = (bf16[96,1792]{1,0:T(8,128)(2,1)S(1)}, bf16[96,1792]{1,0:T(8,128)(2,1)S(1)}, u32[]{:S(2)}, u32[]{:S(2)}) collective-permute-start(bf16[96,1792]{1,0:T(8,128)(2,1)S(1)} %collective-permute-done.2.refs_2_), channel_id=1, source_target_pairs={{0,2},{2,4},{4,6},{6,0},{1,3},{3,5},{5,7},{7,1},{8,10},{10,12},{12... | collective-permute-start | bytes 1032200 | tf_op jit(solution)/shard_map/ppermute | solution.py:53
  69.6 20.7 %collective-permute-start.16 = (bf16[96,2304]{1,0:T(8,128)(2,1)S(1)}, bf16[96,2304]{1,0:T(8,128)(2,1)S(1)}, u32[]{:S(2)}, u32[]{:S(2)}) collective-permute-start(bf16[96,2304]{1,0:T(8,128)(2,1)S(1)} %copy-done.31), channel_id=1, source_target_pairs={{0,24},{8,16},{16,8},{24,0},{1,25},{9,17},{17,9},{25,1},{2,26},{10... | collective-permute-start | bytes 1327112 | tf_op jit(solution)/shard_map/ppermute | solution.py:44
  93.2 338.8 %reduce-scatter.4.cloned.1.call-start = ((), (), s32[]{:S(2)}) async-start(), calls=%async_computation.5 | async-start | bytes 4423680 | tf_op jit(solution)/shard_map/reduce_scatter | solution.py:796
  93.4 16.2 %collective-permute-start.10 = (bf16[8,96,1792]{2,1,0:T(8,128)(2,1)S(1)}, bf16[8,96,1792]{2,1,0:T(8,128)(2,1)}, u32[]{:S(2)}, u32[]{:S(2)}) collective-permute-start(bf16[8,96,1792]{2,1,0:T(8,128)(2,1)S(1)} %shard_map.265.mine_ref), channel_id=1, source_target_pairs={{0,8},{8,0},{16,24},{24,16},{1,9},{9,1},{17,25},{25,17},{2,10},{10... | collective-permute-start | bytes 8257544 | tf_op jit(solution)/shard_map/ppermute | solution.py:44
  117.0 73.5 %collective-permute-start.17 = (bf16[512,1536]{1,0:T(8,128)(2,1)}, bf16[512,1536]{1,0:T(8,128)(2,1)}, u32[]{:S(2)}, u32[]{:S(2)}) collective-permute-start(bf16[512,1536]{1,0:T(8,128)(2,1)} %fusion.9.refs_0_), channel_id=1, source_target_pairs={{0,16},{8,24},{16,0},{24,8},{1,17},{9,25},{17,1},{25,9},{2,18},{10... | collective-permute-start | bytes 4718600 | tf_op jit(solution)/shard_map/ppermute | solution.py:44
  117.9 42.6 %collective-permute-start.12 = (bf16[512,256]{1,0:T(8,128)(2,1)}, bf16[512,256]{1,0:T(8,128)(2,1)S(1)}, u32[]{:S(2)}, u32[]{:S(2)}) collective-permute-start(bf16[512,256]{1,0:T(8,128)(2,1)} %get-tuple-element.172), channel_id=1, source_target_pairs={{0,4},{2,6},{4,0},{6,2},{1,5},{3,7},{5,1},{7,3},{8,12},{10,14},{12... | collective-permute-start | bytes 786440 | tf_op jit(solution)/shard_map/ppermute | solution.py:53
  117.9 42.6 %collective-permute-start.11 = (bf16[512,256]{1,0:T(8,128)(2,1)}, bf16[512,256]{1,0:T(8,128)(2,1)S(1)}, u32[]{:S(2)}, u32[]{:S(2)}) collective-permute-start(bf16[512,256]{1,0:T(8,128)(2,1)} %get-tuple-element.172), channel_id=1, source_target_pairs={{0,2},{2,4},{4,6},{6,0},{1,3},{3,5},{5,7},{7,1},{8,10},{10,12},{12... | collective-permute-start | bytes 786440 | tf_op jit(solution)/shard_map/ppermute | solution.py:53
  123.2 74.1 %collective-permute-start.19 = (bf16[512,1536]{1,0:T(8,128)(2,1)}, bf16[512,1536]{1,0:T(8,128)(2,1)}, u32[]{:S(2)}, u32[]{:S(2)}) collective-permute-start(bf16[512,1536]{1,0:T(8,128)(2,1)} %fusion.9.refs_0_), channel_id=1, source_target_pairs={{0,8},{8,0},{16,24},{24,16},{1,9},{9,1},{17,25},{25,17},{2,10},{10... | collective-permute-start | bytes 4718600 | tf_op jit(solution)/shard_map/ppermute | solution.py:44
  190.5 23.7 %collective-permute-start.20 = (bf16[512,1536]{1,0:T(8,128)(2,1)}, bf16[512,1536]{1,0:T(8,128)(2,1)}, u32[]{:S(2)}, u32[]{:S(2)}) collective-permute-start(bf16[512,1536]{1,0:T(8,128)(2,1)} %collective-permute-done.17.refs_1_), channel_id=1, source_target_pairs={{0,8},{8,0},{16,24},{24,16},{1,9},{9,1},{17,25},{25,17},{2,10},{10... | collective-permute-start | bytes 4718600 | tf_op jit(solution)/shard_map/ppermute | solution.py:44
  194.5 19.7 %collective-permute-start.18 = (bf16[256,1536]{1,0:T(8,128)(2,1)}, bf16[256,1536]{1,0:T(8,128)(2,1)S(1)}, u32[]{:S(2)}, u32[]{:S(2)}) collective-permute-start(bf16[256,1536]{1,0:T(8,128)(2,1)} %convolution_convert_fusion.2), channel_id=1, source_target_pairs={{0,1},{1,0},{2,3},{3,2},{4,5},{5,4},{6,7},{7,6},{8,9},{9,8},{10,11... | collective-permute-start | bytes 2359304 | tf_op jit(solution)/shard_map/ppermute | solution.py:48
  215.5 18.8 %collective-permute-start.22 = (bf16[256,1536]{1,0:T(8,128)(2,1)S(1)}, bf16[256,1536]{1,0:T(8,128)(2,1)S(1)}, u32[]{:S(2)}, u32[]{:S(2)}) collective-permute-start(bf16[256,1536]{1,0:T(8,128)(2,1)S(1)} %multiply_convert_fusion.refs_0_), channel_id=1, source_target_pairs={{0,1},{1,0},{2,3},{3,2},{4,5},{5,4},{6,7},{7,6},{8,9},{9,8},{10,11... | collective-permute-start | bytes 2359304 | tf_op jit(solution)/shard_map/ppermute | solution.py:48
  215.8 18.7 %collective-permute-start.21 = (bf16[256,1536]{1,0:T(8,128)(2,1)S(1)}, bf16[256,1536]{1,0:T(8,128)(2,1)S(1)}, u32[]{:S(2)}, u32[]{:S(2)}) collective-permute-start(bf16[256,1536]{1,0:T(8,128)(2,1)S(1)} %multiply_convert_fusion.refs_0_), channel_id=1, source_target_pairs={{0,16},{8,24},{16,0},{24,8},{1,17},{9,25},{17,1},{25,9},{2,18},{10... | collective-permute-start | bytes 2359304 | tf_op jit(solution)/shard_map/ppermute | solution.py:44
  215.8 21.1 %collective-permute-start.25 = (bf16[256,1536]{1,0:T(8,128)(2,1)S(1)}, bf16[256,1536]{1,0:T(8,128)(2,1)S(1)}, u32[]{:S(2)}, u32[]{:S(2)}) collective-permute-start(bf16[256,1536]{1,0:T(8,128)(2,1)S(1)} %multiply_convert_fusion.refs_0_), channel_id=1, source_target_pairs={{0,8},{8,0},{16,24},{24,16},{1,9},{9,1},{17,25},{25,17},{2,10},{10... | collective-permute-start | bytes 2359304 | tf_op jit(solution)/shard_map/ppermute | solution.py:44
  323.6 24.2 %collective-permute-start.29 = (bf16[1024,1536]{1,0:T(8,128)(2,1)}, bf16[1024,1536]{1,0:T(8,128)(2,1)}, u32[]{:S(2)}, u32[]{:S(2)}) collective-permute-start(bf16[1024,1536]{1,0:T(8,128)(2,1)} %get-tuple-element.204), channel_id=1, source_target_pairs={{0,8},{8,0},{16,24},{24,16},{1,9},{9,1},{17,25},{25,17},{2,10},{10... | collective-permute-start | bytes 9437192 | tf_op jit(solution)/shard_map/ppermute | solution.py:44
  323.8 170.2 %reduce-scatter.8.cloned.1.call-start = ((), (), s32[]{:S(2)}) async-start(), calls=%async_computation.7 | async-start | bytes 2949120 | tf_op jit(solution)/shard_map/reduce_scatter | solution.py:796
  350.5 14.1 %collective-permute-start.31 = (bf16[128,1536]{1,0:T(8,128)(2,1)}, bf16[128,1536]{1,0:T(8,128)(2,1)S(1)}, u32[]{:S(2)}, u32[]{:S(2)}) collective-permute-start(bf16[128,1536]{1,0:T(8,128)(2,1)} %get-tuple-element.302), channel_id=1, source_target_pairs={{0,1},{1,0},{2,3},{3,2},{4,5},{5,4},{6,7},{7,6},{8,9},{9,8},{10,11... | collective-permute-start | bytes 1179656 | tf_op jit(solution)/shard_map/ppermute | solution.py:48
  351.0 13.5 %collective-permute-start.30 = (bf16[128,1536]{1,0:T(8,128)(2,1)S(1)}, bf16[128,1536]{1,0:T(8,128)(2,1)S(1)}, u32[]{:S(2)}, u32[]{:S(2)}) collective-permute-start(bf16[128,1536]{1,0:T(8,128)(2,1)S(1)} %get-tuple-element.303), channel_id=1, source_target_pairs={{0,16},{8,24},{16,0},{24,8},{1,17},{9,25},{17,1},{25,9},{2,18},{10... | collective-permute-start | bytes 1179656 | tf_op jit(solution)/shard_map/ppermute | solution.py:44
  367.6 24.7 %collective-permute-start.32 = (bf16[256,1536]{1,0:T(8,128)(2,1)S(1)}, bf16[256,1536]{1,0:T(8,128)(2,1)}, u32[]{:S(2)}, u32[]{:S(2)}) collective-permute-start(bf16[256,1536]{1,0:T(8,128)(2,1)S(1)} %pad_maximum_fusion.5), channel_id=1, source_target_pairs={{0,16},{8,24},{16,0},{24,8},{1,17},{9,25},{17,1},{25,9},{2,18},{10... | collective-permute-start | bytes 2359304 | tf_op jit(solution)/shard_map/ppermute | solution.py:44
  370.3 22.0 %collective-permute-start.33 = (bf16[256,1536]{1,0:T(8,128)(2,1)}, bf16[256,1536]{1,0:T(8,128)(2,1)}, u32[]{:S(2)}, u32[]{:S(2)}) collective-permute-start(bf16[256,1536]{1,0:T(8,128)(2,1)} %pad_maximum_fusion.6), channel_id=1, source_target_pairs={{0,1},{1,0},{2,3},{3,2},{4,5},{5,4},{6,7},{7,6},{8,9},{9,8},{10,11... | collective-permute-start | bytes 2359304 | tf_op jit(solution)/shard_map/ppermute | solution.py:48
  398.6 20.3 %collective-permute-start.35 = (bf16[1024,1536]{1,0:T(8,128)(2,1)}, bf16[1024,1536]{1,0:T(8,128)(2,1)}, u32[]{:S(2)}, u32[]{:S(2)}) collective-permute-start(bf16[1024,1536]{1,0:T(8,128)(2,1)} %get-tuple-element.216), channel_id=1, source_target_pairs={{0,8},{8,0},{16,24},{24,16},{1,9},{9,1},{17,25},{25,17},{2,10},{10... | collective-permute-start | bytes 9437192 | tf_op jit(solution)/shard_map/ppermute | solution.py:44
  398.7 246.7 %reduce-scatter.6.cloned.1.call-start = ((), (), s32[]{:S(2)}) async-start(), calls=%async_computation.6 | async-start | bytes 5898240 | tf_op jit(solution)/shard_map/reduce_scatter | solution.py:796
  398.8 20.1 %collective-permute-start.34 = (bf16[256,1536]{1,0:T(8,128)(2,1)S(1)}, bf16[256,1536]{1,0:T(8,128)(2,1)}, u32[]{:S(2)}, u32[]{:S(2)}) collective-permute-start(bf16[256,1536]{1,0:T(8,128)(2,1)S(1)} %fusion.110), channel_id=1, source_target_pairs={{0,1},{1,0},{2,3},{3,2},{4,5},{5,4},{6,7},{7,6},{8,9},{9,8},{10,11... | collective-permute-start | bytes 2359304 | tf_op jit(solution)/shard_map/ppermute | solution.py:48
  431.9 47.9 %collective-permute-start.41 = (bf16[4,192,768]{2,1,0:T(8,128)(2,1)}, bf16[4,192,768]{2,1,0:T(8,128)(2,1)}, u32[]{:S(2)}, u32[]{:S(2)}) collective-permute-start(bf16[4,192,768]{2,1,0:T(8,128)(2,1)} %dynamic-slice_bitcast_fusion.1), channel_id=1, source_target_pairs={{0,8},{8,0},{16,24},{24,16},{1,9},{9,1},{17,25},{25,17},{2,10},{10... | collective-permute-start | bytes 3538952 | tf_op jit(solution)/shard_map/ppermute | solution.py:44
  436.9 42.9 %collective-permute-start.38 = (bf16[256,1536]{1,0:T(8,128)(2,1)}, bf16[256,1536]{1,0:T(8,128)(2,1)}, u32[]{:S(2)}, u32[]{:S(2)}) collective-permute-start(bf16[256,1536]{1,0:T(8,128)(2,1)} %pad_maximum_fusion.7), channel_id=1, source_target_pairs={{0,16},{8,24},{16,0},{24,8},{1,17},{9,25},{17,1},{25,9},{2,18},{10... | collective-permute-start | bytes 2359304 | tf_op jit(solution)/shard_map/ppermute | solution.py:44
  438.6 41.2 %collective-permute-start.39 = (bf16[256,1536]{1,0:T(8,128)(2,1)}, bf16[256,1536]{1,0:T(8,128)(2,1)}, u32[]{:S(2)}, u32[]{:S(2)}) collective-permute-start(bf16[256,1536]{1,0:T(8,128)(2,1)} %pad_maximum_fusion.8), channel_id=1, source_target_pairs={{0,1},{1,0},{2,3},{3,2},{4,5},{5,4},{6,7},{7,6},{8,9},{9,8},{10,11... | collective-permute-start | bytes 2359304 | tf_op jit(solution)/shard_map/ppermute | solution.py:48
  483.8 63.7 %collective-permute-start.46 = (bf16[4,192,768]{2,1,0:T(8,128)(2,1)}, bf16[4,192,768]{2,1,0:T(8,128)(2,1)}, u32[]{:S(2)}, u32[]{:S(2)}) collective-permute-start(bf16[4,192,768]{2,1,0:T(8,128)(2,1)} %dynamic-slice_bitcast_fusion), channel_id=1, source_target_pairs={{0,8},{8,0},{16,24},{24,16},{1,9},{9,1},{17,25},{25,17},{2,10},{10... | collective-permute-start | bytes 3538952 | tf_op jit(solution)/shard_map/ppermute | solution.py:44
  489.4 22.7 %collective-permute-start.40 = (bf16[256,1536]{1,0:T(8,128)(2,1)}, bf16[256,1536]{1,0:T(8,128)(2,1)}, u32[]{:S(2)}, u32[]{:S(2)}) collective-permute-start(bf16[256,1536]{1,0:T(8,128)(2,1)} %fusion.17), channel_id=1, source_target_pairs={{0,1},{1,0},{2,3},{3,2},{4,5},{5,4},{6,7},{7,6},{8,9},{9,8},{10,11... | collective-permute-start | bytes 2359304 | tf_op jit(solution)/shard_map/ppermute | solution.py:48
  493.9 53.6 %collective-permute-start.45 = (bf16[4,96,768]{2,1,0:T(8,128)(2,1)}, bf16[4,96,768]{2,1,0:T(8,128)(2,1)}, u32[]{:S(2)}, u32[]{:S(2)}) collective-permute-start(bf16[4,96,768]{2,1,0:T(8,128)(2,1)} %fusion.51), channel_id=1, source_target_pairs={{0,16},{8,24},{16,0},{24,8},{1,17},{9,25},{17,1},{25,9},{2,18},{10... | collective-permute-start | bytes 1769480 | tf_op jit(solution)/shard_map/ppermute | solution.py:44
  495.9 26.7 %collective-permute-start.44 = (bf16[512,256]{1,0:T(8,128)(2,1)S(1)}, bf16[512,256]{1,0:T(8,128)(2,1)S(1)}, u32[]{:S(2)}, u32[]{:S(2)}) collective-permute-start(bf16[512,256]{1,0:T(8,128)(2,1)S(1)} %get-tuple-element.291), channel_id=1, source_target_pairs={{0,2},{2,4},{4,6},{6,0},{1,3},{3,5},{5,7},{7,1},{8,10},{10,12},{12... | collective-permute-start | bytes 786440 | tf_op jit(solution)/shard_map/ppermute | solution.py:53
  510.2 26.8 %collective-permute-start.43 = (bf16[512,256]{1,0:T(8,128)(2,1)S(1)}, bf16[512,256]{1,0:T(8,128)(2,1)S(1)}, u32[]{:S(2)}, u32[]{:S(2)}) collective-permute-start(bf16[512,256]{1,0:T(8,128)(2,1)S(1)} %get-tuple-element.292), channel_id=1, source_target_pairs={{0,4},{2,6},{4,0},{6,2},{1,5},{3,7},{5,1},{7,3},{8,12},{10,14},{12... | collective-permute-start | bytes 786440 | tf_op jit(solution)/shard_map/ppermute | solution.py:53
  512.2 35.4 %collective-permute-start.42 = (bf16[512,256]{1,0:T(8,128)(2,1)S(1)}, bf16[512,256]{1,0:T(8,128)(2,1)S(1)}, u32[]{:S(2)}, u32[]{:S(2)}) collective-permute-start(bf16[512,256]{1,0:T(8,128)(2,1)S(1)} %get-tuple-element.293), channel_id=1, source_target_pairs={{0,6},{2,0},{4,2},{6,4},{1,7},{3,1},{5,3},{7,5},{8,14},{10,8},{12,... | collective-permute-start | bytes 786440 | tf_op jit(solution)/shard_map/ppermute | solution.py:53
  522.5 124.2 %collective-permute-start.65 = (bf16[96,1152]{1,0:T(8,128)(2,1)}, bf16[96,1152]{1,0:T(8,128)(2,1)S(1)}, u32[]{:S(2)}, u32[]{:S(2)}) collective-permute-start(bf16[96,1152]{1,0:T(8,128)(2,1)} %get-tuple-element.296), channel_id=1, source_target_pairs={{0,24},{8,16},{16,8},{24,0},{1,25},{9,17},{17,9},{25,1},{2,26},{10... | collective-permute-start | bytes 663560 | tf_op jit(solution)/shard_map/ppermute | solution.py:44
  537.0 109.8 %collective-permute-start.64 = (bf16[96,1152]{1,0:T(8,128)(2,1)}, bf16[96,1152]{1,0:T(8,128)(2,1)S(1)}, u32[]{:S(2)}, u32[]{:S(2)}) collective-permute-start(bf16[96,1152]{1,0:T(8,128)(2,1)} %get-tuple-element.297), channel_id=1, source_target_pairs={{0,16},{8,24},{16,0},{24,8},{1,17},{9,25},{17,1},{25,9},{2,18},{10... | collective-permute-start | bytes 663560 | tf_op jit(solution)/shard_map/ppermute | solution.py:44
  552.5 19.8 %collective-permute-start.49 = (bf16[256,1536]{1,0:T(8,128)(2,1)S(1)}, bf16[256,1536]{1,0:T(8,128)(2,1)S(1)}, u32[]{:S(2)}, u32[]{:S(2)}) collective-permute-start(bf16[256,1536]{1,0:T(8,128)(2,1)S(1)} %fusion.14), channel_id=1, source_target_pairs={{0,1},{1,0},{2,3},{3,2},{4,5},{5,4},{6,7},{7,6},{8,9},{9,8},{10,11... | collective-permute-start | bytes 2359304 | tf_op jit(solution)/shard_map/ppermute | solution.py:48
  556.6 15.8 %collective-permute-start.47 = (bf16[4,96,768]{2,1,0:T(8,128)(2,1)S(1)}, bf16[4,96,768]{2,1,0:T(8,128)(2,1)S(1)}, u32[]{:S(2)}, u32[]{:S(2)}) collective-permute-start(bf16[4,96,768]{2,1,0:T(8,128)(2,1)S(1)} %fusion.52), channel_id=1, source_target_pairs={{0,16},{8,24},{16,0},{24,8},{1,17},{9,25},{17,1},{25,9},{2,18},{10... | collective-permute-start | bytes 1769480 | tf_op jit(solution)/shard_map/ppermute | solution.py:44
  579.4 34.3 %collective-permute-start.52 = (bf16[256,1536]{1,0:T(8,128)(2,1)S(1)}, bf16[256,1536]{1,0:T(8,128)(2,1)S(1)}, u32[]{:S(2)}, u32[]{:S(2)}) collective-permute-start(bf16[256,1536]{1,0:T(8,128)(2,1)S(1)} %fusion.18), channel_id=1, source_target_pairs={{0,1},{1,0},{2,3},{3,2},{4,5},{5,4},{6,7},{7,6},{8,9},{9,8},{10,11... | collective-permute-start | bytes 2359304 | tf_op jit(solution)/shard_map/ppermute | solution.py:48
  581.3 17.5 %collective-permute-start.55 = (f32[4096]{0:T(1024)S(1)}, f32[4096]{0:T(1024)S(1)}, u32[]{:S(2)}, u32[]{:S(2)}) collective-permute-start(f32[4096]{0:T(1024)S(1)} %add.490), channel_id=1, source_target_pairs={{0,2},{2,0},{4,6},{6,4},{1,3},{3,1},{5,7},{7,5},{8,10},{10,8},{12,... | collective-permute-start | bytes 49160 | tf_op jit(solution)/shard_map/ppermute | solution.py:614
  613.7 36.7 %collective-permute-start.63 = (bf16[96,1152]{1,0:T(8,128)(2,1)}, bf16[96,1152]{1,0:T(8,128)(2,1)S(1)}, u32[]{:S(2)}, u32[]{:S(2)}) collective-permute-start(bf16[96,1152]{1,0:T(8,128)(2,1)} %get-tuple-element.298), channel_id=1, source_target_pairs={{0,8},{8,0},{16,24},{24,16},{1,9},{9,1},{17,25},{25,17},{2,10},{10... | collective-permute-start | bytes 663560 | tf_op jit(solution)/shard_map/ppermute | solution.py:44
  646.8 18.1 %collective-permute-start.68 = (bf16[96,1536]{1,0:T(8,128)(2,1)S(1)}, bf16[96,1536]{1,0:T(8,128)(2,1)S(1)}, u32[]{:S(2)}, u32[]{:S(2)}) collective-permute-start(bf16[96,1536]{1,0:T(8,128)(2,1)S(1)} %get-tuple-element.287), channel_id=1, source_target_pairs={{0,24},{8,16},{16,8},{24,0},{1,25},{9,17},{17,9},{25,1},{2,26},{10... | collective-permute-start | bytes 884744 | tf_op jit(solution)/shard_map/ppermute | solution.py:44
  646.8 18.0 %collective-permute-start.67 = (bf16[96,1536]{1,0:T(8,128)(2,1)S(1)}, bf16[96,1536]{1,0:T(8,128)(2,1)S(1)}, u32[]{:S(2)}, u32[]{:S(2)}) collective-permute-start(bf16[96,1536]{1,0:T(8,128)(2,1)S(1)} %get-tuple-element.288), channel_id=1, source_target_pairs={{0,16},{8,24},{16,0},{24,8},{1,17},{9,25},{17,1},{25,9},{2,18},{10... | collective-permute-start | bytes 884744 | tf_op jit(solution)/shard_map/ppermute | solution.py:44
  650.3 14.5 %collective-permute-start.66 = (bf16[96,1536]{1,0:T(8,128)(2,1)S(1)}, bf16[96,1536]{1,0:T(8,128)(2,1)S(1)}, u32[]{:S(2)}, u32[]{:S(2)}) collective-permute-start(bf16[96,1536]{1,0:T(8,128)(2,1)S(1)} %get-tuple-element.289), channel_id=1, source_target_pairs={{0,8},{8,0},{16,24},{24,16},{1,9},{9,1},{17,25},{25,17},{2,10},{10... | collective-permute-start | bytes 884744 | tf_op jit(solution)/shard_map/ppermute | solution.py:44
  650.4 14.5 %collective-permute-start.70 = (bf16[96,768]{1,0:T(8,128)(2,1)S(1)}, bf16[96,768]{1,0:T(8,128)(2,1)S(1)}, u32[]{:S(2)}, u32[]{:S(2)}) collective-permute-start(bf16[96,768]{1,0:T(8,128)(2,1)S(1)} %copy-done.62), channel_id=1, source_target_pairs={{0,16},{8,24},{16,0},{24,8},{1,17},{9,25},{17,1},{25,9},{2,18},{10... | collective-permute-start | bytes 442376 | tf_op jit(solution)/shard_map/ppermute | solution.py:44
  (117 other events, 1248.5 us)
Sparse Core Ops, SparseCore 0:
  41.9 71.5 all-gather.4
  115.1 139.8 all-gather.2
  323.9 77.1 reduce-scatter.3
  403.2 54.4 reduce-scatter.7
  459.9 101.6 reduce-scatter.5

commit v2 on v1

--- a/solution.py
+++ b/solution.py
@@ -167,7 +167,7 @@
 
 def attend_back_kernel(
     rows, factor, scale, repeat, flag_ref, q_ref, k_ref, v_ref, do_ref, lse_ref, cos_ref, sin_ref,
-    sq_ref, pq_ref, sk_ref, pk_ref, dq_ref, dk_ref, dv_ref, dk_acc, dv_acc, dq_acc,
+    sq_ref, pq_ref, sk_ref, pk_ref, dq_ref, dkv_ref, dk_acc, dv_acc, dq_acc,
     p_keep, dp_keep, delta_ref,
 ):
     head = pl.program_id(0)
@@ -228,8 +228,8 @@
 
     @pl.when(lax.rem(head, repeat) == repeat - 1)
     def _():
-        dk_ref[...] = (dk_acc[...] * scale).astype(dk_ref.dtype)
-        dv_ref[...] = dv_acc[...].astype(dv_ref.dtype)
+        dkv_ref[:, :HEAD_DIM] = (dk_acc[...] * scale).astype(dkv_ref.dtype)
+        dkv_ref[:, HEAD_DIM:] = dv_acc[...].astype(dkv_ref.dtype)
 
 
 def attend_back(q, keys, values, d_o, lse, cosine, sine, seg_q, pos_q, seg_k, pos_k, flags):
@@ -241,7 +241,6 @@
     blocks = length // rows
     whole = lambda *shape: pl.BlockSpec(shape, lambda h: (0,) * len(shape))
     per_head = pl.BlockSpec((rows, HEAD_DIM), lambda h: (0, h))
-    per_pair = pl.BlockSpec((length, HEAD_DIM), lambda h: (0, h // repeat))
     held = pl.BlockSpec(
         (length, HEAD_DIM), lambda h: (0, h // repeat), pipeline_mode=pl.Buffered(1)
     )
@@ -264,11 +263,10 @@
             whole(blocks, 1, rows),
             whole(blocks, 1, rows),
         ],
-        out_specs=[per_head, per_pair, per_pair],
+        out_specs=[per_head, pl.BlockSpec((length, 2 * HEAD_DIM), lambda h: (0, h // repeat))],
         out_shape=[
             jax.ShapeDtypeStruct((rows, width), BF16),
-            jax.ShapeDtypeStruct(keys.shape, BF16),
-            jax.ShapeDtypeStruct(values.shape, BF16),
+            jax.ShapeDtypeStruct((length, 2 * keys.shape[1]), BF16),
         ],
         scratch_shapes=[
             pltpu.VMEM((length, HEAD_DIM), F32),
@@ -434,27 +432,19 @@
 
 def lay_kernel(cut, place_ref, *refs):
     n_dp = cut.n_dp
-    firsts, pairs, downs = (refs[i * n_dp : (i + 1) * n_dp] for i in range(3))
-    outs = refs[3 * n_dp :]
+    firsts, *seconds = (refs[i * n_dp : (i + 1) * n_dp] for i in range(4))
+    outs = refs[4 * n_dp :]
     for i, out in enumerate(outs):
         for part in range(2):
             main, width = cut.main[part], cut.width[part]
             for k in range(n_dp):
-                if part == 0:
-                    piece = firsts[k].at[:, i * width : (i + 1) * width]
-                elif i < 2:
-                    piece = pairs[k].at[:, i * width : (i + 1) * width]
-                else:
-                    piece = downs[k]
+                piece = seconds[i][k] if part else firsts[k].at[:, i * width : (i + 1) * width]
                 owner = place_ref[k]
                 low = pl.multiple_of(cut.start[part] + owner * main, 128)
                 out[:, pl.ds(low, main)] = piece[:, :main].astype(F32)
         if cut.rest:
-            main, width = cut.main[1], cut.width[1]
-            tails = []
-            for k in range(n_dp):
-                piece = pairs[k].at[:, i * width : (i + 1) * width] if i < 2 else downs[k]
-                tails.append(piece[:, main:].astype(F32)[:, : cut.rest])
+            main = cut.main[1]
+            tails = [piece[:, main:].astype(F32)[:, : cut.rest] for piece in seconds[i]]
             laid = []
             for b in range(n_dp):
                 laid.append(
@@ -500,13 +490,13 @@
     back = right_product(gate_back, gate_weight[...]) + right_product(upper_back, up_weight[...])
     out = right_product(activated, down_weight[...])
     if sums:
-        back = back + refs[3][...]
-        out = out + refs[4][...]
+        back = back + refs[3][...].astype(F32)
+        out = out + refs[4][...].astype(F32)
     back_ref[...] = back.astype(back_ref.dtype)
     out_ref[...] = out.astype(out_ref.dtype)
 
 
-def feed(tokens, cots, weights, side, kept, earlier, dtype):
+def feed(tokens, cots, weights, side, kept, earlier):
     rows, width = tokens.shape
     columns = weights.shape[1]
     span = rows // 2
@@ -535,8 +525,8 @@
         out_specs=[block(columns), near, near],
         out_shape=[
             jax.ShapeDtypeStruct((rows, columns), BF16),
-            jax.ShapeDtypeStruct((span, width), dtype),
-            jax.ShapeDtypeStruct((span, width), dtype),
+            jax.ShapeDtypeStruct((span, width), BF16),
+            jax.ShapeDtypeStruct((span, width), BF16),
         ],
         input_output_aliases=aliases,
         compiler_params=pltpu.CompilerParams(vmem_limit_bytes=56 * MIB),
@@ -575,6 +565,61 @@
     )(tokens, cots, kept)
 
 
+def d_o_kernel(own_ref, other_ref, w_ref, d_o_ref, rows_ref):
+    half = own_ref.shape[0]
+    weights = w_ref[...]
+    d_o_ref[:half] = product(own_ref[...], weights).astype(BF16)
+    d_o_ref[half:] = product(other_ref[...], weights).astype(BF16)
+    rows_ref[:half] = own_ref[...]
+    rows_ref[half:] = other_ref[...]
+
+
+def d_o_of(own, other, weights, first, count):
+    half, width = own.shape
+    wide = math.gcd(first, count)
+    whole = lambda *shape: pl.BlockSpec(shape, lambda i: (0, 0))
+    return pl.pallas_call(
+        d_o_kernel,
+        grid=(count // wide,),
+        in_specs=[
+            whole(half, width),
+            whole(half, width),
+            pl.BlockSpec((width, wide), lambda i: (0, first // wide + i)),
+        ],
+        out_specs=[pl.BlockSpec((2 * half, wide), lambda i: (0, i)), whole(2 * half, width)],
+        out_shape=[
+            jax.ShapeDtypeStruct((2 * half, count), BF16),
+            jax.ShapeDtypeStruct((2 * half, width), BF16),
+        ],
+        compiler_params=pltpu.CompilerParams(vmem_limit_bytes=32 * MIB),
+        cost_estimate=FREE,
+    )(own, other, weights)
+
+
+def halves_kernel(n_seq, share, core_ref, left_ref, right_ref, own_ref, sent_ref, keep_ref):
+    keep_ref[...] = left_product(left_ref[...], right_ref[...]).astype(BF16)
+    tall = own_ref.shape[1]
+    for z in range(n_seq):
+        for out, core in ((own_ref, core_ref[0]), (sent_ref, 1 - core_ref[0])):
+            at = pl.multiple_of((z * 2 + core) * tall, share)
+            out[z] = keep_ref[pl.ds(at, tall), :]
+
+
+def gradient_halves(left, right, core, n_seq, share):
+    width, columns = left.shape[1], right.shape[1]
+    vmem = pl.BlockSpec(memory_space=pltpu.VMEM)
+    half = jax.ShapeDtypeStruct((n_seq, width // (2 * n_seq), columns), BF16)
+    return pl.pallas_call(
+        functools.partial(halves_kernel, n_seq, share),
+        out_shape=[half, half],
+        in_specs=[pl.BlockSpec(memory_space=pltpu.SMEM), vmem, vmem],
+        out_specs=[vmem, vmem],
+        scratch_shapes=[pltpu.VMEM((width, columns), BF16)],
+        compiler_params=pltpu.CompilerParams(vmem_limit_bytes=32 * MIB),
+        cost_estimate=FREE,
+    )(core, left, right)
+
+
 def plane_gather(own, *others):
     cut = own.shape[0] // 2
     over_x, over_y, *others = together(dp_swap(own, 2), y_swap(own), *others)
@@ -587,33 +632,30 @@
     return near + [far] + across + [dp_swap(far, 1)], others
 
 
-def plane_scatter(near, over_core, beside):
-    t = near.shape[0] // 4
-    cut = t // 2
-
-    def summed(low, high):
-        return near[low:high] + over_core[low:high].astype(F32)
-
-    corner = summed(3 * t, 4 * t).astype(BF16)
-    corner_x, corner_y = beside[0](corner, dp_swap(corner[:cut], 2), y_swap(corner[cut:]))
-    to_y = jnp.concatenate(
-        [summed(t, t + cut) + corner_x.astype(F32), summed(t + cut, 2 * t)], axis=0
-    ).astype(BF16)
-    to_x = jnp.concatenate(
-        [summed(2 * t, 2 * t + cut), summed(2 * t + cut, 3 * t) + corner_y.astype(F32)], axis=0
-    ).astype(BF16)
-    over_x, over_y = beside[1](to_x, dp_swap(to_x, 2), y_swap(to_y))
-    return summed(0, t) + over_x.astype(F32) + over_y.astype(F32)
-
-
-def sum_over(values, axes):
-    for axis in axes:
-        size = lax.axis_size(axis)
-        flip = 1
-        while flip < size:
-            values = values + lax.ppermute(values, axis, [(i, i ^ flip) for i in range(size)])
-            flip *= 2
-    return values
+class PlaneScatter:
+    def __init__(self, near, over_core):
+        self.near, self.over_core = near, over_core
+        self.t = near.shape[0] // 4
+        self.cut = self.t // 2
+
+    def summed(self, low, high):
+        return self.near[low:high].astype(F32) + self.over_core[low:high].astype(F32)
+
+    def corner(self):
+        corner = self.summed(3 * self.t, 4 * self.t).astype(BF16)
+        return corner[: self.cut], corner[self.cut :]
+
+    def sides(self, corner_x, corner_y):
+        t, cut = self.t, self.cut
+        to_y = [self.summed(t, t + cut) + corner_x.astype(F32), self.summed(t + cut, 2 * t)]
+        to_x = [
+            self.summed(2 * t, 2 * t + cut),
+            self.summed(2 * t + cut, 3 * t) + corner_y.astype(F32),
+        ]
+        return tuple(jnp.concatenate(part, axis=0).astype(BF16) for part in (to_x, to_y))
+
+    def home(self, over_x, over_y):
+        return self.summed(0, self.t) + over_x.astype(F32) + over_y.astype(F32)
 
 
 def on_device(
@@ -702,9 +744,7 @@
             moved, over_x[s] = together(moved, over_x[s])
         line.append(moved)
     mine = assemble(line + over_x, jnp.arange(2 * n_seq, dtype=jnp.int32))
-    mine, *second_parts = together(mine, *second_parts)
     theirs = dp_swap(mine, 1)
-    second_parts = spread(second_parts)
     all_places = slots_of((0, 2, 1, 3))
 
     own_place = relative(lax.dynamic_slice_in_dim(positions, seq * rows, rows))
@@ -719,12 +759,12 @@
     qkv_end = q_width + 2 * kv_width
     attention_weights = attention_weights.reshape(width, qkv_end + q_width)
     qkv_full, out_full = attention_weights[:, :qkv_end], attention_weights[:, qkv_end:]
-    own_kv, cot_own = together(own_kv, cot_own)
-    cot_x = dp_swap(cot_own, 2)
     group_kv = [own_kv] + [z_shift(own_kv, s) for s in range(1, n_seq)]
+    second_parts = spread([after(part, own_kv) for part in second_parts])
+    *group_kv, cot_own, second_parts = together(*group_kv, cot_own, second_parts)
     second_stacked = stack_units(second_parts)
     second_units = lax.all_gather(second_stacked, "seq", axis=0, tiled=True)
-    *group_kv, second_stacked = together(*group_kv, second_stacked)
+    cot_x = dp_swap(cot_own, 2)
     group_kv = jnp.concatenate(group_kv, axis=0)
     keys, values = group_kv[:, :kv_width], group_kv[:, kv_width:]
 
@@ -743,16 +783,14 @@
         own_segment[:, None], own_place[:, None], seg_k[:, None, :], pos_k[:, None, :], flags,
     )
     attended, lse = attend(queries, keys, values, *pairs)
-    attended, cot_x = together(attended, cot_x)
-    cot_pieces = [cot_own, cot_x, dp_swap(cot_own, 1), dp_swap(cot_x, 1)]
-
     def reduce_halves(part):
         return part[:half] + y_swap(part[half:].astype(BF16)).astype(F32)
 
     inputs_half = inputs[:half].astype(F32)
     out_theirs = y_swap(right_product(attended[half:], out_full).astype(BF16))
     out_mine = right_product(attended[:half], out_full)
-    out_theirs, out_mine, *cot_pieces = together(out_theirs, out_mine, *cot_pieces)
+    out_theirs, out_mine, cot_x = together(out_theirs, out_mine, cot_x)
+    cot_pieces = [cot_own, cot_x, dp_swap(cot_own, 1), dp_swap(cot_x, 1)]
     cots = assemble(cot_pieces, jnp.arange(4, dtype=jnp.int32)).reshape(-1, width)
     residual = inputs_half + out_mine + out_theirs.astype(F32)
     second_inverse = inverse_rms(residual)
@@ -762,100 +800,99 @@
     gathered, (cots,) = plane_gather(second_rounded, cots)
     tokens = assemble(gathered, jnp.arange(len(gathered), dtype=jnp.int32)).reshape(-1, width)
 
-    kept, *far = feed(tokens, cots, first_units, 1, None, None, F32)
-    kept, *near = feed(tokens, cots, first_units, 0, kept, None, F32)
+    kept, *far = feed(tokens, cots, first_units, 1, None, None)
+    kept, *near = feed(tokens, cots, first_units, 0, kept, None)
     first_gradient = unit_gradients(tokens, cots, kept)
     second_weights = after(second_units, first_gradient)
-    second_kept, back_far, out_far = feed(tokens, cots, second_weights, 1, None, far, BF16)
+    second_kept, back_far, out_far = feed(tokens, cots, second_weights, 1, None, far)
     second_kept, back_near, out_near = feed(
-        tokens, cots, second_weights, 0, second_kept, near, F32
-    )
-    second_gradients = []
-
-    def cost_of(count):
-        flops = 2 * count * tokens.size * cut.width[1]
-        return pl.CostEstimate(flops=flops, bytes_accessed=0, transcendentals=0)
-
-    def gradients_beside(which):
-        def run(operand, *moved):
-            gradient = unit_gradients(
-                tokens, cots, after(second_kept, operand), which, cost_of(len(which))
-            )
-            *moved, gradient = together(*moved, gradient)
-            second_gradients.append(gradient)
-            return moved
-
-        return run
-
-    back_core, back_near = together(dp_swap(back_far, 1), back_near)
-    second_back = plane_scatter(
-        back_near, back_core, (gradients_beside((2,)), gradients_beside((0, 1)))
-    )
-
-    def scatter_units(gradient):
+        tokens, cots, second_weights, 0, second_kept, near
+    )
+    first_share = lax.psum_scatter(first_gradient, "seq", scatter_dimension=0, tiled=True)
+    flops = 2 * tokens.size * cut.width[1]
+    cost = pl.CostEstimate(flops=flops, bytes_accessed=0, transcendentals=0)
+
+    def second_gradient(which, operand):
+        return unit_gradients(tokens, cots, after(second_kept, operand), (which,), cost)
+
+    def sum_along_seq(gradient):
         return lax.psum_scatter(gradient, "seq", scatter_dimension=0, tiled=True)
+
+    back = PlaneScatter(*reversed(together(dp_swap(back_far, 1), back_near)))
+    corner = back.corner()
+    *corners, down_gradient = together(
+        dp_swap(corner[0], 2), y_swap(corner[1]), second_gradient(2, corner[0])
+    )
+    down_share = sum_along_seq(down_gradient)
+    sides = back.sides(*corners)
+    *over, gate_gradient, first_share = together(
+        dp_swap(sides[0], 2), y_swap(sides[1]), second_gradient(0, sides[0]), first_share
+    )
+    gate_share = sum_along_seq(gate_gradient)
+    second_back = back.home(*over)
+
+    residual_inner, second_gain_term = norm_backward(
+        second_back, second_normed, second_inverse, gain_second
+    )
+    residual_back = cot_own[:half].astype(F32) + residual_inner
+    back_half = residual_back.astype(BF16)
+    back_other, out_core, up_gradient, down_share = together(
+        y_swap(back_half), dp_swap(after(out_far, back_half), 1), second_gradient(1, back_half),
+        down_share,
+    )
+    down = PlaneScatter(out_near, out_core)
+    attended_back, attention_back = d_o_of(
+        back_half, back_other, attention_weights, qkv_end, q_width
+    )
+
+    take = lax.dynamic_index_in_dim
+    core, x = dp % 2, dp // 2
+
+    def halves_of(left, right):
+        return gradient_halves(left, right, core.astype(jnp.int32)[None], n_seq, share)
+
+    def x_halves(own, over_core):
+        parts = own.astype(F32) + over_core.astype(F32)
+        parts = parts.reshape(n_seq, n_dp // 2, share, own.shape[2])
+        return take(parts, x, 1, keepdims=False), take(parts, 1 - x, 1, keepdims=False).astype(BF16)
+
+    def place_of(parts, s):
+        return take(parts, seq_places[s % n_seq], 0, keepdims=False)
 
     def exchange_units(mine):
         mine = mine.reshape(n_dp, share, mine.shape[1])
         pieces = []
         for k in range(n_dp):
-            piece = lax.dynamic_index_in_dim(mine, dp_slots[k], 0, keepdims=False)
+            piece = take(mine, dp_slots[k], 0, keepdims=False)
             pieces.append(dp_swap(piece, k) if k else piece)
         return pieces
 
-    first_share = scatter_units(first_gradient)
-    second_shares = [scatter_units(g) for g in second_gradients]
-
-    residual_inner, second_gain_term = norm_backward(
-        second_back, second_normed, second_inverse, gain_second
-    )
-    residual_back = cot_own[:half].astype(F32) + residual_inner
-    back_half = residual_back.astype(BF16)
-    back_other, out_core = together(y_swap(back_half), dp_swap(after(out_far, back_half), 1))
-    attention_back = jnp.concatenate([back_half, back_other], axis=0)
-
-    take = lax.dynamic_index_in_dim
-    core, x = dp % 2, dp // 2
-
-    def core_halves(gradient):
-        parts = gradient.reshape(n_seq, 2, (n_dp // 2) * share, gradient.shape[1])
-        return take(parts, core, 1, keepdims=False), take(parts, 1 - core, 1, keepdims=False)
-
-    def x_halves(own, over_core):
-        parts = own.astype(F32) + over_core.astype(F32)
-        parts = parts.reshape(n_seq, n_dp // 2, share, own.shape[2])
-        return take(parts, x, 1, keepdims=False), take(parts, 1 - x, 1, keepdims=False).astype(BF16)
-
-    def place_of(parts, s):
-        return take(parts, seq_places[s % n_seq], 0, keepdims=False)
-
-    attended_back = product(attention_back, out_full).astype(BF16)
-    out_own, out_sent = core_halves(
-        left_product(attention_back, attended).astype(BF16)
-    )
-    attended_back, first_share, out_sent = together(attended_back, first_share, out_sent)
-
-    over_core = dp_swap(out_sent, 1)
-    query_linear_back, key_parts, value_parts = attend_back(
+    first_pieces = exchange_units(after(first_share, back_other))
+    out_own, sent = halves_of(attention_back, attended)
+    out_over_core = dp_swap(sent, 1)
+    query_linear_back, kv_parts = attend_back(
         queries, keys, values, attended_back, lse, cosine, sine, *pairs
     )
-
-    def plain(operand, *moved):
-        *moved, operand = together(*moved, operand)
-        return moved
-
-    kv_parts = jnp.concatenate([key_parts, value_parts], axis=1)
-    kv_parts, over_core, query_linear_back = together(kv_parts, over_core, query_linear_back)
+    corner = down.corner()
+    query_linear_back, kv_parts, out_over_core, gate_share, *arrived = together(
+        query_linear_back, kv_parts, out_over_core, gate_share,
+        dp_swap(corner[0], 2), y_swap(corner[1]), *first_pieces,
+    )
+    corners, first_pieces = arrived[:2], arrived[2:]
 
     kv_moved = [z_shift(kv_parts[s * rows : (s + 1) * rows], -s) for s in range(1, n_seq)]
-    out_parts, out_sent = x_halves(out_own, over_core)
-    out_over_x = dp_swap(out_sent, 2)
-    query_own, query_sent = core_halves(
-        left_product(first_rounded, query_linear_back).astype(BF16)
-    )
-    over_core = dp_swap(query_sent, 1)
-    *kv_moved, out_over_x, over_core = together(*kv_moved, out_over_x, over_core)
-    out_parts = out_parts + out_over_x.astype(F32)
+    out_own, sent = x_halves(out_own, out_over_core)
+    out_over_x = dp_swap(sent, 2)
+    query_own, query_sent = halves_of(first_rounded, query_linear_back)
+    sides = down.sides(*corners)
+    out_over_x, query_own, query_sent, up_gradient, *arrived = together(
+        out_over_x, query_own, query_sent, up_gradient,
+        dp_swap(sides[0], 2), y_swap(sides[1]), *kv_moved,
+    )
+    over, kv_moved = arrived[:2], arrived[2:]
+    out_half = from_inner((residual + down.home(*over)).astype(BF16))
+    out_rows = out_own + out_over_x.astype(F32)
+    up_share = sum_along_seq(up_gradient)
     kv_back = kv_parts[:rows].astype(F32)
     for moved in kv_moved:
         kv_back = kv_back + moved.astype(F32)
@@ -865,55 +902,77 @@
     kv_linear_back = jnp.concatenate([key_linear_back, kv_back[:, kv_width:]], axis=1).astype(BF16)
     linear_back = jnp.concatenate([query_linear_back, kv_linear_back], axis=1)
 
-    query_parts, query_sent = x_halves(query_own, over_core)
-    query_over_x = dp_swap(query_sent, 2)
-    kv_own, kv_sent = core_halves(left_product(first_rounded, kv_linear_back).astype(BF16))
-    over_core = dp_swap(kv_sent, 1)
+    query_over_core = dp_swap(query_sent, 1)
+    kv_own, sent = halves_of(first_rounded, kv_linear_back)
+    kv_over_core = dp_swap(sent, 1)
     first_theirs = y_swap(right_product(linear_back[half:], qkv_full).astype(BF16))
     first_mine = right_product(linear_back[:half], qkv_full)
-    query_over_x, over_core, first_theirs, first_mine = together(
-        query_over_x, over_core, first_theirs, first_mine
-    )
+    bias_terms = jnp.sum(linear_back.astype(F32), axis=0)
+    query_over_core, kv_over_core, out_half = together(query_over_core, kv_over_core, out_half)
+
+    query_own, query_sent = x_halves(query_own, query_over_core)
+    query_over_x = dp_swap(query_sent, 2)
+    kv_own, sent = x_halves(kv_own, kv_over_core)
+    kv_over_x = dp_swap(sent, 2)
+    out_other = y_swap(out_half)
+    query_over_x, kv_over_x, first_theirs, first_mine, bias_terms = together(
+        query_over_x, kv_over_x, first_theirs, first_mine, bias_terms
+    )
+    large = jnp.concatenate([query_own + query_over_x.astype(F32), out_rows], axis=2)
+    kv_rows = kv_own + kv_over_x.astype(F32)
+
+    total = z_shift(place_of(large, 1).astype(BF16), 1)
+    kv_total = z_shift(place_of(kv_rows, 1).astype(BF16), 1)
     first_back = first_mine + first_theirs.astype(F32)
-    query_parts = query_parts + query_over_x.astype(F32)
-    large = jnp.concatenate([query_parts, out_parts], axis=2)
-
-    kv_own, kv_sent = x_halves(kv_own, over_core)
-    kv_over_x = dp_swap(kv_sent, 2)
-    total = z_shift(place_of(large, 1).astype(BF16), 1)
     first_inverse = inverse_rms(inputs_half)
     input_inner, first_gain_term = norm_backward(
         first_back, inputs_half * first_inverse, first_inverse, gain_first
     )
     input_half = from_inner((residual_back + input_inner).astype(BF16))
+    sums = jnp.concatenate([first_gain_term, second_gain_term, bias_terms])
+    total, kv_total, sums, input_half, out_other = together(
+        total, kv_total, sums, input_half, out_other
+    )
+    total = place_of(large, 2) + total.astype(F32)
+    kv_total = place_of(kv_rows, 2) + kv_total.astype(F32)
+
+    def shift_add(values, axis):
+        size = lax.axis_size(axis)
+        moved = [
+            lax.ppermute(values, axis, [(i, (i + s) % size) for i in range(size)])
+            for s in range(1, size)
+        ]
+        return functools.reduce(jnp.add, moved, values)
+
     input_other = y_swap(input_half)
-    total, kv_over_x, input_other = together(total, kv_over_x, input_other)
+    pieces = [exchange_units(share_of) for share_of in (down_share, gate_share)]
+    for s in range(2, n_seq):
+        total = z_shift(total.astype(BF16), 1)
+        kv_total = z_shift(kv_total.astype(BF16), 1)
+        if s == 2:
+            sums = shift_add(sums, "dp")
+            total, kv_total, sums, up_share, pieces[0] = together(
+                total, kv_total, sums, up_share, pieces[0]
+            )
+        elif s == 3:
+            sums = shift_add(sums, "seq")
+            total, kv_total, sums, input_other, pieces[1] = together(
+                total, kv_total, sums, input_other, pieces[1]
+            )
+        total = place_of(large, s + 1) + total.astype(F32)
+        kv_total = place_of(kv_rows, s + 1) + kv_total.astype(F32)
+    down_pieces, gate_pieces = pieces
+    up_pieces = exchange_units(up_share)
+    gain_terms = shift_add(sums[: 2 * width], "tensor")
+    bias_terms = sums[2 * width :]
     input_gradient = relative(jnp.concatenate([input_half, input_other], axis=0))
-    kv_rows = kv_own + kv_over_x.astype(F32)
-    kv_total = place_of(kv_rows, 1).astype(BF16)
-    first_received = exchange_units(first_share)
-    for s in range(1, n_seq):
-        total = place_of(large, s + 1) + total.astype(F32)
-        kv_total = place_of(kv_rows, s + 1) + z_shift(kv_total, 1).astype(F32)
-        if s + 1 < n_seq:
-            total, kv_total = together(z_shift(total.astype(BF16), 1), kv_total.astype(BF16))
+    output = relative(jnp.concatenate([out_half, out_other], axis=0))
     large_share, kv_share = total, kv_total
     out_gradient = large_share[:, q_width:].T
-    down_out = plane_scatter(out_near, out_core, (plain, plain))
-    out_half = from_inner((residual + down_out).astype(BF16))
-    output = relative(jnp.concatenate([out_half, y_swap(out_half)], axis=0))
-    second_pieces = [exchange_units(share_of) for share_of in second_shares]
     gate_gradient, up_gradient, down_gradient = lay_units(
-        cut, first_received + second_pieces[1] + second_pieces[0], dp_owners
+        cut, first_pieces + gate_pieces + up_pieces + down_pieces, dp_owners
     )
     down_gradient = down_gradient.T
-
-    bias_terms = jnp.sum(linear_back.astype(F32), axis=0)
-    sums = sum_over(
-        jnp.concatenate([first_gain_term, second_gain_term, bias_terms]), ("dp", "seq")
-    )
-    gain_terms = sum_over(sums[: 2 * width], ("tensor",))
-    bias_terms = sums[2 * width :]
     return (
         output,
         input_gradient,

time: 682 us -> 600 us (0.88)
  waiting for transfers between devices: 228 us -> 181 us
  Pallas kernels: 209 us -> 190 us
  matrix products: 39.8 us -> 28.9 us
    ppermute x15, waiting for transfers between devices: 92 us -> 65.3 us  [z_shift(): lax.ppermute(value, 'seq', [(i, (i + step) % size) for i in range(size)])]
    ppermute x41 -> x44, starting transfers between devices: 20.6 us -> 43.7 us  [dp_swap(): return lax.ppermute(value, 'dp', [(i, i ^ flip) for i in range(size)])]
    ppermute x11, waiting for transfers between devices: 57.9 us -> 36.9 us  [y_swap(): return lax.ppermute(value, 'tensor', [(0, 1), (1, 0)])]
    reduce_scatter x3 -> x4, waiting for transfers between devices: 0.01 us -> 16.8 us  [the longest x3 16.8 us: sum_along_seq(): return lax.psum_scatter(gradient, 'seq', scatter_dimension=0, tiled=True)]
    ppermute x5 -> x7, starting transfers between devices: 21.9 us -> 5.76 us  [shift_add(): lax.ppermute(values, axis, [(i, (i + s) % size) for i in range(size)])]
    pallas_call x1, Pallas kernels: 29.9 us -> 13.9 us  [attend_back(): pl.pallas_call(functools.partial(attend_back_kernel, rows, HEAD_DIM ** (-...]
    pallas_call x1, Pallas kernels: 28.7 us -> 13.7 us  [attend(): pl.pallas_call(functools.partial(attend_kernel, rows, HEAD_DIM ** (-0.5)...]
    ppermute x15, starting transfers between devices: 34.3 us -> 19.8 us  [z_shift(): lax.ppermute(value, 'seq', [(i, (i + step) % size) for i in range(size)])]
  transfers between devices with their start and end apart: 77 -> 83, of which waited for: 33 -> 25; matrix products, arithmetic and copies ran while one was open for 15% -> 14% of each run, Pallas kernels for 27% -> 32%
where the time goes in v2:
time: 600 us; the launch traced here: 595 us
  Pallas kernels  190 us (32%)
  waiting for transfers between devices  181 us (30%)
  starting transfers between devices  82 us (14%)
  other arithmetic  41.4 us (7%)
  local copies, waits for them, and re-layouts  35.9 us (6%)
  between operations  35 us (6%)
  matrix products  28.9 us (5%)
    pallas_call x4, Pallas kernels, feed(): pl.pallas_call(functools.partial(feed_kernel, columns // 3, earlier is no...  74.8 us
    ppermute x15, waiting for transfers between devices, z_shift(): lax.ppermute(value, 'seq', [(i, (i + step) % size) for i in range(size)])  65.3 us
    ppermute x44, waiting for transfers between devices, dp_swap(): return lax.ppermute(value, 'dp', [(i, i ^ flip) for i in range(size)])  62.2 us
    pallas_call x4, Pallas kernels, unit_gradients(): pl.pallas_call(functools.partial(grads_kernel, split), grid=(each * len(w...  57.8 us
    ppermute x44, starting transfers between devices, dp_swap(): return lax.ppermute(value, 'dp', [(i, i ^ flip) for i in range(size)])  43.7 us
    ppermute x11, waiting for transfers between devices, y_swap(): return lax.ppermute(value, 'tensor', [(0, 1), (1, 0)])  36.9 us
    dot_general x6, matrix products, right_product(): lax.dot_general(left, right, (((1,), (1,)), ((), ())), preferred_element_...  20.6 us
    ppermute x15, starting transfers between devices, z_shift(): lax.ppermute(value, 'seq', [(i, (i + step) % size) for i in range(size)])  19.8 us
  transfers between devices with their start and end apart: 83, of which 25 were waited for; matrix products, arithmetic and copies ran while one was open for 14% of the time, Pallas kernels for 32%

profile of v2, /device:TPU:0, one launch (start us, length us, event | category | flops | bytes accessed | tf_op | source)
XLA Modules:
  0.0 594.6 jit_solution(15007369694086904851)
XLA Ops:
  8.3 3.0 collective-permute-start.1
  16.5 2.8 shard_map.263
  25.1 4.2 fusion.8.x_ref
  29.2 9.2 %collective-permute-done.5.refs_2_ = bf16[96,1152]{1,0:T(8,128)(2,1)S(1)} collective-permute-done((bf16[96,1152]{1,0:T(8,128)(2,1)S(1)}, bf16[96,1152]{1,0:T(8,128)(2,1)S(1)}, u32[]{:S(2)}, u32[]{:S(2)}) %collective-permute-start.5) | collective-permute-done | bytes 221216 | tf_op jit(solution)/shard_map/ppermute | solution.py:44
  45.0 7.4 %collective-permute-done.8.refs_6_ = bf16[96,1792]{1,0:T(8,128)(2,1)S(1)} collective-permute-done((bf16[96,1792]{1,0:T(8,128)(2,1)S(1)}, bf16[96,1792]{1,0:T(8,128)(2,1)S(1)}, u32[]{:S(2)}, u32[]{:S(2)}) %collective-permute-start.8) | collective-permute-done | bytes 344096 | tf_op jit(solution)/shard_map/ppermute | solution.py:44
  52.4 5.6 collective-permute-done.7.refs_3_
  58.0 4.2 fusion.9.refs_0_
  62.2 5.3 collective-permute-done.9.refs_7_
  83.3 6.0 %shard_map.266 = (bf16[512,768]{1,0:T(8,128)(2,1)S(1)}, bf16[512,256]{1,0:T(8,128)(2,1)S(1)}, bf16[512,1536]{1,0:T(8,128)(2,1)S(1)}, bf16[16,96,1792]{2,1,0:T(8,128)(2,1)}) custom-call(s32[16]{0:T(128)S(1)} %stack.102.place_ref, bf16[8,96,1792]{2,1,0:T(8,128)(2,1)S(1)} %shard_map.265.mine_ref, bf16[8,96,1792]{2,1,0:T(8,128)(2,1)} %collective-permute-done.10.theirs_ref, ...), custom_call_target="tpu_custom_call" | custom-call | tf_op jit(solution)/shard_map/pallas_call | solution.py:355
  91.6 17.1 %collective-permute-done.13 = bf16[512,256]{1,0:T(8,128)(2,1)S(1)} collective-permute-done((bf16[512,256]{1,0:T(8,128)(2,1)S(1)}, bf16[512,256]{1,0:T(8,128)(2,1)S(1)}, u32[]{:S(2)}, u32[]{:S(2)}) %collective-permute-start.13) | collective-permute-done | bytes 262176 | tf_op jit(solution)/shard_map/ppermute | solution.py:53
  108.7 5.0 collective-permute-start.11
  113.7 21.4 %collective-permute-done.12 = bf16[512,256]{1,0:T(8,128)(2,1)S(1)} collective-permute-done((bf16[512,256]{1,0:T(8,128)(2,1)S(1)}, bf16[512,256]{1,0:T(8,128)(2,1)S(1)}, u32[]{:S(2)}, u32[]{:S(2)}) %collective-permute-start.12) | collective-permute-done | bytes 262176 | tf_op jit(solution)/shard_map/ppermute | solution.py:53
  135.2 2.8 shard_map.270
  143.3 13.7 %shard_map.267 = (bf16[512,768]{1,0:T(8,128)(2,1)S(1)}, f32[6,512,1]{2,1,0:T(8,128)S(1)}) custom-call(s32[4]{0:T(128)S(1)} %convert_add_fusion.8.flag_ref, bf16[512,768]{1,0:T(8,128)(2,1)S(1)} %get-tuple-element.201.q_ref, bf16[2048,128]{1,0:T(8,128)(2,1)S(1)} %get-tuple-element.353.k_ref, bf16[2048,128]{1,0:T(8,128)(2,1)S(1)} %get-tuple-element.352.v_ref, ...), custom_call_target="tpu_custom_call" | custom-call | tf_op jit(solution)/shard_map/pallas_call | solution.py:137
  157.0 4.2 convolution_convert_fusion
  165.4 15.5 %collective-permute-done.17 = bf16[256,1536]{1,0:T(8,128)(2,1)S(1)} collective-permute-done((bf16[256,1536]{1,0:T(8,128)(2,1)}, bf16[256,1536]{1,0:T(8,128)(2,1)S(1)}, u32[]{:S(2)}, u32[]{:S(2)}) %collective-permute-start.17) | collective-permute-done | bytes 786464 | tf_op jit(solution)/shard_map/ppermute | solution.py:48
  185.6 16.3 %collective-permute-start.19 = (bf16[256,1536]{1,0:T(8,128)(2,1)S(1)}, bf16[256,1536]{1,0:T(8,128)(2,1)S(1)}, u32[]{:S(2)}, u32[]{:S(2)}) collective-permute-start(bf16[256,1536]{1,0:T(8,128)(2,1)S(1)} %multiply_convert_fusion.refs_0_), channel_id=1, source_target_pairs={{0,16},{8,24},{16,0},{24,8},{1,17},{9,25},{17,1},{25,9},{2,18},{10... | collective-permute-start | bytes 2359304 | tf_op jit(solution)/shard_map/ppermute | solution.py:44
  204.4 2.7 copy-done
  207.1 12.7 %collective-permute-done.19.refs_2_ = bf16[256,1536]{1,0:T(8,128)(2,1)S(1)} collective-permute-done((bf16[256,1536]{1,0:T(8,128)(2,1)S(1)}, bf16[256,1536]{1,0:T(8,128)(2,1)S(1)}, u32[]{:S(2)}, u32[]{:S(2)}) %collective-permute-start.19) | collective-permute-done | bytes 786464 | tf_op jit(solution)/shard_map/ppermute | solution.py:44
  223.0 8.5 %collective-permute-done.23 = bf16[128,1536]{1,0:T(8,128)(2,1)S(1)} collective-permute-done((bf16[128,1536]{1,0:T(8,128)(2,1)S(1)}, bf16[128,1536]{1,0:T(8,128)(2,1)S(1)}, u32[]{:S(2)}, u32[]{:S(2)}) %collective-permute-start.23) | collective-permute-done | bytes 393248 | tf_op jit(solution)/shard_map/ppermute | solution.py:48
  235.5 2.7 copy-done.1
  238.1 14.4 %shard_map.271 = (bf16[2048,1152]{1,0:T(8,128)(2,1)}, bf16[1024,1536]{1,0:T(8,128)(2,1)}, bf16[1024,1536]{1,0:T(8,128)(2,1)}) custom-call(bf16[2048,1536]{1,0:T(8,128)(2,1)} %bitcast.158, bf16[2048,1536]{1,0:T(8,128)(2,1)} %bitcast.150, bf16[1536,1152]{1,0:T(8,128)(2,1)} %all-gather.5.cloned.1.call-done.refs_2_), custom_call_target="tpu_custom_call" | custom-call | tf_op jit(solution)/shard_map/pallas_call | solution.py:521
  252.6 14.4 %shard_map.272 = (bf16[2048,1152]{1,0:T(8,128)(2,1)}, bf16[1024,1536]{1,0:T(8,128)(2,1)}, bf16[1024,1536]{1,0:T(8,128)(2,1)}) custom-call(bf16[2048,1536]{1,0:T(8,128)(2,1)} %bitcast.159, bf16[2048,1536]{1,0:T(8,128)(2,1)} %bitcast.151, bf16[1536,1152]{1,0:T(8,128)(2,1)} %all-gather.5.cloned.1.call-done.refs_2_, ...), custom_call_target="tpu_custom_call", output_to_operand_aliasing={{0}: (3, {})} | custom-call | tf_op jit(solution)/shard_map/pallas_call | solution.py:521
  267.0 16.8 %shard_map.273 = bf16[1536,1152]{1,0:T(8,128)(2,1)} custom-call(bf16[2048,1536]{1,0:T(8,128)(2,1)} %bitcast.160, bf16[2048,1536]{1,0:T(8,128)(2,1)} %bitcast.152, bf16[2048,1152]{1,0:T(8,128)(2,1)} %get-tuple-element.224.p_ref), custom_call_target="tpu_custom_call" | custom-call | tf_op jit(solution)/shard_map/pallas_call | solution.py:557
  283.9 23.0 %shard_map.274 = (bf16[2048,2304]{1,0:T(8,128)(2,1)}, bf16[1024,1536]{1,0:T(8,128)(2,1)}, bf16[1024,1536]{1,0:T(8,128)(2,1)}) custom-call(bf16[2048,1536]{1,0:T(8,128)(2,1)} %bitcast.161, bf16[2048,1536]{1,0:T(8,128)(2,1)} %bitcast.153, bf16[1536,2304]{1,0:T(8,128)(2,1)} %all-gather.3.cloned.1.call-done.refs_2_, ...), custom_call_target="tpu_custom_call" | custom-call | tf_op jit(solution)/shard_map/pallas_call | solution.py:521
  306.9 22.9 %shard_map.275 = (bf16[2048,2304]{1,0:T(8,128)(2,1)}, bf16[1024,1536]{1,0:T(8,128)(2,1)}, bf16[1024,1536]{1,0:T(8,128)(2,1)}) custom-call(bf16[2048,1536]{1,0:T(8,128)(2,1)} %bitcast.162, bf16[2048,1536]{1,0:T(8,128)(2,1)} %bitcast.154, bf16[1536,2304]{1,0:T(8,128)(2,1)} %all-gather.3.cloned.1.call-done.refs_2_, ...), custom_call_target="tpu_custom_call", output_to_operand_aliasing={{0}: (5, {})} | custom-call | tf_op jit(solution)/shard_map/pallas_call | solution.py:521
  335.5 13.5 %shard_map.276 = bf16[1536,768]{1,0:T(8,128)(2,1)} custom-call(bf16[2048,1536]{1,0:T(8,128)(2,1)} %bitcast.163, bf16[2048,1536]{1,0:T(8,128)(2,1)} %bitcast.155, bf16[2048,2304]{1,0:T(8,128)(2,1)} %get-tuple-element.244.p_ref), custom_call_target="tpu_custom_call" | custom-call | flops 4831838208 | tf_op jit(solution)/shard_map/pallas_call | solution.py:557
  354.6 14.1 %shard_map.277 = bf16[1536,768]{1,0:T(8,128)(2,1)} custom-call(bf16[2048,1536]{1,0:T(8,128)(2,1)} %bitcast.164, bf16[2048,1536]{1,0:T(8,128)(2,1)} %bitcast.156, bf16[2048,2304]{1,0:T(8,128)(2,1)} %get-tuple-element.244.p_ref), custom_call_target="tpu_custom_call" | custom-call | flops 4831838208 | tf_op jit(solution)/shard_map/pallas_call | solution.py:557
  368.7 3.5 collective-permute-done.32
  373.1 3.3 multiply_reduce_fusion
  376.4 2.7 fusion.98.own_ref
  388.2 13.5 %shard_map.278 = bf16[1536,768]{1,0:T(8,128)(2,1)} custom-call(bf16[2048,1536]{1,0:T(8,128)(2,1)} %bitcast.165, bf16[2048,1536]{1,0:T(8,128)(2,1)} %bitcast.157, bf16[2048,2304]{1,0:T(8,128)(2,1)} %get-tuple-element.244.p_ref), custom_call_target="tpu_custom_call" | custom-call | flops 4831838208 | tf_op jit(solution)/shard_map/pallas_call | solution.py:557
  408.7 2.7 shard_map.280
  418.1 13.9 %shard_map.281 = (bf16[512,768]{1,0:T(8,128)(2,1)}, bf16[2048,256]{1,0:T(8,128)(2,1)}) custom-call(s32[4]{0:T(128)} %copy-done.46, bf16[512,768]{1,0:T(8,128)(2,1)} %copy-done.10, bf16[2048,128]{1,0:T(8,128)(2,1)} %copy-done.8, bf16[2048,128]{1,0:T(8,128)(2,1)} %copy-done.7, bf16[512,768]{1,0:T(8,128)(2,1)} %copy-done.24, f32[6,512,1]{2,1,0:T(8,128)} %copy-done.15, ...), custom_call_target="tpu_custom_call" | custom-call | tf_op jit(solution)/shard_map/pallas_call | solution.py:247
  432.0 16.8 %reduce-scatter.9.cloned.1.call-done = bf16[384,768]{1,0:T(8,128)(2,1)} async-done(((bf16[1536,768]{1,0:T(8,128)(2,1)}), bf16[384,768]{1,0:T(8,128)(2,1)}) %reduce-scatter.9.cloned.1.call-update) | async-done | bytes 589840 | tf_op jit(solution)/shard_map/reduce_scatter | solution.py:819
  475.0 5.1 collective-permute-done.46
  480.1 8.2 %collective-permute-done.42 = bf16[4,96,768]{2,1,0:T(8,128)(2,1)} collective-permute-done((bf16[4,96,768]{2,1,0:T(8,128)(2,1)}, bf16[4,96,768]{2,1,0:T(8,128)(2,1)}, u32[]{:S(2)}, u32[]{:S(2)}) %collective-permute-start.42) | collective-permute-done | bytes 589856 | tf_op jit(solution)/shard_map/ppermute | solution.py:44
  494.0 3.2 fusion.14
  498.8 4.6 fusion.17
  509.0 8.6 %collective-permute-done.52 = bf16[256,1536]{1,0:T(8,128)(2,1)S(1)} collective-permute-done((bf16[256,1536]{1,0:T(8,128)(2,1)S(1)}, bf16[256,1536]{1,0:T(8,128)(2,1)S(1)}, u32[]{:S(2)}, u32[]{:S(2)}) %collective-permute-start.52) | collective-permute-done | bytes 786464 | tf_op jit(solution)/shard_map/ppermute | solution.py:48
  517.6 7.2 %collective-permute-done.51 = bf16[4,96,256]{2,1,0:T(8,128)(2,1)S(1)} collective-permute-done((bf16[4,96,256]{2,1,0:T(8,128)(2,1)S(1)}, bf16[4,96,256]{2,1,0:T(8,128)(2,1)S(1)}, u32[]{:S(2)}, u32[]{:S(2)}) %collective-permute-start.51) | collective-permute-done | bytes 196640 | tf_op jit(solution)/shard_map/ppermute | solution.py:44
  528.0 5.0 fusion.18
  534.0 11.2 %collective-permute-done.54 = bf16[96,256]{1,0:T(8,128)(2,1)S(1)} collective-permute-done((bf16[96,256]{1,0:T(8,128)(2,1)S(1)}, bf16[96,256]{1,0:T(8,128)(2,1)S(1)}, u32[]{:S(2)}, u32[]{:S(2)}) %collective-permute-start.54) | collective-permute-done | bytes 49184 | tf_op jit(solution)/shard_map/ppermute | solution.py:53
  556.6 2.7 collective-permute-done.57
  566.7 3.3 collective-permute-done.71.refs_6_
  571.3 3.4 collective-permute-done.69
  574.9 3.5 maximum_select_fusion.5
  582.4 3.5 shard_map.284
  (484 shorter events, 144.8 us)
Async XLA Ops:
  7.2 231.0 %all-gather.5.cloned.1.call-start = ((), (), s32[]{:S(2)}) async-start(), calls=%async_computation.5 | async-start | bytes 4423680 | tf_op jit(solution)/shard_map/all_gather | solution.py:741
  22.7 16.5 %collective-permute-start.3 = (bf16[96,1792]{1,0:T(8,128)(2,1)S(1)}, bf16[96,1792]{1,0:T(8,128)(2,1)S(1)}, u32[]{:S(2)}, u32[]{:S(2)}) collective-permute-start(bf16[96,1792]{1,0:T(8,128)(2,1)S(1)} %collective-permute-done.refs_1_), channel_id=1, source_target_pairs={{0,16},{8,24},{16,0},{24,8},{1,17},{9,25},{17,1},{25,9},{2,18},{10... | collective-permute-start | bytes 1032200 | tf_op jit(solution)/shard_map/ppermute | solution.py:44
  23.2 15.9 %collective-permute-start.2 = (bf16[96,1792]{1,0:T(8,128)(2,1)S(1)}, bf16[96,1792]{1,0:T(8,128)(2,1)S(1)}, u32[]{:S(2)}, u32[]{:S(2)}) collective-permute-start(bf16[96,1792]{1,0:T(8,128)(2,1)S(1)} %collective-permute-done.refs_1_), channel_id=1, source_target_pairs={{0,2},{2,4},{4,6},{6,0},{1,3},{3,5},{5,7},{7,1},{8,10},{10,12},{12... | collective-permute-start | bytes 1032200 | tf_op jit(solution)/shard_map/ppermute | solution.py:53
  23.2 15.2 %collective-permute-start.5 = (bf16[96,1152]{1,0:T(8,128)(2,1)S(1)}, bf16[96,1152]{1,0:T(8,128)(2,1)S(1)}, u32[]{:S(2)}, u32[]{:S(2)}) collective-permute-start(bf16[96,1152]{1,0:T(8,128)(2,1)S(1)} %get-tuple-element.177), channel_id=1, source_target_pairs={{0,16},{8,24},{16,0},{24,8},{1,17},{9,25},{17,1},{25,9},{2,18},{10... | collective-permute-start | bytes 663560 | tf_op jit(solution)/shard_map/ppermute | solution.py:44
  24.7 14.4 %collective-permute-start.6 = (bf16[96,1152]{1,0:T(8,128)(2,1)S(1)}, bf16[96,1152]{1,0:T(8,128)(2,1)S(1)}, u32[]{:S(2)}, u32[]{:S(2)}) collective-permute-start(bf16[96,1152]{1,0:T(8,128)(2,1)S(1)} %get-tuple-element.178), channel_id=1, source_target_pairs={{0,24},{8,16},{16,8},{24,0},{1,25},{9,17},{17,9},{25,1},{2,26},{10... | collective-permute-start | bytes 663560 | tf_op jit(solution)/shard_map/ppermute | solution.py:44
  41.8 242.1 %all-gather.3.cloned.1.call-start = ((), (), s32[]{:S(2)}) async-start(), calls=%async_computation.4 | async-start | bytes 8847360 | tf_op jit(solution)/shard_map/all_gather | solution.py:766
  43.2 14.8 %collective-permute-start.7 = (bf16[96,1792]{1,0:T(8,128)(2,1)S(1)}, bf16[96,1792]{1,0:T(8,128)(2,1)S(1)}, u32[]{:S(2)}, u32[]{:S(2)}) collective-permute-start(bf16[96,1792]{1,0:T(8,128)(2,1)S(1)} %collective-permute-done.2.refs_2_), channel_id=1, source_target_pairs={{0,2},{2,4},{4,6},{6,0},{1,3},{3,5},{5,7},{7,1},{8,10},{10,12},{12... | collective-permute-start | bytes 1032200 | tf_op jit(solution)/shard_map/ppermute | solution.py:53
  69.2 14.1 %collective-permute-start.10 = (bf16[8,96,1792]{2,1,0:T(8,128)(2,1)S(1)}, bf16[8,96,1792]{2,1,0:T(8,128)(2,1)}, u32[]{:S(2)}, u32[]{:S(2)}) collective-permute-start(bf16[8,96,1792]{2,1,0:T(8,128)(2,1)S(1)} %shard_map.265.mine_ref), channel_id=1, source_target_pairs={{0,8},{8,0},{16,24},{24,16},{1,9},{9,1},{17,25},{25,17},{2,10},{10... | collective-permute-start | bytes 8257544 | tf_op jit(solution)/shard_map/ppermute | solution.py:44
  89.3 19.4 %collective-permute-start.13 = (bf16[512,256]{1,0:T(8,128)(2,1)S(1)}, bf16[512,256]{1,0:T(8,128)(2,1)S(1)}, u32[]{:S(2)}, u32[]{:S(2)}) collective-permute-start(bf16[512,256]{1,0:T(8,128)(2,1)S(1)} %get-tuple-element.202), channel_id=1, source_target_pairs={{0,6},{2,0},{4,2},{6,4},{1,7},{3,1},{5,3},{7,5},{8,14},{10,8},{12,... | collective-permute-start | bytes 786440 | tf_op jit(solution)/shard_map/ppermute | solution.py:53
  89.4 45.8 %collective-permute-start.14 = (bf16[96,2304]{1,0:T(8,128)(2,1)S(1)}, bf16[96,2304]{1,0:T(8,128)(2,1)S(1)}, u32[]{:S(2)}, u32[]{:S(2)}) collective-permute-start(bf16[96,2304]{1,0:T(8,128)(2,1)S(1)} %copy-done.54), channel_id=1, source_target_pairs={{0,8},{8,0},{16,24},{24,16},{1,9},{9,1},{17,25},{25,17},{2,10},{10... | collective-permute-start | bytes 1327112 | tf_op jit(solution)/shard_map/ppermute | solution.py:44
  89.9 45.2 %collective-permute-start.15 = (bf16[96,2304]{1,0:T(8,128)(2,1)S(1)}, bf16[96,2304]{1,0:T(8,128)(2,1)S(1)}, u32[]{:S(2)}, u32[]{:S(2)}) collective-permute-start(bf16[96,2304]{1,0:T(8,128)(2,1)S(1)} %copy-done.52), channel_id=1, source_target_pairs={{0,16},{8,24},{16,0},{24,8},{1,17},{9,25},{17,1},{25,9},{2,18},{10... | collective-permute-start | bytes 1327112 | tf_op jit(solution)/shard_map/ppermute | solution.py:44
  90.8 44.4 %collective-permute-start.16 = (bf16[96,2304]{1,0:T(8,128)(2,1)S(1)}, bf16[96,2304]{1,0:T(8,128)(2,1)S(1)}, u32[]{:S(2)}, u32[]{:S(2)}) collective-permute-start(bf16[96,2304]{1,0:T(8,128)(2,1)S(1)} %copy-done.50), channel_id=1, source_target_pairs={{0,24},{8,16},{16,8},{24,0},{1,25},{9,17},{17,9},{25,1},{2,26},{10... | collective-permute-start | bytes 1327112 | tf_op jit(solution)/shard_map/ppermute | solution.py:44
  91.3 43.8 %collective-permute-start.12 = (bf16[512,256]{1,0:T(8,128)(2,1)S(1)}, bf16[512,256]{1,0:T(8,128)(2,1)S(1)}, u32[]{:S(2)}, u32[]{:S(2)}) collective-permute-start(bf16[512,256]{1,0:T(8,128)(2,1)S(1)} %get-tuple-element.202), channel_id=1, source_target_pairs={{0,4},{2,6},{4,0},{6,2},{1,5},{3,7},{5,1},{7,3},{8,12},{10,14},{12... | collective-permute-start | bytes 786440 | tf_op jit(solution)/shard_map/ppermute | solution.py:53
  108.7 26.4 %collective-permute-start.11 = (bf16[512,256]{1,0:T(8,128)(2,1)S(1)}, bf16[512,256]{1,0:T(8,128)(2,1)S(1)}, u32[]{:S(2)}, u32[]{:S(2)}) collective-permute-start(bf16[512,256]{1,0:T(8,128)(2,1)S(1)} %get-tuple-element.202), channel_id=1, source_target_pairs={{0,2},{2,4},{4,6},{6,0},{1,3},{3,5},{5,7},{7,1},{8,10},{10,12},{12... | collective-permute-start | bytes 786440 | tf_op jit(solution)/shard_map/ppermute | solution.py:53
  138.1 230.6 %reduce-scatter.5.cloned.1.call-start = ((), (), s32[]{:S(2)}) async-start(), calls=%async_computation.6 | async-start | bytes 4423680 | tf_op jit(solution)/shard_map/reduce_scatter | solution.py:811
  142.0 38.9 %collective-permute-start.18 = (bf16[512,1536]{1,0:T(8,128)(2,1)}, bf16[512,1536]{1,0:T(8,128)(2,1)}, u32[]{:S(2)}, u32[]{:S(2)}) collective-permute-start(bf16[512,1536]{1,0:T(8,128)(2,1)} %fusion.9.refs_0_), channel_id=1, source_target_pairs={{0,16},{8,24},{16,0},{24,8},{1,17},{9,25},{17,1},{25,9},{2,18},{10... | collective-permute-start | bytes 4718600 | tf_op jit(solution)/shard_map/ppermute | solution.py:44
  161.2 19.7 %collective-permute-start.17 = (bf16[256,1536]{1,0:T(8,128)(2,1)}, bf16[256,1536]{1,0:T(8,128)(2,1)S(1)}, u32[]{:S(2)}, u32[]{:S(2)}) collective-permute-start(bf16[256,1536]{1,0:T(8,128)(2,1)} %convolution_convert_fusion), channel_id=1, source_target_pairs={{0,1},{1,0},{2,3},{3,2},{4,5},{5,4},{6,7},{7,6},{8,9},{9,8},{10,11... | collective-permute-start | bytes 2359304 | tf_op jit(solution)/shard_map/ppermute | solution.py:48
  162.7 39.1 %collective-permute-start.21 = (bf16[512,1536]{1,0:T(8,128)(2,1)}, bf16[512,1536]{1,0:T(8,128)(2,1)S(1)}, u32[]{:S(2)}, u32[]{:S(2)}) collective-permute-start(bf16[512,1536]{1,0:T(8,128)(2,1)} %fusion.9.refs_0_), channel_id=1, source_target_pairs={{0,8},{8,0},{16,24},{24,16},{1,9},{9,1},{17,25},{25,17},{2,10},{10... | collective-permute-start | bytes 4718600 | tf_op jit(solution)/shard_map/ppermute | solution.py:44
  181.8 20.1 %collective-permute-start.22 = (bf16[512,1536]{1,0:T(8,128)(2,1)}, bf16[512,1536]{1,0:T(8,128)(2,1)S(1)}, u32[]{:S(2)}, u32[]{:S(2)}) collective-permute-start(bf16[512,1536]{1,0:T(8,128)(2,1)} %collective-permute-done.18.refs_1_), channel_id=1, source_target_pairs={{0,8},{8,0},{16,24},{24,16},{1,9},{9,1},{17,25},{25,17},{2,10},{10... | collective-permute-start | bytes 4718600 | tf_op jit(solution)/shard_map/ppermute | solution.py:44
  184.2 22.9 %collective-permute-start.20 = (bf16[256,1536]{1,0:T(8,128)(2,1)S(1)}, bf16[256,1536]{1,0:T(8,128)(2,1)S(1)}, u32[]{:S(2)}, u32[]{:S(2)}) collective-permute-start(bf16[256,1536]{1,0:T(8,128)(2,1)S(1)} %multiply_convert_fusion.refs_0_), channel_id=1, source_target_pairs={{0,1},{1,0},{2,3},{3,2},{4,5},{5,4},{6,7},{7,6},{8,9},{9,8},{10,11... | collective-permute-start | bytes 2359304 | tf_op jit(solution)/shard_map/ppermute | solution.py:48
  185.6 34.3 %collective-permute-start.19 = (bf16[256,1536]{1,0:T(8,128)(2,1)S(1)}, bf16[256,1536]{1,0:T(8,128)(2,1)S(1)}, u32[]{:S(2)}, u32[]{:S(2)}) collective-permute-start(bf16[256,1536]{1,0:T(8,128)(2,1)S(1)} %multiply_convert_fusion.refs_0_), channel_id=1, source_target_pairs={{0,16},{8,24},{16,0},{24,8},{1,17},{9,25},{17,1},{25,9},{2,18},{10... | collective-permute-start | bytes 2359304 | tf_op jit(solution)/shard_map/ppermute | solution.py:44
  201.9 21.1 %collective-permute-start.25 = (bf16[256,1536]{1,0:T(8,128)(2,1)S(1)}, bf16[256,1536]{1,0:T(8,128)(2,1)S(1)}, u32[]{:S(2)}, u32[]{:S(2)}) collective-permute-start(bf16[256,1536]{1,0:T(8,128)(2,1)S(1)} %multiply_convert_fusion.refs_0_), channel_id=1, source_target_pairs={{0,8},{8,0},{16,24},{24,16},{1,9},{9,1},{17,25},{25,17},{2,10},{10... | collective-permute-start | bytes 2359304 | tf_op jit(solution)/shard_map/ppermute | solution.py:44
  283.8 117.9 %reduce-scatter.7.cloned.1.call-start = ((), (), s32[]{:S(2)}) async-start(), calls=%async_computation.7 | async-start | bytes 2949120 | tf_op jit(solution)/shard_map/reduce_scatter | solution.py:819
  306.9 22.9 %collective-permute-start.29 = (bf16[1024,1536]{1,0:T(8,128)(2,1)}, bf16[1024,1536]{1,0:T(8,128)(2,1)S(1)}, u32[]{:S(2)}, u32[]{:S(2)}) collective-permute-start(bf16[1024,1536]{1,0:T(8,128)(2,1)} %get-tuple-element.228), channel_id=1, source_target_pairs={{0,8},{8,0},{16,24},{24,16},{1,9},{9,1},{17,25},{25,17},{2,10},{10... | collective-permute-start | bytes 9437192 | tf_op jit(solution)/shard_map/ppermute | solution.py:44
  332.5 16.5 %collective-permute-start.30 = (bf16[128,1536]{1,0:T(8,128)(2,1)S(1)}, bf16[128,1536]{1,0:T(8,128)(2,1)}, u32[]{:S(2)}, u32[]{:S(2)}) collective-permute-start(bf16[128,1536]{1,0:T(8,128)(2,1)S(1)} %get-tuple-element.361), channel_id=1, source_target_pairs={{0,16},{8,24},{16,0},{24,8},{1,17},{9,25},{17,1},{25,9},{2,18},{10... | collective-permute-start | bytes 1179656 | tf_op jit(solution)/shard_map/ppermute | solution.py:44
  334.3 14.7 %collective-permute-start.31 = (bf16[128,1536]{1,0:T(8,128)(2,1)}, bf16[128,1536]{1,0:T(8,128)(2,1)}, u32[]{:S(2)}, u32[]{:S(2)}) collective-permute-start(bf16[128,1536]{1,0:T(8,128)(2,1)} %get-tuple-element.360), channel_id=1, source_target_pairs={{0,1},{1,0},{2,3},{3,2},{4,5},{5,4},{6,7},{7,6},{8,9},{9,8},{10,11... | collective-permute-start | bytes 1179656 | tf_op jit(solution)/shard_map/ppermute | solution.py:48
  349.0 99.8 %reduce-scatter.9.cloned.1.call-start = ((), (), s32[]{:S(2)}) async-start(), calls=%async_computation.8 | async-start | bytes 2949120 | tf_op jit(solution)/shard_map/reduce_scatter | solution.py:819
  352.6 19.6 %collective-permute-start.32 = (bf16[256,1536]{1,0:T(8,128)(2,1)}, bf16[256,1536]{1,0:T(8,128)(2,1)}, u32[]{:S(2)}, u32[]{:S(2)}) collective-permute-start(bf16[256,1536]{1,0:T(8,128)(2,1)} %pad_maximum_fusion.1), channel_id=1, source_target_pairs={{0,16},{8,24},{16,0},{24,8},{1,17},{9,25},{17,1},{25,9},{2,18},{10... | collective-permute-start | bytes 2359304 | tf_op jit(solution)/shard_map/ppermute | solution.py:44
  353.8 19.3 %collective-permute-start.33 = (bf16[256,1536]{1,0:T(8,128)(2,1)}, bf16[256,1536]{1,0:T(8,128)(2,1)}, u32[]{:S(2)}, u32[]{:S(2)}) collective-permute-start(bf16[256,1536]{1,0:T(8,128)(2,1)} %pad_maximum_fusion.2), channel_id=1, source_target_pairs={{0,1},{1,0},{2,3},{3,2},{4,5},{5,4},{6,7},{7,6},{8,9},{9,8},{10,11... | collective-permute-start | bytes 2359304 | tf_op jit(solution)/shard_map/ppermute | solution.py:48
  379.1 22.5 %collective-permute-start.35 = (bf16[1024,1536]{1,0:T(8,128)(2,1)}, bf16[1024,1536]{1,0:T(8,128)(2,1)}, u32[]{:S(2)}, u32[]{:S(2)}) collective-permute-start(bf16[1024,1536]{1,0:T(8,128)(2,1)} %get-tuple-element.243), channel_id=1, source_target_pairs={{0,8},{8,0},{16,24},{24,16},{1,9},{9,1},{17,25},{25,17},{2,10},{10... | collective-permute-start | bytes 9437192 | tf_op jit(solution)/shard_map/ppermute | solution.py:44
  379.2 180.1 %reduce-scatter.11.cloned.1.call-start = ((), (), s32[]{:S(2)}) async-start(), calls=%async_computation.9 | async-start | bytes 2949120 | tf_op jit(solution)/shard_map/reduce_scatter | solution.py:819
  379.3 22.4 %collective-permute-start.34 = (bf16[256,1536]{1,0:T(8,128)(2,1)S(1)}, bf16[256,1536]{1,0:T(8,128)(2,1)S(1)}, u32[]{:S(2)}, u32[]{:S(2)}) collective-permute-start(bf16[256,1536]{1,0:T(8,128)(2,1)S(1)} %fusion.98.own_ref), channel_id=1, source_target_pairs={{0,1},{1,0},{2,3},{3,2},{4,5},{5,4},{6,7},{7,6},{8,9},{9,8},{10,11... | collective-permute-start | bytes 2359304 | tf_op jit(solution)/shard_map/ppermute | solution.py:48
  411.3 37.5 %collective-permute-start.36 = (bf16[4,192,768]{2,1,0:T(8,128)(2,1)}, bf16[4,192,768]{2,1,0:T(8,128)(2,1)}, u32[]{:S(2)}, u32[]{:S(2)}) collective-permute-start(bf16[4,192,768]{2,1,0:T(8,128)(2,1)} %get-tuple-element.253), channel_id=1, source_target_pairs={{0,8},{8,0},{16,24},{24,16},{1,9},{9,1},{17,25},{25,17},{2,10},{10... | collective-permute-start | bytes 3538952 | tf_op jit(solution)/shard_map/ppermute | solution.py:44
  414.2 17.9 %collective-permute-start.38 = (bf16[128,1536]{1,0:T(8,128)(2,1)}, bf16[128,1536]{1,0:T(8,128)(2,1)}, u32[]{:S(2)}, u32[]{:S(2)}) collective-permute-start(bf16[128,1536]{1,0:T(8,128)(2,1)} %get-tuple-element.358), channel_id=1, source_target_pairs={{0,1},{1,0},{2,3},{3,2},{4,5},{5,4},{6,7},{7,6},{8,9},{9,8},{10,11... | collective-permute-start | bytes 1179656 | tf_op jit(solution)/shard_map/ppermute | solution.py:48
  415.3 16.7 %collective-permute-start.37 = (bf16[128,1536]{1,0:T(8,128)(2,1)}, bf16[128,1536]{1,0:T(8,128)(2,1)}, u32[]{:S(2)}, u32[]{:S(2)}) collective-permute-start(bf16[128,1536]{1,0:T(8,128)(2,1)} %get-tuple-element.359), channel_id=1, source_target_pairs={{0,16},{8,24},{16,0},{24,8},{1,17},{9,25},{17,1},{25,9},{2,18},{10... | collective-permute-start | bytes 1179656 | tf_op jit(solution)/shard_map/ppermute | solution.py:44
  416.2 15.8 %collective-permute-start.40 = (bf16[96,1152]{1,0:T(8,128)(2,1)}, bf16[96,1152]{1,0:T(8,128)(2,1)S(1)}, u32[]{:S(2)}, u32[]{:S(2)}) collective-permute-start(bf16[96,1152]{1,0:T(8,128)(2,1)} %get-tuple-element.355), channel_id=1, source_target_pairs={{0,16},{8,24},{16,0},{24,8},{1,17},{9,25},{17,1},{25,9},{2,18},{10... | collective-permute-start | bytes 663560 | tf_op jit(solution)/shard_map/ppermute | solution.py:44
  450.8 15.8 %collective-permute-start.47 = (bf16[512,256]{1,0:T(8,128)(2,1)}, bf16[512,256]{1,0:T(8,128)(2,1)S(1)}, u32[]{:S(2)}, u32[]{:S(2)}) collective-permute-start(bf16[512,256]{1,0:T(8,128)(2,1)} %get-tuple-element.349), channel_id=1, source_target_pairs={{0,2},{2,4},{4,6},{6,0},{1,3},{3,5},{5,7},{7,1},{8,10},{10,12},{12... | collective-permute-start | bytes 786440 | tf_op jit(solution)/shard_map/ppermute | solution.py:53
  455.0 33.3 %collective-permute-start.43 = (bf16[256,1536]{1,0:T(8,128)(2,1)}, bf16[256,1536]{1,0:T(8,128)(2,1)}, u32[]{:S(2)}, u32[]{:S(2)}) collective-permute-start(bf16[256,1536]{1,0:T(8,128)(2,1)} %pad_maximum_fusion.3), channel_id=1, source_target_pairs={{0,16},{8,24},{16,0},{24,8},{1,17},{9,25},{17,1},{25,9},{2,18},{10... | collective-permute-start | bytes 2359304 | tf_op jit(solution)/shard_map/ppermute | solution.py:44
  457.4 30.9 %collective-permute-start.44 = (bf16[256,1536]{1,0:T(8,128)(2,1)}, bf16[256,1536]{1,0:T(8,128)(2,1)}, u32[]{:S(2)}, u32[]{:S(2)}) collective-permute-start(bf16[256,1536]{1,0:T(8,128)(2,1)} %pad_maximum_fusion.4), channel_id=1, source_target_pairs={{0,1},{1,0},{2,3},{3,2},{4,5},{5,4},{6,7},{7,6},{8,9},{9,8},{10,11... | collective-permute-start | bytes 2359304 | tf_op jit(solution)/shard_map/ppermute | solution.py:48
  462.7 25.5 %collective-permute-start.42 = (bf16[4,96,768]{2,1,0:T(8,128)(2,1)}, bf16[4,96,768]{2,1,0:T(8,128)(2,1)}, u32[]{:S(2)}, u32[]{:S(2)}) collective-permute-start(bf16[4,96,768]{2,1,0:T(8,128)(2,1)} %fusion.47), channel_id=1, source_target_pairs={{0,16},{8,24},{16,0},{24,8},{1,17},{9,25},{17,1},{25,9},{2,18},{10... | collective-permute-start | bytes 1769480 | tf_op jit(solution)/shard_map/ppermute | solution.py:44
  464.7 15.4 %collective-permute-start.46 = (bf16[512,256]{1,0:T(8,128)(2,1)}, bf16[512,256]{1,0:T(8,128)(2,1)S(1)}, u32[]{:S(2)}, u32[]{:S(2)}) collective-permute-start(bf16[512,256]{1,0:T(8,128)(2,1)} %get-tuple-element.350), channel_id=1, source_target_pairs={{0,4},{2,6},{4,0},{6,2},{1,5},{3,7},{5,1},{7,3},{8,12},{10,14},{12... | collective-permute-start | bytes 786440 | tf_op jit(solution)/shard_map/ppermute | solution.py:53
  480.1 72.4 %collective-permute-start.63 = (bf16[96,768]{1,0:T(8,128)(2,1)}, bf16[96,768]{1,0:T(8,128)(2,1)}, u32[]{:S(2)}, u32[]{:S(2)}) collective-permute-start(bf16[96,768]{1,0:T(8,128)(2,1)} %get-tuple-element.372), channel_id=1, source_target_pairs={{0,24},{8,16},{16,8},{24,0},{1,25},{9,17},{17,9},{25,1},{2,26},{10... | collective-permute-start | bytes 442376 | tf_op jit(solution)/shard_map/ppermute | solution.py:44
  497.2 20.4 %collective-permute-start.52 = (bf16[256,1536]{1,0:T(8,128)(2,1)S(1)}, bf16[256,1536]{1,0:T(8,128)(2,1)S(1)}, u32[]{:S(2)}, u32[]{:S(2)}) collective-permute-start(bf16[256,1536]{1,0:T(8,128)(2,1)S(1)} %fusion.14), channel_id=1, source_target_pairs={{0,1},{1,0},{2,3},{3,2},{4,5},{5,4},{6,7},{7,6},{8,9},{9,8},{10,11... | collective-permute-start | bytes 2359304 | tf_op jit(solution)/shard_map/ppermute | solution.py:48
  505.0 19.8 %collective-permute-start.50 = (bf16[4,96,768]{2,1,0:T(8,128)(2,1)S(1)}, bf16[4,96,768]{2,1,0:T(8,128)(2,1)S(1)}, u32[]{:S(2)}, u32[]{:S(2)}) collective-permute-start(bf16[4,96,768]{2,1,0:T(8,128)(2,1)S(1)} %fusion.48), channel_id=1, source_target_pairs={{0,16},{8,24},{16,0},{24,8},{1,17},{9,25},{17,1},{25,9},{2,18},{10... | collective-permute-start | bytes 1769480 | tf_op jit(solution)/shard_map/ppermute | solution.py:44
  506.8 18.0 %collective-permute-start.51 = (bf16[4,96,256]{2,1,0:T(8,128)(2,1)S(1)}, bf16[4,96,256]{2,1,0:T(8,128)(2,1)S(1)}, u32[]{:S(2)}, u32[]{:S(2)}) collective-permute-start(bf16[4,96,256]{2,1,0:T(8,128)(2,1)S(1)} %fusion.68), channel_id=1, source_target_pairs={{0,16},{8,24},{16,0},{24,8},{1,17},{9,25},{17,1},{25,9},{2,18},{10... | collective-permute-start | bytes 589832 | tf_op jit(solution)/shard_map/ppermute | solution.py:44
  508.5 36.7 %collective-permute-start.55 = (bf16[256,1536]{1,0:T(8,128)(2,1)S(1)}, bf16[256,1536]{1,0:T(8,128)(2,1)S(1)}, u32[]{:S(2)}, u32[]{:S(2)}) collective-permute-start(bf16[256,1536]{1,0:T(8,128)(2,1)S(1)} %fusion.17), channel_id=1, source_target_pairs={{0,1},{1,0},{2,3},{3,2},{4,5},{5,4},{6,7},{7,6},{8,9},{9,8},{10,11... | collective-permute-start | bytes 2359304 | tf_op jit(solution)/shard_map/ppermute | solution.py:48
  525.0 20.1 %collective-permute-start.53 = (bf16[96,1536]{1,0:T(8,128)(2,1)S(1)}, bf16[96,1536]{1,0:T(8,128)(2,1)S(1)}, u32[]{:S(2)}, u32[]{:S(2)}) collective-permute-start(bf16[96,1536]{1,0:T(8,128)(2,1)S(1)} %fusion.67), channel_id=1, source_target_pairs={{0,2},{2,4},{4,6},{6,0},{1,3},{3,5},{5,7},{7,1},{8,10},{10,12},{12... | collective-permute-start | bytes 884744 | tf_op jit(solution)/shard_map/ppermute | solution.py:53
  555.3 19.4 %collective-permute-start.69 = (bf16[256,1536]{1,0:T(8,128)(2,1)}, bf16[256,1536]{1,0:T(8,128)(2,1)}, u32[]{:S(2)}, u32[]{:S(2)}) collective-permute-start(bf16[256,1536]{1,0:T(8,128)(2,1)} %fusion.18), channel_id=1, source_target_pairs={{0,1},{1,0},{2,3},{3,2},{4,5},{5,4},{6,7},{7,6},{8,9},{9,8},{10,11... | collective-permute-start | bytes 2359304 | tf_op jit(solution)/shard_map/ppermute | solution.py:48
  (141 other events, 1780.6 us)
Sparse Core Ops, SparseCore 0:
  41.9 94.0 all-gather.4
  138.2 125.6 all-gather.2
  283.9 64.5 reduce-scatter.4
  350.7 48.3 reduce-scatter.6
  401.2 47.5 reduce-scatter.8
  492.8 55.6 reduce-scatter.10

commit v3 on v2

--- a/solution.py
+++ b/solution.py
@@ -3,6 +3,7 @@
 
 import jax
 import jax.numpy as jnp
+import numpy as np
 from jax import lax
 from jax.experimental import pallas as pl
 from jax.experimental.pallas import tpu as pltpu
@@ -79,12 +80,44 @@
     )(places, *pieces)
 
 
+def pick_kernel(count, place_ref, *refs):
+    stacks, outs = refs[:count], refs[count:]
+    for i, out in enumerate(outs):
+        at = 0
+        for stack in stacks:
+            wide = stack.shape[2]
+            out[:, at : at + wide] = stack[place_ref[i]]
+            at += wide
+
+
+def pick_pieces(stacks, places):
+    vmem = pl.BlockSpec(memory_space=pltpu.VMEM)
+    slots, rows = stacks[0].shape[:2]
+    columns = sum(stack.shape[2] for stack in stacks)
+    return pl.pallas_call(
+        functools.partial(pick_kernel, len(stacks)),
+        out_shape=[jax.ShapeDtypeStruct((rows, columns), stacks[0].dtype)] * slots,
+        in_specs=[pl.BlockSpec(memory_space=pltpu.SMEM)] + [vmem] * len(stacks),
+        out_specs=[vmem] * slots,
+        compiler_params=pltpu.CompilerParams(vmem_limit_bytes=24 * MIB),
+        cost_estimate=FREE,
+    )(places, *stacks)
+
+
+SEGMENT_STEP = 1 << 16
+
+
 def pair_mask(seg_q, pos_q, seg_k, pos_k):
     return ((seg_k == 0) | (seg_k == seg_q)) & (pos_k <= pos_q)
 
 
+def block_mask(sq_ref, pq_ref, codes):
+    segments = codes // SEGMENT_STEP
+    return pair_mask(sq_ref[...], pq_ref[...], segments, codes - segments * SEGMENT_STEP)
+
+
 def attend_kernel(
-    rows, factor, flag_ref, q_ref, k_ref, v_ref, sq_ref, pq_ref, sk_ref, pk_ref,
+    rows, factor, flag_ref, q_ref, k_ref, v_ref, sq_ref, pq_ref, code_ref,
     o_ref, lse_ref, top_ref, sum_ref, acc_ref,
 ):
     blocks = k_ref.shape[0] // rows
@@ -95,19 +128,19 @@
 
     def block_step(j, masked):
         span = pl.ds(pl.multiple_of(j * rows, rows), rows)
-        s = right_product(q, k_ref[span, :]) * factor
+        s = right_product(k_ref[span, :], q) * factor
         if masked:
-            mask = pair_mask(sq_ref[...], pq_ref[...], sk_ref[j], pk_ref[j])
+            mask = block_mask(sq_ref, pq_ref, code_ref[j])
             s = jnp.where(mask, s, NEG_FILL)
         top = top_ref[...]
-        new_top = jnp.maximum(top, jnp.max(s, axis=1, keepdims=True))
+        new_top = jnp.maximum(top, jnp.max(s, axis=0, keepdims=True))
         e = jnp.exp2(s - new_top)
         if masked:
             e = jnp.where(mask, e, 0.0)
         shrink = jnp.exp2(top - new_top)
         top_ref[...] = new_top
-        sum_ref[...] = sum_ref[...] * shrink + jnp.sum(e, axis=1, keepdims=True)
-        acc_ref[...] = acc_ref[...] * shrink + product(e.astype(BF16), v_ref[span, :])
+        sum_ref[...] = sum_ref[...] * shrink + jnp.sum(e, axis=0, keepdims=True)
+        acc_ref[...] = acc_ref[...] * shrink + left_product(v_ref[span, :], e.astype(BF16))
 
     def step(j, carry):
         @pl.when(flag_ref[j] == 2)
@@ -122,11 +155,11 @@
 
     lax.fori_loop(0, blocks, step, 0)
     total = sum_ref[...]
-    o_ref[...] = (acc_ref[...] / total).astype(o_ref.dtype)
+    o_ref[...] = (acc_ref[...] / total).T.astype(o_ref.dtype)
     lse_ref[...] = (top_ref[...] + jnp.log2(total))[None]
 
 
-def attend(q, keys, values, seg_q, pos_q, seg_k, pos_k, flags):
+def attend(q, keys, values, seg_q, pos_q, codes, flags):
     rows, width = q.shape
     heads = width // HEAD_DIM
     kv_heads = keys.shape[1] // HEAD_DIM
@@ -142,33 +175,31 @@
             pl.BlockSpec((rows, HEAD_DIM), lambda h: (0, h)),
             pl.BlockSpec((length, HEAD_DIM), lambda h: (0, h // repeat)),
             pl.BlockSpec((length, HEAD_DIM), lambda h: (0, h // repeat)),
-            whole(rows, 1),
-            whole(rows, 1),
-            whole(blocks, 1, rows),
-            whole(blocks, 1, rows),
+            whole(1, rows),
+            whole(1, rows),
+            whole(blocks, rows, 1),
         ],
         out_specs=[
             pl.BlockSpec((rows, HEAD_DIM), lambda h: (0, h)),
-            pl.BlockSpec((1, rows, 1), lambda h: (h, 0, 0)),
+            pl.BlockSpec((1, 1, rows), lambda h: (h, 0, 0)),
         ],
         out_shape=[
             jax.ShapeDtypeStruct((rows, width), BF16),
-            jax.ShapeDtypeStruct((heads, rows, 1), F32),
+            jax.ShapeDtypeStruct((heads, 1, rows), F32),
         ],
         scratch_shapes=[
-            pltpu.VMEM((rows, 1), F32),
-            pltpu.VMEM((rows, 1), F32),
-            pltpu.VMEM((rows, HEAD_DIM), F32),
+            pltpu.VMEM((1, rows), F32),
+            pltpu.VMEM((1, rows), F32),
+            pltpu.VMEM((HEAD_DIM, rows), F32),
         ],
         compiler_params=pltpu.CompilerParams(vmem_limit_bytes=40 * MIB),
         cost_estimate=FREE,
-    )(flags, q, keys, values, seg_q, pos_q, seg_k, pos_k)
+    )(flags, q, keys, values, seg_q, pos_q, codes)
 
 
 def attend_back_kernel(
     rows, factor, scale, repeat, flag_ref, q_ref, k_ref, v_ref, do_ref, lse_ref, cos_ref, sin_ref,
-    sq_ref, pq_ref, sk_ref, pk_ref, dq_ref, dkv_ref, dk_acc, dv_acc, dq_acc,
-    p_keep, dp_keep, delta_ref,
+    sq_ref, pq_ref, code_ref, dq_ref, dkv_ref, dk_acc, dv_acc, dq_acc, p_keep, dp_keep, delta_ref,
 ):
     head = pl.program_id(0)
     blocks = k_ref.shape[0] // rows
@@ -188,14 +219,13 @@
         return pl.ds(pl.multiple_of(j * rows, rows), rows)
 
     def first_pass(j, masked):
-        p = jnp.exp2(right_product(q, k_ref[span_of(j), :]) * factor - lse)
+        p = jnp.exp2(right_product(k_ref[span_of(j), :], q) * factor - lse)
         if masked:
-            mask = pair_mask(sq_ref[...], pq_ref[...], sk_ref[j], pk_ref[j])
-            p = jnp.where(mask, p, 0.0)
-        dp = right_product(d_o, v_ref[span_of(j), :])
+            p = jnp.where(block_mask(sq_ref, pq_ref, code_ref[j]), p, 0.0)
+        dp = right_product(v_ref[span_of(j), :], d_o)
         p_keep[j] = p
         dp_keep[j] = dp
-        delta_ref[...] += jnp.sum(p * dp, axis=1, keepdims=True)
+        delta_ref[...] += jnp.sum(p * dp, axis=0, keepdims=True)
 
     def first_step(j, carry):
         @pl.when(flag_ref[j] == 2)
@@ -216,14 +246,14 @@
             p = p_keep[j]
             ds = (p * (dp_keep[j] - delta_ref[...])).astype(BF16)
             span = span_of(j)
-            dv_acc[span, :] += left_product(p.astype(BF16), d_o)
-            dk_acc[span, :] += left_product(ds, q)
-            dq_acc[...] += product(ds, k_ref[span, :])
+            dv_acc[span, :] += product(p.astype(BF16), d_o)
+            dk_acc[span, :] += product(ds, q)
+            dq_acc[...] += left_product(k_ref[span, :], ds)
 
         return carry
 
     lax.fori_loop(0, blocks, second_step, 0)
-    (turned,) = rope_lanes(dq_acc[...] * scale, cos_ref[...], -sin_ref[...])
+    (turned,) = rope_lanes((dq_acc[...] * scale).T, cos_ref[...], -sin_ref[...])
     dq_ref[...] = turned.astype(dq_ref.dtype)
 
     @pl.when(lax.rem(head, repeat) == repeat - 1)
@@ -232,7 +262,7 @@
         dkv_ref[:, HEAD_DIM:] = dv_acc[...].astype(dkv_ref.dtype)
 
 
-def attend_back(q, keys, values, d_o, lse, cosine, sine, seg_q, pos_q, seg_k, pos_k, flags):
+def attend_back(q, keys, values, d_o, lse, cosine, sine, seg_q, pos_q, codes, flags):
     rows, width = q.shape
     heads = width // HEAD_DIM
     kv_heads = keys.shape[1] // HEAD_DIM
@@ -255,15 +285,19 @@
             held,
             held,
             per_head,
-            pl.BlockSpec((1, rows, 1), lambda h: (h, 0, 0)),
+            pl.BlockSpec((1, 1, rows), lambda h: (h, 0, 0)),
             whole(rows, HEAD_DIM),
             whole(rows, HEAD_DIM),
-            whole(rows, 1),
-            whole(rows, 1),
-            whole(blocks, 1, rows),
-            whole(blocks, 1, rows),
-        ],
-        out_specs=[per_head, pl.BlockSpec((length, 2 * HEAD_DIM), lambda h: (0, h // repeat))],
+            whole(1, rows),
+            whole(1, rows),
+            whole(blocks, rows, 1),
+        ],
+        out_specs=[
+            per_head,
+            pl.BlockSpec(
+                (length, 2 * HEAD_DIM), lambda h: (0, h // repeat), pipeline_mode=pl.Buffered(1)
+            ),
+        ],
         out_shape=[
             jax.ShapeDtypeStruct((rows, width), BF16),
             jax.ShapeDtypeStruct((length, 2 * keys.shape[1]), BF16),
@@ -271,14 +305,14 @@
         scratch_shapes=[
             pltpu.VMEM((length, HEAD_DIM), F32),
             pltpu.VMEM((length, HEAD_DIM), F32),
-            pltpu.VMEM((rows, HEAD_DIM), F32),
+            pltpu.VMEM((HEAD_DIM, rows), F32),
             pltpu.VMEM((blocks, rows, rows), F32),
             pltpu.VMEM((blocks, rows, rows), F32),
-            pltpu.VMEM((rows, 1), F32),
+            pltpu.VMEM((1, rows), F32),
         ],
         compiler_params=pltpu.CompilerParams(vmem_limit_bytes=58 * MIB),
         cost_estimate=FREE,
-    )(flags, q, keys, values, d_o, lse, cosine, sine, seg_q, pos_q, seg_k, pos_k)
+    )(flags, q, keys, values, d_o, lse, cosine, sine, seg_q, pos_q, codes)
 
 
 def rope_tables(places, width):
@@ -432,19 +466,22 @@
 
 def lay_kernel(cut, place_ref, *refs):
     n_dp = cut.n_dp
-    firsts, *seconds = (refs[i * n_dp : (i + 1) * n_dp] for i in range(4))
-    outs = refs[4 * n_dp :]
+    firsts, ups = refs[:n_dp], refs[n_dp : 2 * n_dp]
+    outs = refs[2 * n_dp :]
+    down_at = 3 * cut.width[0]
+    lasts = ((firsts, down_at + cut.width[1]), (ups, 0), (firsts, down_at))
     for i, out in enumerate(outs):
-        for part in range(2):
-            main, width = cut.main[part], cut.width[part]
+        last, last_at = lasts[i]
+        for part, (pieces, at) in enumerate(((firsts, i * cut.width[0]), lasts[i])):
+            main = cut.main[part]
             for k in range(n_dp):
-                piece = seconds[i][k] if part else firsts[k].at[:, i * width : (i + 1) * width]
-                owner = place_ref[k]
-                low = pl.multiple_of(cut.start[part] + owner * main, 128)
-                out[:, pl.ds(low, main)] = piece[:, :main].astype(F32)
+                low = pl.multiple_of(cut.start[part] + place_ref[k] * main, 128)
+                out[:, pl.ds(low, main)] = pieces[k][:, at : at + main].astype(F32)
         if cut.rest:
-            main = cut.main[1]
-            tails = [piece[:, main:].astype(F32)[:, : cut.rest] for piece in seconds[i]]
+            tails = [
+                piece[:, last_at + cut.main[1] : last_at + cut.width[1]].astype(F32)[:, : cut.rest]
+                for piece in last
+            ]
             laid = []
             for b in range(n_dp):
                 laid.append(
@@ -534,6 +571,10 @@
     )(*operands)
 
 
+def one_grads_kernel(left_ref, p_ref, o_ref):
+    o_ref[...] = left_product(left_ref[...], p_ref[...]).astype(BF16)
+
+
 def grads_kernel(split, t_ref, c_ref, p_ref, o_ref):
     step = pl.program_id(0)
 
@@ -554,15 +595,18 @@
     split = each * sum(i < 2 for i in which)
     first = which[0] * each
     held = pl.BlockSpec((rows, width), lambda i: (0, 0), pipeline_mode=pl.Buffered(1))
+    kernel, lefts = functools.partial(grads_kernel, split), (tokens, cots)
+    if len(which) == 1:
+        kernel, lefts = one_grads_kernel, ((tokens, tokens, cots)[which[0]],)
     return pl.pallas_call(
-        functools.partial(grads_kernel, split),
+        kernel,
         grid=(each * len(which),),
-        in_specs=[held, held, pl.BlockSpec((rows, wide), lambda i: (0, first + i))],
+        in_specs=[held] * len(lefts) + [pl.BlockSpec((rows, wide), lambda i: (0, first + i))],
         out_specs=pl.BlockSpec((width, wide), lambda i: (0, i)),
         out_shape=jax.ShapeDtypeStruct((width, len(which) * count), BF16),
         compiler_params=pltpu.CompilerParams(vmem_limit_bytes=56 * MIB),
         cost_estimate=cost,
-    )(tokens, cots, kept)
+    )(*lefts, kept)
 
 
 def d_o_kernel(own_ref, other_ref, w_ref, d_o_ref, rows_ref):
@@ -594,6 +638,28 @@
         compiler_params=pltpu.CompilerParams(vmem_limit_bytes=32 * MIB),
         cost_estimate=FREE,
     )(own, other, weights)
+
+
+def against_kernel(left_ref, right_ref, out_ref):
+    out_ref[...] = right_product(left_ref[...], right_ref[...]).astype(out_ref.dtype)
+
+
+def against(left, right, dtype):
+    rows, depth = left.shape
+    count = right.shape[0]
+    wide = 512 if count % 512 == 0 else count
+    return pl.pallas_call(
+        against_kernel,
+        grid=(count // wide,),
+        in_specs=[
+            pl.BlockSpec((rows, depth), lambda i: (0, 0)),
+            pl.BlockSpec((wide, depth), lambda i: (i, 0)),
+        ],
+        out_specs=pl.BlockSpec((rows, wide), lambda i: (0, i)),
+        out_shape=jax.ShapeDtypeStruct((rows, count), dtype),
+        compiler_params=pltpu.CompilerParams(vmem_limit_bytes=32 * MIB),
+        cost_estimate=FREE,
+    )(left, right)
 
 
 def halves_kernel(n_seq, share, core_ref, left_ref, right_ref, own_ref, sent_ref, keep_ref):
@@ -653,6 +719,11 @@
             self.summed(2 * t + cut, 3 * t) + corner_y.astype(F32),
         ]
         return tuple(jnp.concatenate(part, axis=0).astype(BF16) for part in (to_x, to_y))
+
+    def sides_of(self, corner_x):
+        t = self.t
+        to_y = self.summed(t, 2 * t) + corner_x.astype(F32)
+        return self.summed(2 * t, 3 * t).astype(BF16), to_y.astype(BF16)
 
     def home(self, over_x, over_y):
         return self.summed(0, self.t) + over_x.astype(F32) + over_y.astype(F32)
@@ -672,9 +743,25 @@
     blocks = group // rows
     q_width, kv_width = query_weight.shape[1], key_weight.shape[1]
     kv_end = q_width + kv_width
-    dp_owners = jnp.stack([dp ^ k for k in range(n_dp)]).astype(jnp.int32)
-    dp_slots = (dp_owners % 2) * (n_dp // 2) + dp_owners // 2
-    seq_places = jnp.stack([(seq - s) % n_seq for s in range(n_seq)]).astype(jnp.int32)
+    def slots_of(owners):
+        return (owners % 2) * (n_dp // 2) + owners // 2
+
+    dp_owners = dp ^ jnp.arange(n_dp, dtype=jnp.int32)
+    dp_slots = slots_of(dp_owners)
+    seq_places = (seq - jnp.arange(n_seq, dtype=jnp.int32) + n_seq) % n_seq
+    flips = jnp.repeat(np.array([0, 2, 1, 3], np.int32), n_seq)
+    all_places = jnp.tile(seq_places, 4) * n_dp + slots_of(dp ^ flips)
+    core, x = (dp % 2).astype(jnp.int32), (dp // 2).astype(jnp.int32)
+    dp_owners, dp_slots, seq_places, all_places, core_place, core, x, *scalars = together(
+        dp_owners, dp_slots, seq_places, all_places, core[None], core, x,
+        *[seq_places[s] for s in range(n_seq)],
+    )
+
+    def take(values, index, axis):
+        return lax.dynamic_index_in_dim(
+            values, index, axis, keepdims=False, allow_negative_indices=False
+        )
+
 
     def vector_in(vector):
         parts = vector.reshape(n_dp // 2, 2, n_seq, share)
@@ -688,7 +775,7 @@
     owner, place = index // (share * n_seq), index // share % n_seq
     slot = owner % 2 * (n_dp // 2) + owner // 2
     inner_of = (place * n_dp + slot) * share + index % share
-    shuffle = (inner_of[:, None] == index[None, :]).astype(BF16)
+    (shuffle,) = together((inner_of[:, None] == index[None, :]).astype(BF16))
 
     def relative(values):
         turned = jnp.concatenate([values[half:], values[:half]], axis=0)
@@ -698,14 +785,9 @@
         return product(relative(values), shuffle).astype(BF16)
 
     def from_inner(values):
-        return right_product(values, shuffle).astype(BF16)
+        return against(values, shuffle, BF16)
 
     gain_first, gain_second = vector_in(first_gain), vector_in(second_gain)
-
-    def slots_of(flips):
-        return jnp.stack(
-            [seq_places[s] * n_dp + dp_slots[k] for k in flips for s in range(n_seq)]
-        ).astype(jnp.int32)
 
     cut = Cut(gate_weight.shape[1], n_dp)
 
@@ -714,13 +796,22 @@
 
     def stack_units(pieces):
         return assemble(pieces, dp_slots).reshape(n_dp * share, pieces[0].shape[1])
+
+    own_place = relative(take(positions.reshape(blocks, rows), scalars[0], 0))
+    own_segment = relative(take(segments.reshape(blocks, rows), scalars[0], 0))
+    def tables(places):
+        cosine, sine = rope_tables(places, HEAD_DIM)
+        return (
+            jnp.concatenate([cosine, cosine], axis=1), jnp.concatenate([-sine, sine], axis=1)
+        )
+
 
     line = [jnp.concatenate([query_weight, key_weight, value_weight, out_weight.T], axis=1)]
     over_x = []
     for s in range(n_seq):
         over_x.append(dp_swap(line[s], 2))
         if s + 1 == n_seq:
-            cot_own = to_inner(cotangent)
+            cot_own = to_inner(after(cotangent, line[s]))
             over_x[s], cot_own = together(over_x[s], cot_own)
             break
         moved = z_shift(line[s], 1)
@@ -732,9 +823,10 @@
             first_parts, second_parts = parts[:n_dp], parts[n_dp:]
         elif s == 1:
             first_parts = spread(first_parts)
-            inputs = to_inner(hidden)
-            moved, over_x[s], inputs, *first_parts = together(
-                moved, over_x[s], inputs, *first_parts
+            inputs = to_inner(after(hidden, line[s]))
+            cosine, sine = tables(after(own_place, line[s]))
+            moved, over_x[s], inputs, cosine, sine, *first_parts = together(
+                moved, over_x[s], inputs, cosine, sine, *first_parts
             )
         elif s == 2:
             first_stacked = stack_units(first_parts)
@@ -745,13 +837,7 @@
         line.append(moved)
     mine = assemble(line + over_x, jnp.arange(2 * n_seq, dtype=jnp.int32))
     theirs = dp_swap(mine, 1)
-    all_places = slots_of((0, 2, 1, 3))
-
-    own_place = relative(lax.dynamic_slice_in_dim(positions, seq * rows, rows))
-    own_segment = relative(lax.dynamic_slice_in_dim(segments, seq * rows, rows))
-    cosine, sine = rope_tables(own_place, HEAD_DIM)
-    cosine = jnp.concatenate([cosine, cosine], axis=1)
-    sine = jnp.concatenate([-sine, sine], axis=1)
+
     bias = jnp.concatenate([query_bias, key_bias, value_bias]).astype(F32)
     queries, own_kv, first_rounded, attention_weights = project(
         mine, theirs, all_places, inputs, gain_first, bias, cosine, sine, q_width, kv_width
@@ -772,16 +858,15 @@
         taken = jnp.take(vector.reshape(blocks, rows), seq_places, axis=0)
         return relative(taken.T).T
 
-    seg_k, pos_k = key_rows(segments), key_rows(positions)
+    seg_k, pos_k = (key_rows(after(v, own_kv)) for v in (segments, positions))
     seen = pair_mask(
         own_segment[None, :, None], own_place[None, :, None], seg_k[:, None, :], pos_k[:, None, :]
     )
     flags = (jnp.any(seen, axis=(1, 2)).astype(jnp.int32) + jnp.all(seen, axis=(1, 2))).astype(
         jnp.int32
     )
-    pairs = (
-        own_segment[:, None], own_place[:, None], seg_k[:, None, :], pos_k[:, None, :], flags,
-    )
+    codes = (seg_k * SEGMENT_STEP + pos_k)[:, :, None]
+    pairs = (own_segment[None, :], own_place[None, :], codes, flags)
     attended, lse = attend(queries, keys, values, *pairs)
     def reduce_halves(part):
         return part[:half] + y_swap(part[half:].astype(BF16)).astype(F32)
@@ -836,61 +921,52 @@
     )
     residual_back = cot_own[:half].astype(F32) + residual_inner
     back_half = residual_back.astype(BF16)
-    back_other, out_core, up_gradient, down_share = together(
-        y_swap(back_half), dp_swap(after(out_far, back_half), 1), second_gradient(1, back_half),
-        down_share,
+    def exchange_units(*shares):
+        stacks = [mine.reshape(n_dp, share, mine.shape[1]) for mine in shares]
+        pieces = pick_pieces(stacks, dp_slots)
+        return [dp_swap(piece, k) if k else piece for k, piece in enumerate(pieces)]
+
+    out_core = dp_swap(after(out_far, back_half), 1)
+    corner = PlaneScatter(out_near, out_core).summed(3 * half, 4 * half).astype(BF16)
+    back_other, out_core, up_gradient, down_share, corner_x = together(
+        y_swap(back_half), out_core, second_gradient(1, back_half), down_share, dp_swap(corner, 2)
     )
     down = PlaneScatter(out_near, out_core)
     attended_back, attention_back = d_o_of(
         back_half, back_other, attention_weights, qkv_end, q_width
     )
 
-    take = lax.dynamic_index_in_dim
-    core, x = dp % 2, dp // 2
-
     def halves_of(left, right):
-        return gradient_halves(left, right, core.astype(jnp.int32)[None], n_seq, share)
+        return gradient_halves(left, right, core_place, n_seq, share)
 
     def x_halves(own, over_core):
         parts = own.astype(F32) + over_core.astype(F32)
         parts = parts.reshape(n_seq, n_dp // 2, share, own.shape[2])
-        return take(parts, x, 1, keepdims=False), take(parts, 1 - x, 1, keepdims=False).astype(BF16)
+        return take(parts, x, 1), take(parts, 1 - x, 1).astype(BF16)
 
     def place_of(parts, s):
-        return take(parts, seq_places[s % n_seq], 0, keepdims=False)
-
-    def exchange_units(mine):
-        mine = mine.reshape(n_dp, share, mine.shape[1])
-        pieces = []
-        for k in range(n_dp):
-            piece = take(mine, dp_slots[k], 0, keepdims=False)
-            pieces.append(dp_swap(piece, k) if k else piece)
-        return pieces
-
-    first_pieces = exchange_units(after(first_share, back_other))
+        return take(parts, scalars[s % n_seq], 0)
+
     out_own, sent = halves_of(attention_back, attended)
-    out_over_core = dp_swap(sent, 1)
+    sides = down.sides_of(corner_x)
+    over = dp_swap(sides[0], 2), y_swap(sides[1])
+    (out_over_core,) = together(dp_swap(sent, 1))
+    out_own, sent = x_halves(out_own, out_over_core)
+    out_over_x = dp_swap(sent, 2)
+    attended_back, out_sent = together(attended_back, sent)
     query_linear_back, kv_parts = attend_back(
         queries, keys, values, attended_back, lse, cosine, sine, *pairs
     )
-    corner = down.corner()
-    query_linear_back, kv_parts, out_over_core, gate_share, *arrived = together(
-        query_linear_back, kv_parts, out_over_core, gate_share,
-        dp_swap(corner[0], 2), y_swap(corner[1]), *first_pieces,
-    )
-    corners, first_pieces = arrived[:2], arrived[2:]
+    query_linear_back, kv_parts, out_over_x, *over = together(
+        query_linear_back, kv_parts, out_over_x, *over
+    )
 
     kv_moved = [z_shift(kv_parts[s * rows : (s + 1) * rows], -s) for s in range(1, n_seq)]
-    out_own, sent = x_halves(out_own, out_over_core)
-    out_over_x = dp_swap(sent, 2)
     query_own, query_sent = halves_of(first_rounded, query_linear_back)
-    sides = down.sides(*corners)
-    out_over_x, query_own, query_sent, up_gradient, *arrived = together(
-        out_over_x, query_own, query_sent, up_gradient,
-        dp_swap(sides[0], 2), y_swap(sides[1]), *kv_moved,
-    )
-    over, kv_moved = arrived[:2], arrived[2:]
-    out_half = from_inner((residual + down.home(*over)).astype(BF16))
+    query_own, gate_share, query_over_core, *kv_moved = together(
+        query_own, gate_share, dp_swap(query_sent, 1), *kv_moved
+    )
+    *kv_moved, up_gradient = together(*kv_moved, up_gradient)
     out_rows = out_own + out_over_x.astype(F32)
     up_share = sum_along_seq(up_gradient)
     kv_back = kv_parts[:rows].astype(F32)
@@ -902,39 +978,34 @@
     kv_linear_back = jnp.concatenate([key_linear_back, kv_back[:, kv_width:]], axis=1).astype(BF16)
     linear_back = jnp.concatenate([query_linear_back, kv_linear_back], axis=1)
 
-    query_over_core = dp_swap(query_sent, 1)
+    query_own, sent = x_halves(query_own, query_over_core)
+    query_over_x = dp_swap(sent, 2)
     kv_own, sent = halves_of(first_rounded, kv_linear_back)
     kv_over_core = dp_swap(sent, 1)
-    first_theirs = y_swap(right_product(linear_back[half:], qkv_full).astype(BF16))
-    first_mine = right_product(linear_back[:half], qkv_full)
-    bias_terms = jnp.sum(linear_back.astype(F32), axis=0)
-    query_over_core, kv_over_core, out_half = together(query_over_core, kv_over_core, out_half)
-
-    query_own, query_sent = x_halves(query_own, query_over_core)
-    query_over_x = dp_swap(query_sent, 2)
+    first_theirs = y_swap(against(linear_back[half:], attention_weights, BF16))
+    first_mine = against(linear_back[:half], attention_weights, F32)
+    query_over_x, kv_over_core = together(query_over_x, kv_over_core)
+    large = jnp.concatenate([query_own + query_over_x.astype(F32), out_rows], axis=2)
+
     kv_own, sent = x_halves(kv_own, kv_over_core)
     kv_over_x = dp_swap(sent, 2)
+    total = z_shift(place_of(large, 1).astype(BF16), 1)
+    out_half = from_inner((residual + down.home(*over)).astype(BF16))
+    total, kv_over_x, first_theirs, first_mine, out_half = together(
+        total, kv_over_x, first_theirs, first_mine, out_half
+    )
+    kv_rows = kv_own + kv_over_x.astype(F32)
+    total = place_of(large, 2) + total.astype(F32)
+
     out_other = y_swap(out_half)
-    query_over_x, kv_over_x, first_theirs, first_mine, bias_terms = together(
-        query_over_x, kv_over_x, first_theirs, first_mine, bias_terms
-    )
-    large = jnp.concatenate([query_own + query_over_x.astype(F32), out_rows], axis=2)
-    kv_rows = kv_own + kv_over_x.astype(F32)
-
-    total = z_shift(place_of(large, 1).astype(BF16), 1)
-    kv_total = z_shift(place_of(kv_rows, 1).astype(BF16), 1)
     first_back = first_mine + first_theirs.astype(F32)
     first_inverse = inverse_rms(inputs_half)
     input_inner, first_gain_term = norm_backward(
         first_back, inputs_half * first_inverse, first_inverse, gain_first
     )
-    input_half = from_inner((residual_back + input_inner).astype(BF16))
+    input_half = (residual_back + input_inner).astype(BF16)
+    bias_terms = jnp.sum(linear_back.astype(F32), axis=0)
     sums = jnp.concatenate([first_gain_term, second_gain_term, bias_terms])
-    total, kv_total, sums, input_half, out_other = together(
-        total, kv_total, sums, input_half, out_other
-    )
-    total = place_of(large, 2) + total.astype(F32)
-    kv_total = place_of(kv_rows, 2) + kv_total.astype(F32)
 
     def shift_add(values, axis):
         size = lax.axis_size(axis)
@@ -944,33 +1015,36 @@
         ]
         return functools.reduce(jnp.add, moved, values)
 
+    input_half = from_inner(input_half)
     input_other = y_swap(input_half)
-    pieces = [exchange_units(share_of) for share_of in (down_share, gate_share)]
+    pieces = exchange_units(first_share, down_share, gate_share)
+    kv_moved = [z_shift(place_of(kv_rows, s).astype(BF16), -s) for s in range(1, n_seq)]
     for s in range(2, n_seq):
         total = z_shift(total.astype(BF16), 1)
-        kv_total = z_shift(kv_total.astype(BF16), 1)
         if s == 2:
+            total, sums, out_other, up_share, *arrived = together(
+                total, sums, out_other, up_share, *kv_moved, *pieces
+            )
+            kv_moved, pieces = arrived[: n_seq - 1], arrived[n_seq - 1 :]
             sums = shift_add(sums, "dp")
-            total, kv_total, sums, up_share, pieces[0] = together(
-                total, kv_total, sums, up_share, pieces[0]
+            up_pieces = exchange_units(up_share)
+        elif s == 3:
+            total, sums, input_other, *up_pieces = together(
+                total, sums, input_other, *up_pieces
             )
-        elif s == 3:
             sums = shift_add(sums, "seq")
-            total, kv_total, sums, input_other, pieces[1] = together(
-                total, kv_total, sums, input_other, pieces[1]
-            )
         total = place_of(large, s + 1) + total.astype(F32)
-        kv_total = place_of(kv_rows, s + 1) + kv_total.astype(F32)
-    down_pieces, gate_pieces = pieces
-    up_pieces = exchange_units(up_share)
+    kv_share = functools.reduce(
+        lambda a, b: a + b.astype(F32), kv_moved, place_of(kv_rows, 0)
+    )
     gain_terms = shift_add(sums[: 2 * width], "tensor")
     bias_terms = sums[2 * width :]
     input_gradient = relative(jnp.concatenate([input_half, input_other], axis=0))
     output = relative(jnp.concatenate([out_half, out_other], axis=0))
-    large_share, kv_share = total, kv_total
+    large_share = total
     out_gradient = large_share[:, q_width:].T
     gate_gradient, up_gradient, down_gradient = lay_units(
-        cut, first_pieces + gate_pieces + up_pieces + down_pieces, dp_owners
+        cut, pieces + up_pieces, dp_owners
     )
     down_gradient = down_gradient.T
     return (

time: 600 us -> 584 us (0.973)
  Pallas kernels: 190 us -> 209 us
  between operations: 35 us -> 16.1 us
  matrix products: 28.9 us -> 17.9 us
  waiting for transfers between devices: 181 us -> 170 us
  other arithmetic: 41.4 us -> 51.9 us
    ppermute x44 -> x38, starting transfers between devices: 43.7 us -> 21.2 us  [dp_swap(): return lax.ppermute(value, 'dp', [(i, i ^ flip) for i in range(size)])]
    ppermute x15, starting transfers between devices: 19.8 us -> 38.3 us  [z_shift(): lax.ppermute(value, 'seq', [(i, (i + step) % size) for i in range(size)])]
    dot_general x6 -> x2, matrix products: 20.6 us -> 6.01 us  [right_product(): lax.dot_general(left, right, (((1,), (1,)), ((), ())), preferred_element_...]
    reduce_scatter x3, waiting for transfers between devices: 16.8 us -> 3.28 us  [sum_along_seq(): return lax.psum_scatter(gradient, 'seq', scatter_dimension=0, tiled=True)]
    convert_element_type x2 -> x5, other arithmetic: 0.03 us -> 13 us  [the longest x1 3.52 us: sides_of(): return (self.summed(2 * t, 3 * t).astype(BF16), to_y.astype(BF16))]
    ppermute x44 -> x38, waiting for transfers between devices: 62.2 us -> 51.2 us  [dp_swap(): return lax.ppermute(value, 'dp', [(i, i ^ flip) for i in range(size)])]
    pallas_call x1, Pallas kernels: 13.9 us -> 24.7 us  [attend_back(): pl.pallas_call(functools.partial(attend_back_kernel, rows, HEAD_DIM ** (-...]
    ppermute x11 -> x10, waiting for transfers between devices: 36.9 us -> 44.7 us  [y_swap(): return lax.ppermute(value, 'tensor', [(0, 1), (1, 0)])]
  transfers between devices with their start and end apart: 83 -> 76, of which waited for: 25 -> 29; matrix products, arithmetic and copies ran while one was open for 14% -> 14% of each run, Pallas kernels for 32% -> 36%
where the time goes in v3:
time: 584 us; the launch traced here: 576 us
  Pallas kernels  209 us (36%)
  waiting for transfers between devices  170 us (29%)
  starting transfers between devices  78.3 us (13%)
  other arithmetic  51.9 us (9%)
  local copies, waits for them, and re-layouts  32.7 us (6%)
  matrix products  17.9 us (3%)
  between operations  16.1 us (3%)
    pallas_call x4, Pallas kernels, feed(): pl.pallas_call(functools.partial(feed_kernel, columns // 3, earlier is no...  74.5 us
    ppermute x15, waiting for transfers between devices, z_shift(): lax.ppermute(value, 'seq', [(i, (i + step) % size) for i in range(size)])  68.8 us
    pallas_call x4, Pallas kernels, unit_gradients(): pl.pallas_call(kernel, grid=(each * len(which),), in_specs=[held] * len(l...  51.4 us
    ppermute x38, waiting for transfers between devices, dp_swap(): return lax.ppermute(value, 'dp', [(i, i ^ flip) for i in range(size)])  51.2 us
    ppermute x10, waiting for transfers between devices, y_swap(): return lax.ppermute(value, 'tensor', [(0, 1), (1, 0)])  44.7 us
    ppermute x15, starting transfers between devices, z_shift(): lax.ppermute(value, 'seq', [(i, (i + step) % size) for i in range(size)])  38.3 us
    pallas_call x1, Pallas kernels, attend_back(): pl.pallas_call(functools.partial(attend_back_kernel, rows, HEAD_DIM ** (-...  24.7 us
    ppermute x38, starting transfers between devices, dp_swap(): return lax.ppermute(value, 'dp', [(i, i ^ flip) for i in range(size)])  21.2 us
  transfers between devices with their start and end apart: 76, of which 29 were waited for; matrix products, arithmetic and copies ran while one was open for 14% of the time, Pallas kernels for 36%

profile of v3, /device:TPU:0, one launch (start us, length us, event | category | flops | bytes accessed | tf_op | source)
XLA Modules:
  0.0 575.8 jit_solution(8722668894345091501)
XLA Ops:
  8.3 3.0 collective-permute-start.1
  15.8 3.0 fusion.right_ref
  28.7 5.2 convolution_convert_fusion.1.x_ref
  35.2 3.9 collective-permute-done.5.refs_2_
  46.0 7.5 %collective-permute-done.8.refs_6_ = bf16[96,1792]{1,0:T(8,128)(2,1)S(1)} collective-permute-done((bf16[96,1792]{1,0:T(8,128)(2,1)S(1)}, bf16[96,1792]{1,0:T(8,128)(2,1)S(1)}, u32[]{:S(2)}, u32[]{:S(2)}) %collective-permute-start.8) | collective-permute-done | bytes 344096 | tf_op jit(solution)/shard_map/ppermute | solution.py:45
  53.5 4.0 collective-permute-done.7.refs_3_
  57.8 6.7 %convolution_convert_fusion.refs_0_ = bf16[512,1536]{1,0:T(8,128)(2,1)} fusion(bf16[1536,1536]{1,0:T(8,128)(2,1)} %fusion.right_ref, bf16[512,1536]{1,0:T(8,128)(2,1)S(1)} %copy-done.66, bf16[256,1536]{1,0:T(8,128)(2,1)S(1)} %get-tuple-element.379, bf16[256,1536]{1,0:T(8,128)(2,1)S(1)} %get-tuple-element.378, pred[]{:T(512)S(6)} %eq.30), kind=kOutput, calls=%fused_computation.13 | convolution fusion | flops 2420637696 | bytes 9437185 | tf_op jit(solution)/shard_map/dot_general | solution.py:24
  69.1 4.5 collective-permute-done.10.theirs_ref
  75.6 6.0 %shard_map.275 = (bf16[512,768]{1,0:T(8,128)(2,1)S(1)}, bf16[512,256]{1,0:T(8,128)(2,1)S(1)}, bf16[512,1536]{1,0:T(8,128)(2,1)S(1)}, bf16[16,96,1792]{2,1,0:T(8,128)(2,1)}) custom-call(s32[16]{0:T(128)S(1)} %copy-done.48, bf16[8,96,1792]{2,1,0:T(8,128)(2,1)S(1)} %shard_map.274.mine_ref, bf16[8,96,1792]{2,1,0:T(8,128)(2,1)} %collective-permute-done.10.theirs_ref, ...), custom_call_target="tpu_custom_call" | custom-call | tf_op jit(solution)/shard_map/pallas_call | solution.py:389
  84.0 3.8 collective-permute-start.12
  87.8 14.1 %collective-permute-done.13 = bf16[512,256]{1,0:T(8,128)(2,1)S(1)} collective-permute-done((bf16[512,256]{1,0:T(8,128)(2,1)S(1)}, bf16[512,256]{1,0:T(8,128)(2,1)S(1)}, u32[]{:S(2)}, u32[]{:S(2)}) %collective-permute-start.13) | collective-permute-done | bytes 262176 | tf_op jit(solution)/shard_map/ppermute | solution.py:54
  101.9 6.9 %collective-permute-start.11 = (bf16[512,256]{1,0:T(8,128)(2,1)S(1)}, bf16[512,256]{1,0:T(8,128)(2,1)S(1)}, u32[]{:S(2)}, u32[]{:S(2)}) collective-permute-start(bf16[512,256]{1,0:T(8,128)(2,1)S(1)} %get-tuple-element.233), channel_id=1, source_target_pairs={{0,2},{2,4},{4,6},{6,0},{1,3},{3,5},{5,7},{7,1},{8,10},{10,12},{12... | collective-permute-start | bytes 786440 | tf_op jit(solution)/shard_map/ppermute | solution.py:54
  108.8 24.6 %collective-permute-done.12 = bf16[512,256]{1,0:T(8,128)(2,1)S(1)} collective-permute-done((bf16[512,256]{1,0:T(8,128)(2,1)S(1)}, bf16[512,256]{1,0:T(8,128)(2,1)S(1)}, u32[]{:S(2)}, u32[]{:S(2)}) %collective-permute-start.12) | collective-permute-done | bytes 262176 | tf_op jit(solution)/shard_map/ppermute | solution.py:54
  144.5 17.6 %shard_map.276 = (bf16[512,768]{1,0:T(8,128)(2,1)S(1)}, f32[6,1,512]{2,1,0:T(1,128)S(1)}) custom-call(s32[4]{0:T(128)S(1)} %convert_add_fusion.7.flag_ref, bf16[512,768]{1,0:T(8,128)(2,1)S(1)} %copy-done.18, bf16[2048,128]{1,0:T(8,128)(2,1)S(1)} %get-tuple-element.390.k_ref, bf16[2048,128]{1,0:T(8,128)(2,1)S(1)} %get-tuple-element.389.v_ref, ...), custom_call_target="tpu_custom_call" | custom-call | tf_op jit(solution)/shard_map/pallas_call | solution.py:170
  162.2 3.4 convolution_convert_fusion.2
  169.9 15.2 %collective-permute-done.17 = bf16[256,1536]{1,0:T(8,128)(2,1)S(1)} collective-permute-done((bf16[256,1536]{1,0:T(8,128)(2,1)}, bf16[256,1536]{1,0:T(8,128)(2,1)S(1)}, u32[]{:S(2)}, u32[]{:S(2)}) %collective-permute-start.17) | collective-permute-done | bytes 786464 | tf_op jit(solution)/shard_map/ppermute | solution.py:49
  194.5 13.1 %collective-permute-done.20.refs_1_ = bf16[256,1536]{1,0:T(8,128)(2,1)S(1)} collective-permute-done((bf16[256,1536]{1,0:T(8,128)(2,1)S(1)}, bf16[256,1536]{1,0:T(8,128)(2,1)S(1)}, u32[]{:S(2)}, u32[]{:S(2)}) %collective-permute-start.20) | collective-permute-done | bytes 786464 | tf_op jit(solution)/shard_map/ppermute | solution.py:49
  210.2 10.2 %collective-permute-done.23 = bf16[128,1536]{1,0:T(8,128)(2,1)S(1)} collective-permute-done((bf16[128,1536]{1,0:T(8,128)(2,1)S(1)}, bf16[128,1536]{1,0:T(8,128)(2,1)S(1)}, u32[]{:S(2)}, u32[]{:S(2)}) %collective-permute-start.23) | collective-permute-done | bytes 393248 | tf_op jit(solution)/shard_map/ppermute | solution.py:49
  226.9 14.4 %shard_map.280 = (bf16[2048,1152]{1,0:T(8,128)(2,1)}, bf16[1024,1536]{1,0:T(8,128)(2,1)}, bf16[1024,1536]{1,0:T(8,128)(2,1)}) custom-call(bf16[2048,1536]{1,0:T(8,128)(2,1)} %bitcast.102, bf16[2048,1536]{1,0:T(8,128)(2,1)} %bitcast.109, bf16[1536,1152]{1,0:T(8,128)(2,1)} %all-gather.5.cloned.1.call-done.refs_2_), custom_call_target="tpu_custom_call" | custom-call | tf_op jit(solution)/shard_map/pallas_call | solution.py:558
  241.3 14.4 %shard_map.281 = (bf16[2048,1152]{1,0:T(8,128)(2,1)}, bf16[1024,1536]{1,0:T(8,128)(2,1)}, bf16[1024,1536]{1,0:T(8,128)(2,1)}) custom-call(bf16[2048,1536]{1,0:T(8,128)(2,1)} %bitcast.103, bf16[2048,1536]{1,0:T(8,128)(2,1)} %bitcast.110, bf16[1536,1152]{1,0:T(8,128)(2,1)} %all-gather.5.cloned.1.call-done.refs_2_, ...), custom_call_target="tpu_custom_call", output_to_operand_aliasing={{0}: (3, {})} | custom-call | tf_op jit(solution)/shard_map/pallas_call | solution.py:558
  255.7 16.8 %shard_map.282 = bf16[1536,1152]{1,0:T(8,128)(2,1)} custom-call(bf16[2048,1536]{1,0:T(8,128)(2,1)} %bitcast.104, bf16[2048,1536]{1,0:T(8,128)(2,1)} %bitcast.111, bf16[2048,1152]{1,0:T(8,128)(2,1)} %get-tuple-element.256.p_ref), custom_call_target="tpu_custom_call" | custom-call | tf_op jit(solution)/shard_map/pallas_call | solution.py:601
  272.6 22.9 %shard_map.283 = (bf16[2048,2304]{1,0:T(8,128)(2,1)}, bf16[1024,1536]{1,0:T(8,128)(2,1)}, bf16[1024,1536]{1,0:T(8,128)(2,1)}) custom-call(bf16[2048,1536]{1,0:T(8,128)(2,1)} %bitcast.105, bf16[2048,1536]{1,0:T(8,128)(2,1)} %bitcast.112, bf16[1536,2304]{1,0:T(8,128)(2,1)} %all-gather.3.cloned.1.call-done.refs_2_, ...), custom_call_target="tpu_custom_call" | custom-call | tf_op jit(solution)/shard_map/pallas_call | solution.py:558
  295.4 22.8 %shard_map.284 = (bf16[2048,2304]{1,0:T(8,128)(2,1)}, bf16[1024,1536]{1,0:T(8,128)(2,1)}, bf16[1024,1536]{1,0:T(8,128)(2,1)}) custom-call(bf16[2048,1536]{1,0:T(8,128)(2,1)} %bitcast.106, bf16[2048,1536]{1,0:T(8,128)(2,1)} %bitcast.113, bf16[1536,2304]{1,0:T(8,128)(2,1)} %all-gather.3.cloned.1.call-done.refs_2_, ...), custom_call_target="tpu_custom_call", output_to_operand_aliasing={{0}: (5, {})} | custom-call | tf_op jit(solution)/shard_map/pallas_call | solution.py:558
  322.0 11.4 %shard_map.285 = bf16[1536,768]{1,0:T(8,128)(2,1)} custom-call(bf16[2048,1536]{1,0:T(8,128)(2,1)} %bitcast.114, bf16[2048,2304]{1,0:T(8,128)(2,1)} %get-tuple-element.276.p_ref), custom_call_target="tpu_custom_call" | custom-call | flops 4831838208 | tf_op jit(solution)/shard_map/pallas_call | solution.py:601
  339.4 11.8 %shard_map.286 = bf16[1536,768]{1,0:T(8,128)(2,1)} custom-call(bf16[2048,1536]{1,0:T(8,128)(2,1)} %bitcast.107, bf16[2048,2304]{1,0:T(8,128)(2,1)} %get-tuple-element.276.p_ref), custom_call_target="tpu_custom_call" | custom-call | flops 4831838208 | tf_op jit(solution)/shard_map/pallas_call | solution.py:601
  351.2 4.2 collective-permute-done.32
  357.9 3.8 multiply_reduce_fusion
  365.0 5.0 collective-permute-done.35
  372.8 11.4 %shard_map.287 = bf16[1536,768]{1,0:T(8,128)(2,1)} custom-call(bf16[2048,1536]{1,0:T(8,128)(2,1)} %bitcast.108, bf16[2048,2304]{1,0:T(8,128)(2,1)} %get-tuple-element.276.p_ref), custom_call_target="tpu_custom_call" | custom-call | flops 4831838208 | tf_op jit(solution)/shard_map/pallas_call | solution.py:601
  384.2 3.3 reduce-scatter.7.cloned.1.call-done
  387.5 4.9 collective-permute-done.36
  394.9 3.5 shard_map.288
  401.0 3.5 add_convert_fusion.1
  409.8 24.7 %shard_map.290 = (bf16[512,768]{1,0:T(8,128)(2,1)}, bf16[2048,256]{1,0:T(8,128)(2,1)}) custom-call(s32[4]{0:T(128)} %copy-done.45, bf16[512,768]{1,0:T(8,128)(2,1)} %copy-done.17, bf16[2048,128]{1,0:T(8,128)(2,1)} %copy-done.10, bf16[2048,128]{1,0:T(8,128)(2,1)} %copy-done.9, bf16[512,768]{1,0:T(8,128)(2,1)} %copy-done.26, f32[6,1,512]{2,1,0:T(1,128)} %copy-done.44, ...), custom_call_target="tpu_custom_call" | custom-call | tf_op jit(solution)/shard_map/pallas_call | solution.py:277
  434.6 3.2 collective-permute-done.38
  445.6 3.1 collective-permute-start.42
  451.3 4.6 collective-permute-done.44
  455.9 10.3 %collective-permute-done.43 = bf16[512,256]{1,0:T(8,128)(2,1)} collective-permute-done((bf16[512,256]{1,0:T(8,128)(2,1)}, bf16[512,256]{1,0:T(8,128)(2,1)}, u32[]{:S(2)}, u32[]{:S(2)}) %collective-permute-start.43) | collective-permute-done | bytes 262176 | tf_op jit(solution)/shard_map/ppermute | solution.py:54
  475.0 8.1 %collective-permute-done.45 = bf16[4,96,768]{2,1,0:T(8,128)(2,1)S(1)} collective-permute-done((bf16[4,96,768]{2,1,0:T(8,128)(2,1)S(1)}, bf16[4,96,768]{2,1,0:T(8,128)(2,1)S(1)}, u32[]{:S(2)}, u32[]{:S(2)}) %collective-permute-start.45) | collective-permute-done | bytes 589856 | tf_op jit(solution)/shard_map/ppermute | solution.py:45
  484.1 6.2 %collective-permute-start.47 = (bf16[96,1536]{1,0:T(8,128)(2,1)S(1)}, bf16[96,1536]{1,0:T(8,128)(2,1)S(1)}, u32[]{:S(2)}, u32[]{:S(2)}) collective-permute-start(bf16[96,1536]{1,0:T(8,128)(2,1)S(1)} %fusion.40), channel_id=1, source_target_pairs={{0,2},{2,4},{4,6},{6,0},{1,3},{3,5},{5,7},{7,1},{8,10},{10,12},{12... | collective-permute-start | bytes 884744 | tf_op jit(solution)/shard_map/ppermute | solution.py:54
  499.3 5.0 collective-permute-done.47
  509.3 5.1 collective-permute-start.50
  526.1 6.1 %collective-permute-done.54 = bf16[96,256]{1,0:T(8,128)(2,1)S(1)} collective-permute-done((bf16[96,256]{1,0:T(8,128)(2,1)S(1)}, bf16[96,256]{1,0:T(8,128)(2,1)S(1)}, u32[]{:S(2)}, u32[]{:S(2)}) %collective-permute-start.54) | collective-permute-done | bytes 49184 | tf_op jit(solution)/shard_map/ppermute | solution.py:54
  538.0 3.1 maximum_select_fusion.4
  544.9 3.7 collective-permute-done.62
  551.6 3.4 collective-permute-start.68
  556.3 3.0 maximum_select_fusion.5
  560.3 3.2 shard_map.299
  (449 shorter events, 160.3 us)
Async XLA Ops:
  7.2 219.7 %all-gather.5.cloned.1.call-start = ((), (), s32[]{:S(2)}) async-start(), calls=%async_computation.5 | async-start | bytes 4423680 | tf_op jit(solution)/shard_map/all_gather | solution.py:833
  8.3 14.8 %collective-permute-start.1 = (bf16[96,1792]{1,0:T(8,128)(2,1)S(1)}, bf16[96,1792]{1,0:T(8,128)(2,1)S(1)}, u32[]{:S(2)}, u32[]{:S(2)}) collective-permute-start(bf16[96,1792]{1,0:T(8,128)(2,1)S(1)} %pad_maximum_fusion.3.refs_0_), channel_id=1, source_target_pairs={{0,16},{8,24},{16,0},{24,8},{1,17},{9,25},{17,1},{25,9},{2,18},{10... | collective-permute-start | bytes 1032200 | tf_op jit(solution)/shard_map/ppermute | solution.py:45
  23.1 17.2 %collective-permute-start.3 = (bf16[96,1792]{1,0:T(8,128)(2,1)}, bf16[96,1792]{1,0:T(8,128)(2,1)S(1)}, u32[]{:S(2)}, u32[]{:S(2)}) collective-permute-start(bf16[96,1792]{1,0:T(8,128)(2,1)} %collective-permute-done.refs_1_), channel_id=1, source_target_pairs={{0,16},{8,24},{16,0},{24,8},{1,17},{9,25},{17,1},{25,9},{2,18},{10... | collective-permute-start | bytes 1032200 | tf_op jit(solution)/shard_map/ppermute | solution.py:45
  23.7 16.6 %collective-permute-start.2 = (bf16[96,1792]{1,0:T(8,128)(2,1)}, bf16[96,1792]{1,0:T(8,128)(2,1)S(1)}, u32[]{:S(2)}, u32[]{:S(2)}) collective-permute-start(bf16[96,1792]{1,0:T(8,128)(2,1)} %collective-permute-done.refs_1_), channel_id=1, source_target_pairs={{0,2},{2,4},{4,6},{6,0},{1,3},{3,5},{5,7},{7,1},{8,10},{10,12},{12... | collective-permute-start | bytes 1032200 | tf_op jit(solution)/shard_map/ppermute | solution.py:54
  25.2 13.8 %collective-permute-start.5 = (bf16[96,1152]{1,0:T(8,128)(2,1)S(1)}, bf16[96,1152]{1,0:T(8,128)(2,1)S(1)}, u32[]{:S(2)}, u32[]{:S(2)}) collective-permute-start(bf16[96,1152]{1,0:T(8,128)(2,1)S(1)} %get-tuple-element.201), channel_id=1, source_target_pairs={{0,16},{8,24},{16,0},{24,8},{1,17},{9,25},{17,1},{25,9},{2,18},{10... | collective-permute-start | bytes 663560 | tf_op jit(solution)/shard_map/ppermute | solution.py:45
  26.7 13.6 %collective-permute-start.6 = (bf16[96,1152]{1,0:T(8,128)(2,1)S(1)}, bf16[96,1152]{1,0:T(8,128)(2,1)S(1)}, u32[]{:S(2)}, u32[]{:S(2)}) collective-permute-start(bf16[96,1152]{1,0:T(8,128)(2,1)S(1)} %get-tuple-element.202), channel_id=1, source_target_pairs={{0,24},{8,16},{16,8},{24,0},{1,25},{9,17},{17,9},{25,1},{2,26},{10... | collective-permute-start | bytes 663560 | tf_op jit(solution)/shard_map/ppermute | solution.py:45
  43.0 229.6 %all-gather.3.cloned.1.call-start = ((), (), s32[]{:S(2)}) async-start(), calls=%async_computation.4 | async-start | bytes 8847360 | tf_op jit(solution)/shard_map/all_gather | solution.py:852
  44.4 13.0 %collective-permute-start.7 = (bf16[96,1792]{1,0:T(8,128)(2,1)S(1)}, bf16[96,1792]{1,0:T(8,128)(2,1)S(1)}, u32[]{:S(2)}, u32[]{:S(2)}) collective-permute-start(bf16[96,1792]{1,0:T(8,128)(2,1)S(1)} %collective-permute-done.2.refs_2_), channel_id=1, source_target_pairs={{0,2},{2,4},{4,6},{6,0},{1,3},{3,5},{5,7},{7,1},{8,10},{10,12},{12... | collective-permute-start | bytes 1032200 | tf_op jit(solution)/shard_map/ppermute | solution.py:54
  81.6 20.3 %collective-permute-start.13 = (bf16[512,256]{1,0:T(8,128)(2,1)S(1)}, bf16[512,256]{1,0:T(8,128)(2,1)S(1)}, u32[]{:S(2)}, u32[]{:S(2)}) collective-permute-start(bf16[512,256]{1,0:T(8,128)(2,1)S(1)} %get-tuple-element.233), channel_id=1, source_target_pairs={{0,6},{2,0},{4,2},{6,4},{1,7},{3,1},{5,3},{7,5},{8,14},{10,8},{12,... | collective-permute-start | bytes 786440 | tf_op jit(solution)/shard_map/ppermute | solution.py:54
  82.2 51.3 %collective-permute-start.14 = (bf16[96,2304]{1,0:T(8,128)(2,1)S(1)}, bf16[96,2304]{1,0:T(8,128)(2,1)S(1)}, u32[]{:S(2)}, u32[]{:S(2)}) collective-permute-start(bf16[96,2304]{1,0:T(8,128)(2,1)S(1)} %copy-done.54), channel_id=1, source_target_pairs={{0,8},{8,0},{16,24},{24,16},{1,9},{9,1},{17,25},{25,17},{2,10},{10... | collective-permute-start | bytes 1327112 | tf_op jit(solution)/shard_map/ppermute | solution.py:45
  82.2 51.3 %collective-permute-start.15 = (bf16[96,2304]{1,0:T(8,128)(2,1)S(1)}, bf16[96,2304]{1,0:T(8,128)(2,1)S(1)}, u32[]{:S(2)}, u32[]{:S(2)}) collective-permute-start(bf16[96,2304]{1,0:T(8,128)(2,1)S(1)} %copy-done.52), channel_id=1, source_target_pairs={{0,16},{8,24},{16,0},{24,8},{1,17},{9,25},{17,1},{25,9},{2,18},{10... | collective-permute-start | bytes 1327112 | tf_op jit(solution)/shard_map/ppermute | solution.py:45
  83.6 49.9 %collective-permute-start.16 = (bf16[96,2304]{1,0:T(8,128)(2,1)S(1)}, bf16[96,2304]{1,0:T(8,128)(2,1)S(1)}, u32[]{:S(2)}, u32[]{:S(2)}) collective-permute-start(bf16[96,2304]{1,0:T(8,128)(2,1)S(1)} %copy-done.50), channel_id=1, source_target_pairs={{0,24},{8,16},{16,8},{24,0},{1,25},{9,17},{17,9},{25,1},{2,26},{10... | collective-permute-start | bytes 1327112 | tf_op jit(solution)/shard_map/ppermute | solution.py:45
  84.0 49.4 %collective-permute-start.12 = (bf16[512,256]{1,0:T(8,128)(2,1)S(1)}, bf16[512,256]{1,0:T(8,128)(2,1)S(1)}, u32[]{:S(2)}, u32[]{:S(2)}) collective-permute-start(bf16[512,256]{1,0:T(8,128)(2,1)S(1)} %get-tuple-element.233), channel_id=1, source_target_pairs={{0,4},{2,6},{4,0},{6,2},{1,5},{3,7},{5,1},{7,3},{8,12},{10,14},{12... | collective-permute-start | bytes 786440 | tf_op jit(solution)/shard_map/ppermute | solution.py:54
  101.9 31.5 %collective-permute-start.11 = (bf16[512,256]{1,0:T(8,128)(2,1)S(1)}, bf16[512,256]{1,0:T(8,128)(2,1)S(1)}, u32[]{:S(2)}, u32[]{:S(2)}) collective-permute-start(bf16[512,256]{1,0:T(8,128)(2,1)S(1)} %get-tuple-element.233), channel_id=1, source_target_pairs={{0,2},{2,4},{4,6},{6,0},{1,3},{3,5},{5,7},{7,1},{8,10},{10,12},{12... | collective-permute-start | bytes 786440 | tf_op jit(solution)/shard_map/ppermute | solution.py:54
  136.4 214.8 %reduce-scatter.5.cloned.1.call-start = ((), (), s32[]{:S(2)}) async-start(), calls=%async_computation.6 | async-start | bytes 4423680 | tf_op jit(solution)/shard_map/reduce_scatter | solution.py:896
  141.7 43.4 %collective-permute-start.18 = (bf16[512,1536]{1,0:T(8,128)(2,1)}, bf16[512,1536]{1,0:T(8,128)(2,1)}, u32[]{:S(2)}, u32[]{:S(2)}) collective-permute-start(bf16[512,1536]{1,0:T(8,128)(2,1)} %convolution_convert_fusion.refs_0_), channel_id=1, source_target_pairs={{0,16},{8,24},{16,0},{24,8},{1,17},{9,25},{17,1},{25,9},{2,18},{10... | collective-permute-start | bytes 4718600 | tf_op jit(solution)/shard_map/ppermute | solution.py:45
  165.6 19.5 %collective-permute-start.17 = (bf16[256,1536]{1,0:T(8,128)(2,1)}, bf16[256,1536]{1,0:T(8,128)(2,1)S(1)}, u32[]{:S(2)}, u32[]{:S(2)}) collective-permute-start(bf16[256,1536]{1,0:T(8,128)(2,1)} %convolution_convert_fusion.2), channel_id=1, source_target_pairs={{0,1},{1,0},{2,3},{3,2},{4,5},{5,4},{6,7},{7,6},{8,9},{9,8},{10,11... | collective-permute-start | bytes 2359304 | tf_op jit(solution)/shard_map/ppermute | solution.py:49
  167.3 22.0 %collective-permute-start.21 = (bf16[512,1536]{1,0:T(8,128)(2,1)}, bf16[512,1536]{1,0:T(8,128)(2,1)S(1)}, u32[]{:S(2)}, u32[]{:S(2)}) collective-permute-start(bf16[512,1536]{1,0:T(8,128)(2,1)} %convolution_convert_fusion.refs_0_), channel_id=1, source_target_pairs={{0,8},{8,0},{16,24},{24,16},{1,9},{9,1},{17,25},{25,17},{2,10},{10... | collective-permute-start | bytes 4718600 | tf_op jit(solution)/shard_map/ppermute | solution.py:45
  187.5 20.0 %collective-permute-start.20 = (bf16[256,1536]{1,0:T(8,128)(2,1)S(1)}, bf16[256,1536]{1,0:T(8,128)(2,1)S(1)}, u32[]{:S(2)}, u32[]{:S(2)}) collective-permute-start(bf16[256,1536]{1,0:T(8,128)(2,1)S(1)} %multiply_convert_fusion.refs_0_), channel_id=1, source_target_pairs={{0,1},{1,0},{2,3},{3,2},{4,5},{5,4},{6,7},{7,6},{8,9},{9,8},{10,11... | collective-permute-start | bytes 2359304 | tf_op jit(solution)/shard_map/ppermute | solution.py:49
  189.1 19.7 %collective-permute-start.19 = (bf16[256,1536]{1,0:T(8,128)(2,1)S(1)}, bf16[256,1536]{1,0:T(8,128)(2,1)S(1)}, u32[]{:S(2)}, u32[]{:S(2)}) collective-permute-start(bf16[256,1536]{1,0:T(8,128)(2,1)S(1)} %multiply_convert_fusion.refs_0_), channel_id=1, source_target_pairs={{0,16},{8,24},{16,0},{24,8},{1,17},{9,25},{17,1},{25,9},{2,18},{10... | collective-permute-start | bytes 2359304 | tf_op jit(solution)/shard_map/ppermute | solution.py:45
  189.1 21.2 %collective-permute-start.25 = (bf16[256,1536]{1,0:T(8,128)(2,1)S(1)}, bf16[256,1536]{1,0:T(8,128)(2,1)S(1)}, u32[]{:S(2)}, u32[]{:S(2)}) collective-permute-start(bf16[256,1536]{1,0:T(8,128)(2,1)S(1)} %multiply_convert_fusion.refs_0_), channel_id=1, source_target_pairs={{0,8},{8,0},{16,24},{24,16},{1,9},{9,1},{17,25},{25,17},{2,10},{10... | collective-permute-start | bytes 2359304 | tf_op jit(solution)/shard_map/ppermute | solution.py:45
  272.5 115.0 %reduce-scatter.7.cloned.1.call-start = ((), (), s32[]{:S(2)}) async-start(), calls=%async_computation.7 | async-start | bytes 2949120 | tf_op jit(solution)/shard_map/reduce_scatter | solution.py:904
  295.4 22.8 %collective-permute-start.29 = (bf16[1024,1536]{1,0:T(8,128)(2,1)}, bf16[1024,1536]{1,0:T(8,128)(2,1)S(1)}, u32[]{:S(2)}, u32[]{:S(2)}) collective-permute-start(bf16[1024,1536]{1,0:T(8,128)(2,1)} %get-tuple-element.260), channel_id=1, source_target_pairs={{0,8},{8,0},{16,24},{24,16},{1,9},{9,1},{17,25},{25,17},{2,10},{10... | collective-permute-start | bytes 9437192 | tf_op jit(solution)/shard_map/ppermute | solution.py:45
  320.3 13.1 %collective-permute-start.30 = (bf16[128,1536]{1,0:T(8,128)(2,1)S(1)}, bf16[128,1536]{1,0:T(8,128)(2,1)S(1)}, u32[]{:S(2)}, u32[]{:S(2)}) collective-permute-start(bf16[128,1536]{1,0:T(8,128)(2,1)S(1)} %get-tuple-element.392), channel_id=1, source_target_pairs={{0,16},{8,24},{16,0},{24,8},{1,17},{9,25},{17,1},{25,9},{2,18},{10... | collective-permute-start | bytes 1179656 | tf_op jit(solution)/shard_map/ppermute | solution.py:45
  335.9 19.5 %collective-permute-start.32 = (bf16[256,1536]{1,0:T(8,128)(2,1)S(1)}, bf16[256,1536]{1,0:T(8,128)(2,1)}, u32[]{:S(2)}, u32[]{:S(2)}) collective-permute-start(bf16[256,1536]{1,0:T(8,128)(2,1)S(1)} %pad_maximum_fusion.1), channel_id=1, source_target_pairs={{0,16},{8,24},{16,0},{24,8},{1,17},{9,25},{17,1},{25,9},{2,18},{10... | collective-permute-start | bytes 2359304 | tf_op jit(solution)/shard_map/ppermute | solution.py:45
  338.7 19.3 %collective-permute-start.33 = (bf16[256,1536]{1,0:T(8,128)(2,1)}, bf16[256,1536]{1,0:T(8,128)(2,1)}, u32[]{:S(2)}, u32[]{:S(2)}) collective-permute-start(bf16[256,1536]{1,0:T(8,128)(2,1)} %pad_maximum_fusion.2), channel_id=1, source_target_pairs={{0,1},{1,0},{2,3},{3,2},{4,5},{5,4},{6,7},{7,6},{8,9},{9,8},{10,11... | collective-permute-start | bytes 2359304 | tf_op jit(solution)/shard_map/ppermute | solution.py:49
  339.4 111.9 %reduce-scatter.9.cloned.1.call-start = ((), (), s32[]{:S(2)}) async-start(), calls=%async_computation.8 | async-start | bytes 2949120 | tf_op jit(solution)/shard_map/reduce_scatter | solution.py:904
  364.0 20.2 %collective-permute-start.34 = (bf16[256,1536]{1,0:T(8,128)(2,1)S(1)}, bf16[256,1536]{1,0:T(8,128)(2,1)}, u32[]{:S(2)}, u32[]{:S(2)}) collective-permute-start(bf16[256,1536]{1,0:T(8,128)(2,1)S(1)} %fusion.78.own_ref), channel_id=1, source_target_pairs={{0,1},{1,0},{2,3},{3,2},{4,5},{5,4},{6,7},{7,6},{8,9},{9,8},{10,11... | collective-permute-start | bytes 2359304 | tf_op jit(solution)/shard_map/ppermute | solution.py:49
  364.9 168.7 %reduce-scatter.11.cloned.1.call-start = ((), (), s32[]{:S(2)}) async-start(), calls=%async_computation.9 | async-start | bytes 2949120 | tf_op jit(solution)/shard_map/reduce_scatter | solution.py:904
  372.4 19.9 %collective-permute-start.36 = (bf16[256,1536]{1,0:T(8,128)(2,1)}, bf16[256,1536]{1,0:T(8,128)(2,1)}, u32[]{:S(2)}, u32[]{:S(2)}) collective-permute-start(bf16[256,1536]{1,0:T(8,128)(2,1)} %add_convert_fusion.3), channel_id=1, source_target_pairs={{0,16},{8,24},{16,0},{24,8},{1,17},{9,25},{17,1},{25,9},{2,18},{10... | collective-permute-start | bytes 2359304 | tf_op jit(solution)/shard_map/ppermute | solution.py:45
  404.5 30.0 %collective-permute-start.40 = (bf16[256,1536]{1,0:T(8,128)(2,1)}, bf16[256,1536]{1,0:T(8,128)(2,1)S(1)}, u32[]{:S(2)}, u32[]{:S(2)}) collective-permute-start(bf16[256,1536]{1,0:T(8,128)(2,1)} %get-tuple-element.371), channel_id=1, source_target_pairs={{0,1},{1,0},{2,3},{3,2},{4,5},{5,4},{6,7},{7,6},{8,9},{9,8},{10,11... | collective-permute-start | bytes 2359304 | tf_op jit(solution)/shard_map/ppermute | solution.py:49
  405.3 29.2 %collective-permute-start.39 = (bf16[256,1536]{1,0:T(8,128)(2,1)S(1)}, bf16[256,1536]{1,0:T(8,128)(2,1)S(1)}, u32[]{:S(2)}, u32[]{:S(2)}) collective-permute-start(bf16[256,1536]{1,0:T(8,128)(2,1)S(1)} %get-tuple-element.372), channel_id=1, source_target_pairs={{0,16},{8,24},{16,0},{24,8},{1,17},{9,25},{17,1},{25,9},{2,18},{10... | collective-permute-start | bytes 2359304 | tf_op jit(solution)/shard_map/ppermute | solution.py:45
  408.1 29.7 %collective-permute-start.38 = (bf16[4,96,768]{2,1,0:T(8,128)(2,1)}, bf16[4,96,768]{2,1,0:T(8,128)(2,1)}, u32[]{:S(2)}, u32[]{:S(2)}) collective-permute-start(bf16[4,96,768]{2,1,0:T(8,128)(2,1)} %fusion.23), channel_id=1, source_target_pairs={{0,16},{8,24},{16,0},{24,8},{1,17},{9,25},{17,1},{25,9},{2,18},{10... | collective-permute-start | bytes 1769480 | tf_op jit(solution)/shard_map/ppermute | solution.py:45
  442.5 23.7 %collective-permute-start.41 = (bf16[4,192,768]{2,1,0:T(8,128)(2,1)}, bf16[4,192,768]{2,1,0:T(8,128)(2,1)}, u32[]{:S(2)}, u32[]{:S(2)}) collective-permute-start(bf16[4,192,768]{2,1,0:T(8,128)(2,1)} %get-tuple-element.294), channel_id=1, source_target_pairs={{0,8},{8,0},{16,24},{24,16},{1,9},{9,1},{17,25},{25,17},{2,10},{10... | collective-permute-start | bytes 3538952 | tf_op jit(solution)/shard_map/ppermute | solution.py:45
  444.7 21.6 %collective-permute-start.43 = (bf16[512,256]{1,0:T(8,128)(2,1)}, bf16[512,256]{1,0:T(8,128)(2,1)}, u32[]{:S(2)}, u32[]{:S(2)}) collective-permute-start(bf16[512,256]{1,0:T(8,128)(2,1)} %get-tuple-element.387), channel_id=1, source_target_pairs={{0,4},{2,6},{4,0},{6,2},{1,5},{3,7},{5,1},{7,3},{8,12},{10,14},{12... | collective-permute-start | bytes 786440 | tf_op jit(solution)/shard_map/ppermute | solution.py:54
  445.6 20.6 %collective-permute-start.42 = (bf16[512,256]{1,0:T(8,128)(2,1)}, bf16[512,256]{1,0:T(8,128)(2,1)}, u32[]{:S(2)}, u32[]{:S(2)}) collective-permute-start(bf16[512,256]{1,0:T(8,128)(2,1)} %get-tuple-element.388), channel_id=1, source_target_pairs={{0,6},{2,0},{4,2},{6,4},{1,7},{3,1},{5,3},{7,5},{8,14},{10,8},{12,... | collective-permute-start | bytes 786440 | tf_op jit(solution)/shard_map/ppermute | solution.py:54
  468.4 14.6 %collective-permute-start.45 = (bf16[4,96,768]{2,1,0:T(8,128)(2,1)S(1)}, bf16[4,96,768]{2,1,0:T(8,128)(2,1)S(1)}, u32[]{:S(2)}, u32[]{:S(2)}) collective-permute-start(bf16[4,96,768]{2,1,0:T(8,128)(2,1)S(1)} %fusion.24), channel_id=1, source_target_pairs={{0,16},{8,24},{16,0},{24,8},{1,17},{9,25},{17,1},{25,9},{2,18},{10... | collective-permute-start | bytes 1769480 | tf_op jit(solution)/shard_map/ppermute | solution.py:45
  473.7 25.5 %collective-permute-start.49 = (bf16[256,1536]{1,0:T(8,128)(2,1)S(1)}, bf16[256,1536]{1,0:T(8,128)(2,1)S(1)}, u32[]{:S(2)}, u32[]{:S(2)}) collective-permute-start(bf16[256,1536]{1,0:T(8,128)(2,1)S(1)} %shard_map.293), channel_id=1, source_target_pairs={{0,1},{1,0},{2,3},{3,2},{4,5},{5,4},{6,7},{7,6},{8,9},{9,8},{10,11... | collective-permute-start | bytes 2359304 | tf_op jit(solution)/shard_map/ppermute | solution.py:49
  484.1 20.2 %collective-permute-start.47 = (bf16[96,1536]{1,0:T(8,128)(2,1)S(1)}, bf16[96,1536]{1,0:T(8,128)(2,1)S(1)}, u32[]{:S(2)}, u32[]{:S(2)}) collective-permute-start(bf16[96,1536]{1,0:T(8,128)(2,1)S(1)} %fusion.40), channel_id=1, source_target_pairs={{0,2},{2,4},{4,6},{6,0},{1,3},{3,5},{5,7},{7,1},{8,10},{10,12},{12... | collective-permute-start | bytes 884744 | tf_op jit(solution)/shard_map/ppermute | solution.py:54
  495.5 21.0 %collective-permute-start.55 = (bf16[96,2688]{1,0:T(8,128)(2,1)S(1)}, bf16[96,2688]{1,0:T(8,128)(2,1)S(1)}, u32[]{:S(2)}, u32[]{:S(2)}) collective-permute-start(bf16[96,2688]{1,0:T(8,128)(2,1)S(1)} %get-tuple-element.325), channel_id=1, source_target_pairs={{0,8},{8,0},{16,24},{24,16},{1,9},{9,1},{17,25},{25,17},{2,10},{10... | collective-permute-start | bytes 1548296 | tf_op jit(solution)/shard_map/ppermute | solution.py:45
  495.5 23.7 %collective-permute-start.56 = (bf16[96,2688]{1,0:T(8,128)(2,1)S(1)}, bf16[96,2688]{1,0:T(8,128)(2,1)S(1)}, u32[]{:S(2)}, u32[]{:S(2)}) collective-permute-start(bf16[96,2688]{1,0:T(8,128)(2,1)S(1)} %get-tuple-element.326), channel_id=1, source_target_pairs={{0,16},{8,24},{16,0},{24,8},{1,17},{9,25},{17,1},{25,9},{2,18},{10... | collective-permute-start | bytes 1548296 | tf_op jit(solution)/shard_map/ppermute | solution.py:45
  499.1 21.4 %collective-permute-start.57 = (bf16[96,2688]{1,0:T(8,128)(2,1)S(1)}, bf16[96,2688]{1,0:T(8,128)(2,1)S(1)}, u32[]{:S(2)}, u32[]{:S(2)}) collective-permute-start(bf16[96,2688]{1,0:T(8,128)(2,1)S(1)} %get-tuple-element.327), channel_id=1, source_target_pairs={{0,24},{8,16},{16,8},{24,0},{1,25},{9,17},{17,9},{25,1},{2,26},{10... | collective-permute-start | bytes 1548296 | tf_op jit(solution)/shard_map/ppermute | solution.py:45
  504.3 29.3 %collective-permute-start.51 = (bf16[256,1536]{1,0:T(8,128)(2,1)S(1)}, bf16[256,1536]{1,0:T(8,128)(2,1)}, u32[]{:S(2)}, u32[]{:S(2)}) collective-permute-start(bf16[256,1536]{1,0:T(8,128)(2,1)S(1)} %shard_map.295), channel_id=1, source_target_pairs={{0,1},{1,0},{2,3},{3,2},{4,5},{5,4},{6,7},{7,6},{8,9},{9,8},{10,11... | collective-permute-start | bytes 2359304 | tf_op jit(solution)/shard_map/ppermute | solution.py:49
  509.3 24.3 %collective-permute-start.50 = (bf16[96,1536]{1,0:T(8,128)(2,1)S(1)}, bf16[96,1536]{1,0:T(8,128)(2,1)S(1)}, u32[]{:S(2)}, u32[]{:S(2)}) collective-permute-start(bf16[96,1536]{1,0:T(8,128)(2,1)S(1)} %fusion.33), channel_id=1, source_target_pairs={{0,2},{2,4},{4,6},{6,0},{1,3},{3,5},{5,7},{7,1},{8,10},{10,12},{12... | collective-permute-start | bytes 884744 | tf_op jit(solution)/shard_map/ppermute | solution.py:54
  516.4 15.7 %collective-permute-start.54 = (bf16[96,256]{1,0:T(8,128)(2,1)S(1)}, bf16[96,256]{1,0:T(8,128)(2,1)S(1)}, u32[]{:S(2)}, u32[]{:S(2)}) collective-permute-start(bf16[96,256]{1,0:T(8,128)(2,1)S(1)} %get-tuple-element.395), channel_id=1, source_target_pairs={{0,2},{2,4},{4,6},{6,0},{1,3},{3,5},{5,7},{7,1},{8,10},{10,12},{12... | collective-permute-start | bytes 147464 | tf_op jit(solution)/shard_map/ppermute | solution.py:54
  519.3 14.3 %collective-permute-start.53 = (bf16[96,256]{1,0:T(8,128)(2,1)S(1)}, bf16[96,256]{1,0:T(8,128)(2,1)S(1)}, u32[]{:S(2)}, u32[]{:S(2)}) collective-permute-start(bf16[96,256]{1,0:T(8,128)(2,1)S(1)} %get-tuple-element.396), channel_id=1, source_target_pairs={{0,4},{2,6},{4,0},{6,2},{1,5},{3,7},{5,1},{7,3},{8,12},{10,14},{12... | collective-permute-start | bytes 147464 | tf_op jit(solution)/shard_map/ppermute | solution.py:54
  532.1 16.5 %collective-permute-start.62 = (bf16[256,1536]{1,0:T(8,128)(2,1)S(1)}, bf16[256,1536]{1,0:T(8,128)(2,1)}, u32[]{:S(2)}, u32[]{:S(2)}) collective-permute-start(bf16[256,1536]{1,0:T(8,128)(2,1)S(1)} %shard_map.297), channel_id=1, source_target_pairs={{0,1},{1,0},{2,3},{3,2},{4,5},{5,4},{6,7},{7,6},{8,9},{9,8},{10,11... | collective-permute-start | bytes 2359304 | tf_op jit(solution)/shard_map/ppermute | solution.py:49
  537.2 14.4 %collective-permute-start.58 = (bf16[96,1536]{1,0:T(8,128)(2,1)S(1)}, bf16[96,1536]{1,0:T(8,128)(2,1)S(1)}, u32[]{:S(2)}, u32[]{:S(2)}) collective-permute-start(bf16[96,1536]{1,0:T(8,128)(2,1)S(1)} %fusion.37), channel_id=1, source_target_pairs={{0,2},{2,4},{4,6},{6,0},{1,3},{3,5},{5,7},{7,1},{8,10},{10,12},{12... | collective-permute-start | bytes 884744 | tf_op jit(solution)/shard_map/ppermute | solution.py:54
  (120 other events, 1202.6 us)
Sparse Core Ops, SparseCore 0:
  43.1 93.5 all-gather.4
  138.3 127.1 all-gather.2
  272.6 64.3 reduce-scatter.4
  339.5 47.9 reduce-scatter.6
  389.6 47.5 reduce-scatter.8
  466.4 62.4 reduce-scatter.10

commit v4 on v3

--- a/solution.py
+++ b/solution.py
@@ -78,6 +78,24 @@
         compiler_params=pltpu.CompilerParams(vmem_limit_bytes=24 * MIB),
         cost_estimate=FREE,
     )(places, *pieces)
+
+
+def join_kernel(place_ref, own_ref, other_ref, out_ref):
+    half = own_ref.shape[0]
+    for ref, place in ((own_ref, place_ref[0]), (other_ref, 1 - place_ref[0])):
+        out_ref[pl.ds(pl.multiple_of(place * half, half), half), :] = ref[...]
+
+
+def join_halves(own, other, place):
+    vmem = pl.BlockSpec(memory_space=pltpu.VMEM)
+    return pl.pallas_call(
+        join_kernel,
+        out_shape=jax.ShapeDtypeStruct((2 * own.shape[0], own.shape[1]), own.dtype),
+        in_specs=[pl.BlockSpec(memory_space=pltpu.SMEM), vmem, vmem],
+        out_specs=vmem,
+        compiler_params=pltpu.CompilerParams(vmem_limit_bytes=24 * MIB),
+        cost_estimate=FREE,
+    )(place, own, other)
 
 
 def pick_kernel(count, place_ref, *refs):
@@ -426,19 +444,26 @@
 
 
 def cut_kernel(cut, place_ref, *refs):
-    weights, outs = refs[:3], refs[3:]
     n_dp = cut.n_dp
-    for part in range(2):
-        main, width = cut.main[part], cut.width[part]
-        for k in range(n_dp):
-            owner = place_ref[k]
-            out = outs[part * n_dp + k]
-            for i, w in enumerate(weights):
+    sources, outs, (scratch, sems) = refs[:3], refs[3 : 3 + 2 * n_dp], refs[3 + 2 * n_dp :]
+    copies = [
+        pltpu.make_async_copy(source, scratch.at[i], sems.at[i])
+        for i, source in enumerate(sources)
+    ]
+    for copy in copies:
+        copy.start()
+    for i, copy in enumerate(copies):
+        copy.wait()
+        for part in range(2):
+            main, width = cut.main[part], cut.width[part]
+            for k in range(n_dp):
+                owner = place_ref[k]
+                out = outs[part * n_dp + k]
                 at = i * width
                 low = pl.multiple_of(cut.start[part] + owner * main, 128)
-                out[:, at : at + main] = w[:, pl.ds(low, main)]
+                out[:, at : at + main] = scratch[i, :, pl.ds(low, main)]
                 if part == 1 and cut.rest:
-                    tail = w[:, cut.rest_at :]
+                    tail = scratch[i, :, cut.rest_at :]
                     rest = pick(
                         [tail[:, b * cut.rest : (b + 1) * cut.rest] for b in range(n_dp)], owner
                     )
@@ -456,8 +481,13 @@
             for part in range(2)
             for _ in range(cut.n_dp)
         ],
-        in_specs=[pl.BlockSpec(memory_space=pltpu.SMEM)] + [vmem] * 3,
+        in_specs=[pl.BlockSpec(memory_space=pltpu.SMEM)]
+        + [pl.BlockSpec(memory_space=pl.ANY)] * 3,
         out_specs=[vmem] * (2 * cut.n_dp),
+        scratch_shapes=[
+            pltpu.VMEM((3,) + weights[0].shape, BF16),
+            pltpu.SemaphoreType.DMA((3,)),
+        ],
         compiler_params=pltpu.CompilerParams(vmem_limit_bytes=24 * MIB),
         cost_estimate=FREE,
     )(owners, *weights)
@@ -510,12 +540,10 @@
 def feed_kernel(count, sums, *refs):
     t_ref, c_ref, w_ref = refs[:3]
     p_ref, back_ref, out_ref = refs[-3:]
-    gate_weight, up_weight, down_weight = (
-        w_ref.at[:, i * count : (i + 1) * count] for i in range(3)
-    )
-    tokens = t_ref[...]
-    gate = product(tokens, gate_weight[...])
-    upper = product(tokens, up_weight[...])
+    pair_weights = w_ref.at[:, : 2 * count]
+    down_weight = w_ref.at[:, 2 * count :]
+    pair = product(t_ref[...], pair_weights[...])
+    gate, upper = pair[:, :count], pair[:, count:]
     act_back = product(c_ref[...], down_weight[...])
     sigma = 1.0 / (1.0 + jnp.exp(-gate))
     swish = gate * sigma
@@ -524,7 +552,7 @@
     upper_back = (act_back * swish).astype(BF16)
     for i, value in enumerate((gate_back, upper_back, activated)):
         p_ref[:, i * count : (i + 1) * count] = value
-    back = right_product(gate_back, gate_weight[...]) + right_product(upper_back, up_weight[...])
+    back = right_product(p_ref[:, : 2 * count], pair_weights[...])
     out = right_product(activated, down_weight[...])
     if sums:
         back = back + refs[3][...].astype(F32)
@@ -752,8 +780,9 @@
     flips = jnp.repeat(np.array([0, 2, 1, 3], np.int32), n_seq)
     all_places = jnp.tile(seq_places, 4) * n_dp + slots_of(dp ^ flips)
     core, x = (dp % 2).astype(jnp.int32), (dp // 2).astype(jnp.int32)
-    dp_owners, dp_slots, seq_places, all_places, core_place, core, x, *scalars = together(
-        dp_owners, dp_slots, seq_places, all_places, core[None], core, x,
+    tensor_place = tensor.astype(jnp.int32)[None]
+    dp_owners, dp_slots, seq_places, all_places, core_place, tensor_place, core, x, *scalars = together(
+        dp_owners, dp_slots, seq_places, all_places, core[None], tensor_place, core, x,
         *[seq_places[s] for s in range(n_seq)],
     )
 
@@ -775,17 +804,17 @@
     owner, place = index // (share * n_seq), index // share % n_seq
     slot = owner % 2 * (n_dp // 2) + owner // 2
     inner_of = (place * n_dp + slot) * share + index % share
-    (shuffle,) = together((inner_of[:, None] == index[None, :]).astype(BF16))
+    shuffles = []
 
     def relative(values):
         turned = jnp.concatenate([values[half:], values[:half]], axis=0)
         return jnp.where(tensor == 0, values, turned)
 
     def to_inner(values):
-        return product(relative(values), shuffle).astype(BF16)
+        return product(relative(values), shuffles[0]).astype(BF16)
 
     def from_inner(values):
-        return against(values, shuffle, BF16)
+        return against(values, shuffles[0], BF16)
 
     gain_first, gain_second = vector_in(first_gain), vector_in(second_gain)
 
@@ -823,6 +852,8 @@
             first_parts, second_parts = parts[:n_dp], parts[n_dp:]
         elif s == 1:
             first_parts = spread(first_parts)
+            inner = after(inner_of, line[s])
+            shuffles.extend(together((inner[:, None] == index[None, :]).astype(BF16)))
             inputs = to_inner(after(hidden, line[s]))
             cosine, sine = tables(after(own_place, line[s]))
             moved, over_x[s], inputs, cosine, sine, *first_parts = together(
@@ -847,26 +878,26 @@
     qkv_full, out_full = attention_weights[:, :qkv_end], attention_weights[:, qkv_end:]
     group_kv = [own_kv] + [z_shift(own_kv, s) for s in range(1, n_seq)]
     second_parts = spread([after(part, own_kv) for part in second_parts])
-    *group_kv, cot_own, second_parts = together(*group_kv, cot_own, second_parts)
+    def key_rows(vector):
+        taken = jnp.take(vector.reshape(blocks, rows), seq_places, axis=0)
+        return relative(taken.T).T
+
+    seg_k, pos_k = (key_rows(after(v, own_kv)) for v in (segments, positions))
+    seen = pair_mask(
+        own_segment[None, :, None], own_place[None, :, None], seg_k[:, None, :], pos_k[:, None, :]
+    )
+    flags = (jnp.any(seen, axis=(1, 2)).astype(jnp.int32) + jnp.all(seen, axis=(1, 2))).astype(
+        jnp.int32
+    )
+    codes = (seg_k * SEGMENT_STEP + pos_k)[:, :, None]
+    pairs = (own_segment[None, :], own_place[None, :], codes, flags)
+    *group_kv, cot_own, second_parts, pairs = together(*group_kv, cot_own, second_parts, pairs)
     second_stacked = stack_units(second_parts)
     second_units = lax.all_gather(second_stacked, "seq", axis=0, tiled=True)
     cot_x = dp_swap(cot_own, 2)
     group_kv = jnp.concatenate(group_kv, axis=0)
     keys, values = group_kv[:, :kv_width], group_kv[:, kv_width:]
 
-    def key_rows(vector):
-        taken = jnp.take(vector.reshape(blocks, rows), seq_places, axis=0)
-        return relative(taken.T).T
-
-    seg_k, pos_k = (key_rows(after(v, own_kv)) for v in (segments, positions))
-    seen = pair_mask(
-        own_segment[None, :, None], own_place[None, :, None], seg_k[:, None, :], pos_k[:, None, :]
-    )
-    flags = (jnp.any(seen, axis=(1, 2)).astype(jnp.int32) + jnp.all(seen, axis=(1, 2))).astype(
-        jnp.int32
-    )
-    codes = (seg_k * SEGMENT_STEP + pos_k)[:, :, None]
-    pairs = (own_segment[None, :], own_place[None, :], codes, flags)
     attended, lse = attend(queries, keys, values, *pairs)
     def reduce_halves(part):
         return part[:half] + y_swap(part[half:].astype(BF16)).astype(F32)
@@ -1019,6 +1050,7 @@
     input_other = y_swap(input_half)
     pieces = exchange_units(first_share, down_share, gate_share)
     kv_moved = [z_shift(place_of(kv_rows, s).astype(BF16), -s) for s in range(1, n_seq)]
+    sums = shift_add(sums, "dp")
     for s in range(2, n_seq):
         total = z_shift(total.astype(BF16), 1)
         if s == 2:
@@ -1026,21 +1058,20 @@
                 total, sums, out_other, up_share, *kv_moved, *pieces
             )
             kv_moved, pieces = arrived[: n_seq - 1], arrived[n_seq - 1 :]
-            sums = shift_add(sums, "dp")
             up_pieces = exchange_units(up_share)
+            sums = shift_add(sums, "seq")
         elif s == 3:
             total, sums, input_other, *up_pieces = together(
                 total, sums, input_other, *up_pieces
             )
-            sums = shift_add(sums, "seq")
         total = place_of(large, s + 1) + total.astype(F32)
     kv_share = functools.reduce(
         lambda a, b: a + b.astype(F32), kv_moved, place_of(kv_rows, 0)
     )
     gain_terms = shift_add(sums[: 2 * width], "tensor")
     bias_terms = sums[2 * width :]
-    input_gradient = relative(jnp.concatenate([input_half, input_other], axis=0))
-    output = relative(jnp.concatenate([out_half, out_other], axis=0))
+    input_gradient = join_halves(input_half, input_other, tensor_place)
+    output = join_halves(out_half, out_other, tensor_place)
     large_share = total
     out_gradient = large_share[:, q_width:].T
     gate_gradient, up_gradient, down_gradient = lay_units(

time: 584 us -> 584 us (level)
  local copies, waits for them, and re-layouts: 32.7 us -> 48.3 us
    ppermute x10, waiting for transfers between devices: 44.7 us -> 29.1 us  [y_swap(): return lax.ppermute(value, 'tensor', [(0, 1), (1, 0)])]
    ppermute x15, starting transfers between devices: 38.3 us -> 23.9 us  [z_shift(): lax.ppermute(value, 'seq', [(i, (i + step) % size) for i in range(size)])]
    unnamed x188 -> x220, local copies, waits for them, and re-layouts: 16.7 us -> 29.1 us
    ppermute x38, starting transfers between devices: 21.2 us -> 32.7 us  [dp_swap(): return lax.ppermute(value, 'dp', [(i, i ^ flip) for i in range(size)])]
    ppermute x38, waiting for transfers between devices: 51.2 us -> 62.4 us  [dp_swap(): return lax.ppermute(value, 'dp', [(i, i ^ flip) for i in range(size)])]
  transfers between devices with their start and end apart: 76 -> 76, of which waited for: 29 -> 32; matrix products, arithmetic and copies ran while one was open for 14% -> 14% of each run, Pallas kernels for 36% -> 36%
where the time goes in v4:
time: 584 us; the launch traced here: 575 us
  Pallas kernels  207 us (35%)
  waiting for transfers between devices  165 us (28%)
  starting transfers between devices  74.2 us (13%)
  local copies, waits for them, and re-layouts  48.3 us (8%)
  other arithmetic  47.7 us (8%)
  matrix products  16.8 us (3%)
  between operations  16 us (3%)
    pallas_call x4, Pallas kernels, feed(): pl.pallas_call(functools.partial(feed_kernel, columns // 3, earlier is no...  70.1 us
    ppermute x15, waiting for transfers between devices, z_shift(): lax.ppermute(value, 'seq', [(i, (i + step) % size) for i in range(size)])  67.4 us
    ppermute x38, waiting for transfers between devices, dp_swap(): return lax.ppermute(value, 'dp', [(i, i ^ flip) for i in range(size)])  62.4 us
    pallas_call x4, Pallas kernels, unit_gradients(): pl.pallas_call(kernel, grid=(each * len(which),), in_specs=[held] * len(l...  51 us
    ppermute x38, starting transfers between devices, dp_swap(): return lax.ppermute(value, 'dp', [(i, i ^ flip) for i in range(size)])  32.7 us
    unnamed x220, local copies, waits for them, and re-layouts  29.1 us
    ppermute x10, waiting for transfers between devices, y_swap(): return lax.ppermute(value, 'tensor', [(0, 1), (1, 0)])  29.1 us
    pallas_call x1, Pallas kernels, attend_back(): pl.pallas_call(functools.partial(attend_back_kernel, rows, HEAD_DIM ** (-...  24.4 us
  transfers between devices with their start and end apart: 76, of which 32 were waited for; matrix products, arithmetic and copies ran while one was open for 14% of the time, Pallas kernels for 36%

profile of v4, /device:TPU:0, one launch (start us, length us, event | category | flops | bytes accessed | tf_op | source)
XLA Modules:
  0.0 575.1 jit_solution(8895607200656985020)
XLA Ops:
  8.3 3.0 collective-permute-start.1
  30.6 4.3 convolution_convert_fusion.1.x_ref
  36.2 5.2 collective-permute-done.5.refs_2_
  49.0 4.8 collective-permute-done.8.refs_6_
  53.7 3.2 collective-permute-done.7.refs_3_
  59.5 6.6 %convolution_convert_fusion.refs_0_ = bf16[512,1536]{1,0:T(8,128)(2,1)} fusion(bf16[1536,1536]{1,0:T(8,128)(2,1)} %copy-done.3, bf16[512,1536]{1,0:T(8,128)(2,1)S(1)} %copy-done.76, bf16[256,1536]{1,0:T(8,128)(2,1)S(1)} %get-tuple-element.392, bf16[256,1536]{1,0:T(8,128)(2,1)S(1)} %get-tuple-element.391, pred[]{:T(512)S(6)} %eq.52), kind=kOutput, calls=%fused_computation.13 | convolution fusion | flops 2420637696 | bytes 9437185 | tf_op jit(solution)/shard_map/dot_general | solution.py:24
  75.8 6.0 %shard_map.275 = (bf16[512,768]{1,0:T(8,128)(2,1)S(1)}, bf16[512,256]{1,0:T(8,128)(2,1)S(1)}, bf16[512,1536]{1,0:T(8,128)(2,1)S(1)}, bf16[16,96,1792]{2,1,0:T(8,128)(2,1)}) custom-call(s32[16]{0:T(128)S(1)} %copy-done.60, bf16[8,96,1792]{2,1,0:T(8,128)(2,1)S(1)} %shard_map.274.mine_ref, bf16[8,96,1792]{2,1,0:T(8,128)(2,1)} %collective-permute-done.10.theirs_ref, ...), custom_call_target="tpu_custom_call" | custom-call | tf_op jit(solution)/shard_map/pallas_call | solution.py:407
  91.9 11.4 %collective-permute-done.13 = bf16[512,256]{1,0:T(8,128)(2,1)S(1)} collective-permute-done((bf16[512,256]{1,0:T(8,128)(2,1)S(1)}, bf16[512,256]{1,0:T(8,128)(2,1)S(1)}, u32[]{:S(2)}, u32[]{:S(2)}) %collective-permute-start.13) | collective-permute-done | bytes 262176 | tf_op jit(solution)/shard_map/ppermute | solution.py:54
  105.6 30.2 %collective-permute-done.12 = bf16[512,256]{1,0:T(8,128)(2,1)S(1)} collective-permute-done((bf16[512,256]{1,0:T(8,128)(2,1)S(1)}, bf16[512,256]{1,0:T(8,128)(2,1)S(1)}, u32[]{:S(2)}, u32[]{:S(2)}) %collective-permute-start.12) | collective-permute-done | bytes 262176 | tf_op jit(solution)/shard_map/ppermute | solution.py:54
  137.4 2.8 shard_map.279
  143.6 17.5 %shard_map.276 = (bf16[512,768]{1,0:T(8,128)(2,1)S(1)}, f32[6,1,512]{2,1,0:T(1,128)S(1)}) custom-call(s32[4]{0:T(128)S(1)} %convert_add_fusion.7.flag_ref, bf16[512,768]{1,0:T(8,128)(2,1)S(1)} %copy-done.18, bf16[2048,128]{1,0:T(8,128)(2,1)S(1)} %get-tuple-element.403.k_ref, bf16[2048,128]{1,0:T(8,128)(2,1)S(1)} %get-tuple-element.402.v_ref, ...), custom_call_target="tpu_custom_call" | custom-call | tf_op jit(solution)/shard_map/pallas_call | solution.py:188
  161.2 3.4 convolution_convert_fusion.2
  168.9 7.9 %collective-permute-done.17 = bf16[256,1536]{1,0:T(8,128)(2,1)S(1)} collective-permute-done((bf16[256,1536]{1,0:T(8,128)(2,1)}, bf16[256,1536]{1,0:T(8,128)(2,1)S(1)}, u32[]{:S(2)}, u32[]{:S(2)}) %collective-permute-start.17) | collective-permute-done | bytes 786464 | tf_op jit(solution)/shard_map/ppermute | solution.py:49
  181.6 7.2 %collective-permute-start.19 = (bf16[256,1536]{1,0:T(8,128)(2,1)S(1)}, bf16[256,1536]{1,0:T(8,128)(2,1)S(1)}, u32[]{:S(2)}, u32[]{:S(2)}) collective-permute-start(bf16[256,1536]{1,0:T(8,128)(2,1)S(1)} %multiply_convert_fusion.refs_0_), channel_id=1, source_target_pairs={{0,16},{8,24},{16,0},{24,8},{1,17},{9,25},{17,1},{25,9},{2,18},{10... | collective-permute-start | bytes 2359304 | tf_op jit(solution)/shard_map/ppermute | solution.py:45
  191.3 2.7 copy-done.1
  194.0 6.1 %collective-permute-done.20.refs_1_ = bf16[256,1536]{1,0:T(8,128)(2,1)S(1)} collective-permute-done((bf16[256,1536]{1,0:T(8,128)(2,1)S(1)}, bf16[256,1536]{1,0:T(8,128)(2,1)S(1)}, u32[]{:S(2)}, u32[]{:S(2)}) %collective-permute-start.20) | collective-permute-done | bytes 786464 | tf_op jit(solution)/shard_map/ppermute | solution.py:49
  200.1 6.6 %collective-permute-done.19.refs_2_ = bf16[256,1536]{1,0:T(8,128)(2,1)S(1)} collective-permute-done((bf16[256,1536]{1,0:T(8,128)(2,1)S(1)}, bf16[256,1536]{1,0:T(8,128)(2,1)S(1)}, u32[]{:S(2)}, u32[]{:S(2)}) %collective-permute-start.19) | collective-permute-done | bytes 786464 | tf_op jit(solution)/shard_map/ppermute | solution.py:45
  209.7 8.7 %collective-permute-done.23 = bf16[128,1536]{1,0:T(8,128)(2,1)S(1)} collective-permute-done((bf16[128,1536]{1,0:T(8,128)(2,1)S(1)}, bf16[128,1536]{1,0:T(8,128)(2,1)S(1)}, u32[]{:S(2)}, u32[]{:S(2)}) %collective-permute-start.23) | collective-permute-done | bytes 393248 | tf_op jit(solution)/shard_map/ppermute | solution.py:49
  222.2 2.7 copy-done
  224.8 12.5 %shard_map.280 = (bf16[2048,1152]{1,0:T(8,128)(2,1)}, bf16[1024,1536]{1,0:T(8,128)(2,1)}, bf16[1024,1536]{1,0:T(8,128)(2,1)}) custom-call(bf16[2048,1536]{1,0:T(8,128)(2,1)} %bitcast.103, bf16[2048,1536]{1,0:T(8,128)(2,1)} %bitcast.110, bf16[1536,1152]{1,0:T(8,128)(2,1)} %all-gather.5.cloned.1.call-done.refs_2_), custom_call_target="tpu_custom_call" | custom-call | tf_op jit(solution)/shard_map/pallas_call | solution.py:586
  237.3 12.5 %shard_map.281 = (bf16[2048,1152]{1,0:T(8,128)(2,1)}, bf16[1024,1536]{1,0:T(8,128)(2,1)}, bf16[1024,1536]{1,0:T(8,128)(2,1)}) custom-call(bf16[2048,1536]{1,0:T(8,128)(2,1)} %bitcast.104, bf16[2048,1536]{1,0:T(8,128)(2,1)} %bitcast.111, bf16[1536,1152]{1,0:T(8,128)(2,1)} %all-gather.5.cloned.1.call-done.refs_2_, ...), custom_call_target="tpu_custom_call", output_to_operand_aliasing={{0}: (3, {})} | custom-call | tf_op jit(solution)/shard_map/pallas_call | solution.py:586
  249.8 16.6 %shard_map.282 = bf16[1536,1152]{1,0:T(8,128)(2,1)} custom-call(bf16[2048,1536]{1,0:T(8,128)(2,1)} %bitcast.105, bf16[2048,1536]{1,0:T(8,128)(2,1)} %bitcast.112, bf16[2048,1152]{1,0:T(8,128)(2,1)} %get-tuple-element.268.p_ref), custom_call_target="tpu_custom_call" | custom-call | tf_op jit(solution)/shard_map/pallas_call | solution.py:629
  266.5 2.9 all-gather.3.cloned.1.call-done.refs_2_
  269.4 22.5 %shard_map.283 = (bf16[2048,2304]{1,0:T(8,128)(2,1)}, bf16[1024,1536]{1,0:T(8,128)(2,1)}, bf16[1024,1536]{1,0:T(8,128)(2,1)}) custom-call(bf16[2048,1536]{1,0:T(8,128)(2,1)} %bitcast.106, bf16[2048,1536]{1,0:T(8,128)(2,1)} %bitcast.113, bf16[1536,2304]{1,0:T(8,128)(2,1)} %all-gather.3.cloned.1.call-done.refs_2_, ...), custom_call_target="tpu_custom_call" | custom-call | tf_op jit(solution)/shard_map/pallas_call | solution.py:586
  292.0 22.6 %shard_map.284 = (bf16[2048,2304]{1,0:T(8,128)(2,1)}, bf16[1024,1536]{1,0:T(8,128)(2,1)}, bf16[1024,1536]{1,0:T(8,128)(2,1)}) custom-call(bf16[2048,1536]{1,0:T(8,128)(2,1)} %bitcast.107, bf16[2048,1536]{1,0:T(8,128)(2,1)} %bitcast.114, bf16[1536,2304]{1,0:T(8,128)(2,1)} %all-gather.3.cloned.1.call-done.refs_2_, ...), custom_call_target="tpu_custom_call", output_to_operand_aliasing={{0}: (5, {})} | custom-call | tf_op jit(solution)/shard_map/pallas_call | solution.py:586
  320.4 11.4 %shard_map.285 = bf16[1536,768]{1,0:T(8,128)(2,1)} custom-call(bf16[2048,1536]{1,0:T(8,128)(2,1)} %bitcast.115, bf16[2048,2304]{1,0:T(8,128)(2,1)} %get-tuple-element.288.p_ref), custom_call_target="tpu_custom_call" | custom-call | flops 4831838208 | tf_op jit(solution)/shard_map/pallas_call | solution.py:629
  338.2 11.5 %shard_map.286 = bf16[1536,768]{1,0:T(8,128)(2,1)} custom-call(bf16[2048,1536]{1,0:T(8,128)(2,1)} %bitcast.108, bf16[2048,2304]{1,0:T(8,128)(2,1)} %get-tuple-element.288.p_ref), custom_call_target="tpu_custom_call" | custom-call | flops 4831838208 | tf_op jit(solution)/shard_map/pallas_call | solution.py:629
  349.7 6.0 %collective-permute-done.32 = bf16[256,1536]{1,0:T(8,128)(2,1)} collective-permute-done((bf16[256,1536]{1,0:T(8,128)(2,1)}, bf16[256,1536]{1,0:T(8,128)(2,1)}, u32[]{:S(2)}, u32[]{:S(2)}) %collective-permute-start.32) | collective-permute-done | bytes 786464 | tf_op jit(solution)/shard_map/ppermute | solution.py:45
  356.8 3.5 multiply_reduce_fusion
  363.3 5.4 collective-permute-done.35
  372.5 11.4 %shard_map.287 = bf16[1536,768]{1,0:T(8,128)(2,1)} custom-call(bf16[2048,1536]{1,0:T(8,128)(2,1)} %bitcast.109, bf16[2048,2304]{1,0:T(8,128)(2,1)} %get-tuple-element.288.p_ref), custom_call_target="tpu_custom_call" | custom-call | flops 4831838208 | tf_op jit(solution)/shard_map/pallas_call | solution.py:629
  383.9 3.0 reduce-scatter.7.cloned.1.call-done
  386.9 4.1 collective-permute-done.36
  393.6 3.5 shard_map.288
  399.7 3.5 add_convert_fusion.1
  408.2 24.4 %shard_map.290 = (bf16[512,768]{1,0:T(8,128)(2,1)}, bf16[2048,256]{1,0:T(8,128)(2,1)}) custom-call(s32[4]{0:T(128)} %copy-done.57, bf16[512,768]{1,0:T(8,128)(2,1)} %copy-done.17, bf16[2048,128]{1,0:T(8,128)(2,1)} %copy-done.10, bf16[2048,128]{1,0:T(8,128)(2,1)} %copy-done.9, bf16[512,768]{1,0:T(8,128)(2,1)} %copy-done.26, f32[6,1,512]{2,1,0:T(1,128)} %copy-done.54, ...), custom_call_target="tpu_custom_call" | custom-call | tf_op jit(solution)/shard_map/pallas_call | solution.py:295
  432.6 3.3 collective-permute-done.38
  444.7 3.5 collective-permute-start.42
  450.8 4.4 collective-permute-done.44
  455.2 10.3 %collective-permute-done.43 = bf16[512,256]{1,0:T(8,128)(2,1)} collective-permute-done((bf16[512,256]{1,0:T(8,128)(2,1)}, bf16[512,256]{1,0:T(8,128)(2,1)}, u32[]{:S(2)}, u32[]{:S(2)}) %collective-permute-start.43) | collective-permute-done | bytes 262176 | tf_op jit(solution)/shard_map/ppermute | solution.py:54
  475.8 6.5 %collective-permute-done.45 = bf16[4,96,768]{2,1,0:T(8,128)(2,1)S(1)} collective-permute-done((bf16[4,96,768]{2,1,0:T(8,128)(2,1)S(1)}, bf16[4,96,768]{2,1,0:T(8,128)(2,1)S(1)}, u32[]{:S(2)}, u32[]{:S(2)}) %collective-permute-start.45) | collective-permute-done | bytes 589856 | tf_op jit(solution)/shard_map/ppermute | solution.py:45
  483.4 6.2 %collective-permute-start.47 = (bf16[96,1536]{1,0:T(8,128)(2,1)S(1)}, bf16[96,1536]{1,0:T(8,128)(2,1)S(1)}, u32[]{:S(2)}, u32[]{:S(2)}) collective-permute-start(bf16[96,1536]{1,0:T(8,128)(2,1)S(1)} %fusion.40), channel_id=1, source_target_pairs={{0,2},{2,4},{4,6},{6,0},{1,3},{3,5},{5,7},{7,1},{8,10},{10,12},{12... | collective-permute-start | bytes 884744 | tf_op jit(solution)/shard_map/ppermute | solution.py:54
  500.4 2.8 collective-permute-done.47
  511.2 10.3 %collective-permute-done.60.refs_3_ = bf16[96,2688]{1,0:T(8,128)(2,1)S(1)} collective-permute-done((bf16[96,2688]{1,0:T(8,128)(2,1)S(1)}, bf16[96,2688]{1,0:T(8,128)(2,1)S(1)}, u32[]{:S(2)}, u32[]{:S(2)}) %collective-permute-start.60) | collective-permute-done | bytes 516128 | tf_op jit(solution)/shard_map/ppermute | solution.py:45
  527.4 3.3 collective-permute-start.56
  530.6 4.6 collective-permute-done.57
  549.5 5.2 collective-permute-done.65.other_ref
  563.3 3.2 shard_map.301
  (481 shorter events, 177.8 us)
Async XLA Ops:
  7.2 217.7 %all-gather.5.cloned.1.call-start = ((), (), s32[]{:S(2)}) async-start(), calls=%async_computation.5 | async-start | bytes 4423680 | tf_op jit(solution)/shard_map/all_gather | solution.py:864
  8.3 17.2 %collective-permute-start.1 = (bf16[96,1792]{1,0:T(8,128)(2,1)S(1)}, bf16[96,1792]{1,0:T(8,128)(2,1)S(1)}, u32[]{:S(2)}, u32[]{:S(2)}) collective-permute-start(bf16[96,1792]{1,0:T(8,128)(2,1)S(1)} %pad_maximum_fusion.3.refs_0_), channel_id=1, source_target_pairs={{0,16},{8,24},{16,0},{24,8},{1,17},{9,25},{17,1},{25,9},{2,18},{10... | collective-permute-start | bytes 1032200 | tf_op jit(solution)/shard_map/ppermute | solution.py:45
  11.3 14.3 %collective-permute-start = (bf16[96,1792]{1,0:T(8,128)(2,1)S(1)}, bf16[96,1792]{1,0:T(8,128)(2,1)S(1)}, u32[]{:S(2)}, u32[]{:S(2)}) collective-permute-start(bf16[96,1792]{1,0:T(8,128)(2,1)S(1)} %pad_maximum_fusion.3.refs_0_), channel_id=1, source_target_pairs={{0,2},{2,4},{4,6},{6,0},{1,3},{3,5},{5,7},{7,1},{8,10},{10,12},{12... | collective-permute-start | bytes 1032200 | tf_op jit(solution)/shard_map/ppermute | solution.py:54
  25.6 17.0 %collective-permute-start.3 = (bf16[96,1792]{1,0:T(8,128)(2,1)S(1)}, bf16[96,1792]{1,0:T(8,128)(2,1)S(1)}, u32[]{:S(2)}, u32[]{:S(2)}) collective-permute-start(bf16[96,1792]{1,0:T(8,128)(2,1)S(1)} %collective-permute-done.refs_1_), channel_id=1, source_target_pairs={{0,16},{8,24},{16,0},{24,8},{1,17},{9,25},{17,1},{25,9},{2,18},{10... | collective-permute-start | bytes 1032200 | tf_op jit(solution)/shard_map/ppermute | solution.py:45
  26.2 17.2 %collective-permute-start.2 = (bf16[96,1792]{1,0:T(8,128)(2,1)S(1)}, bf16[96,1792]{1,0:T(8,128)(2,1)S(1)}, u32[]{:S(2)}, u32[]{:S(2)}) collective-permute-start(bf16[96,1792]{1,0:T(8,128)(2,1)S(1)} %collective-permute-done.refs_1_), channel_id=1, source_target_pairs={{0,2},{2,4},{4,6},{6,0},{1,3},{3,5},{5,7},{7,1},{8,10},{10,12},{12... | collective-permute-start | bytes 1032200 | tf_op jit(solution)/shard_map/ppermute | solution.py:54
  27.8 13.6 %collective-permute-start.5 = (bf16[96,1152]{1,0:T(8,128)(2,1)S(1)}, bf16[96,1152]{1,0:T(8,128)(2,1)S(1)}, u32[]{:S(2)}, u32[]{:S(2)}) collective-permute-start(bf16[96,1152]{1,0:T(8,128)(2,1)S(1)} %get-tuple-element.209), channel_id=1, source_target_pairs={{0,16},{8,24},{16,0},{24,8},{1,17},{9,25},{17,1},{25,9},{2,18},{10... | collective-permute-start | bytes 663560 | tf_op jit(solution)/shard_map/ppermute | solution.py:45
  29.3 13.4 %collective-permute-start.6 = (bf16[96,1152]{1,0:T(8,128)(2,1)S(1)}, bf16[96,1152]{1,0:T(8,128)(2,1)S(1)}, u32[]{:S(2)}, u32[]{:S(2)}) collective-permute-start(bf16[96,1152]{1,0:T(8,128)(2,1)S(1)} %get-tuple-element.210), channel_id=1, source_target_pairs={{0,24},{8,16},{16,8},{24,0},{1,25},{9,17},{17,9},{25,1},{2,26},{10... | collective-permute-start | bytes 663560 | tf_op jit(solution)/shard_map/ppermute | solution.py:45
  48.9 220.5 %all-gather.3.cloned.1.call-start = ((), (), s32[]{:S(2)}) async-start(), calls=%async_computation.4 | async-start | bytes 8847360 | tf_op jit(solution)/shard_map/all_gather | solution.py:896
  83.8 19.6 %collective-permute-start.13 = (bf16[512,256]{1,0:T(8,128)(2,1)S(1)}, bf16[512,256]{1,0:T(8,128)(2,1)S(1)}, u32[]{:S(2)}, u32[]{:S(2)}) collective-permute-start(bf16[512,256]{1,0:T(8,128)(2,1)S(1)} %get-tuple-element.242), channel_id=1, source_target_pairs={{0,6},{2,0},{4,2},{6,4},{1,7},{3,1},{5,3},{7,5},{8,14},{10,8},{12,... | collective-permute-start | bytes 786440 | tf_op jit(solution)/shard_map/ppermute | solution.py:54
  84.3 51.4 %collective-permute-start.12 = (bf16[512,256]{1,0:T(8,128)(2,1)S(1)}, bf16[512,256]{1,0:T(8,128)(2,1)S(1)}, u32[]{:S(2)}, u32[]{:S(2)}) collective-permute-start(bf16[512,256]{1,0:T(8,128)(2,1)S(1)} %get-tuple-element.242), channel_id=1, source_target_pairs={{0,4},{2,6},{4,0},{6,2},{1,5},{3,7},{5,1},{7,3},{8,12},{10,14},{12... | collective-permute-start | bytes 786440 | tf_op jit(solution)/shard_map/ppermute | solution.py:54
  85.0 50.7 %collective-permute-start.11 = (bf16[512,256]{1,0:T(8,128)(2,1)S(1)}, bf16[512,256]{1,0:T(8,128)(2,1)S(1)}, u32[]{:S(2)}, u32[]{:S(2)}) collective-permute-start(bf16[512,256]{1,0:T(8,128)(2,1)S(1)} %get-tuple-element.242), channel_id=1, source_target_pairs={{0,2},{2,4},{4,6},{6,0},{1,3},{3,5},{5,7},{7,1},{8,10},{10,12},{12... | collective-permute-start | bytes 786440 | tf_op jit(solution)/shard_map/ppermute | solution.py:54
  89.8 46.0 %collective-permute-start.14 = (bf16[96,2304]{1,0:T(8,128)(2,1)}, bf16[96,2304]{1,0:T(8,128)(2,1)S(1)}, u32[]{:S(2)}, u32[]{:S(2)}) collective-permute-start(bf16[96,2304]{1,0:T(8,128)(2,1)} %copy-done.63), channel_id=1, source_target_pairs={{0,8},{8,0},{16,24},{24,16},{1,9},{9,1},{17,25},{25,17},{2,10},{10... | collective-permute-start | bytes 1327112 | tf_op jit(solution)/shard_map/ppermute | solution.py:45
  89.9 45.9 %collective-permute-start.15 = (bf16[96,2304]{1,0:T(8,128)(2,1)}, bf16[96,2304]{1,0:T(8,128)(2,1)S(1)}, u32[]{:S(2)}, u32[]{:S(2)}) collective-permute-start(bf16[96,2304]{1,0:T(8,128)(2,1)} %copy-done.62), channel_id=1, source_target_pairs={{0,16},{8,24},{16,0},{24,8},{1,17},{9,25},{17,1},{25,9},{2,18},{10... | collective-permute-start | bytes 1327112 | tf_op jit(solution)/shard_map/ppermute | solution.py:45
  103.4 32.4 %collective-permute-start.16 = (bf16[96,2304]{1,0:T(8,128)(2,1)}, bf16[96,2304]{1,0:T(8,128)(2,1)S(1)}, u32[]{:S(2)}, u32[]{:S(2)}) collective-permute-start(bf16[96,2304]{1,0:T(8,128)(2,1)} %copy-done.61), channel_id=1, source_target_pairs={{0,24},{8,16},{16,8},{24,0},{1,25},{9,17},{17,9},{25,1},{2,26},{10... | collective-permute-start | bytes 1327112 | tf_op jit(solution)/shard_map/ppermute | solution.py:45
  140.3 209.4 %reduce-scatter.5.cloned.1.call-start = ((), (), s32[]{:S(2)}) async-start(), calls=%async_computation.6 | async-start | bytes 4423680 | tf_op jit(solution)/shard_map/reduce_scatter | solution.py:927
  140.7 36.9 %collective-permute-start.18 = (bf16[512,1536]{1,0:T(8,128)(2,1)}, bf16[512,1536]{1,0:T(8,128)(2,1)}, u32[]{:S(2)}, u32[]{:S(2)}) collective-permute-start(bf16[512,1536]{1,0:T(8,128)(2,1)} %convolution_convert_fusion.refs_0_), channel_id=1, source_target_pairs={{0,16},{8,24},{16,0},{24,8},{1,17},{9,25},{17,1},{25,9},{2,18},{10... | collective-permute-start | bytes 4718600 | tf_op jit(solution)/shard_map/ppermute | solution.py:45
  166.3 22.5 %collective-permute-start.21 = (bf16[512,1536]{1,0:T(8,128)(2,1)}, bf16[512,1536]{1,0:T(8,128)(2,1)S(1)}, u32[]{:S(2)}, u32[]{:S(2)}) collective-permute-start(bf16[512,1536]{1,0:T(8,128)(2,1)} %convolution_convert_fusion.refs_0_), channel_id=1, source_target_pairs={{0,8},{8,0},{16,24},{24,16},{1,9},{9,1},{17,25},{25,17},{2,10},{10... | collective-permute-start | bytes 4718600 | tf_op jit(solution)/shard_map/ppermute | solution.py:45
  180.1 20.0 %collective-permute-start.20 = (bf16[256,1536]{1,0:T(8,128)(2,1)S(1)}, bf16[256,1536]{1,0:T(8,128)(2,1)S(1)}, u32[]{:S(2)}, u32[]{:S(2)}) collective-permute-start(bf16[256,1536]{1,0:T(8,128)(2,1)S(1)} %multiply_convert_fusion.refs_0_), channel_id=1, source_target_pairs={{0,1},{1,0},{2,3},{3,2},{4,5},{5,4},{6,7},{7,6},{8,9},{9,8},{10,11... | collective-permute-start | bytes 2359304 | tf_op jit(solution)/shard_map/ppermute | solution.py:49
  181.6 25.1 %collective-permute-start.19 = (bf16[256,1536]{1,0:T(8,128)(2,1)S(1)}, bf16[256,1536]{1,0:T(8,128)(2,1)S(1)}, u32[]{:S(2)}, u32[]{:S(2)}) collective-permute-start(bf16[256,1536]{1,0:T(8,128)(2,1)S(1)} %multiply_convert_fusion.refs_0_), channel_id=1, source_target_pairs={{0,16},{8,24},{16,0},{24,8},{1,17},{9,25},{17,1},{25,9},{2,18},{10... | collective-permute-start | bytes 2359304 | tf_op jit(solution)/shard_map/ppermute | solution.py:45
  188.8 20.9 %collective-permute-start.25 = (bf16[256,1536]{1,0:T(8,128)(2,1)S(1)}, bf16[256,1536]{1,0:T(8,128)(2,1)S(1)}, u32[]{:S(2)}, u32[]{:S(2)}) collective-permute-start(bf16[256,1536]{1,0:T(8,128)(2,1)S(1)} %multiply_convert_fusion.refs_0_), channel_id=1, source_target_pairs={{0,8},{8,0},{16,24},{24,16},{1,9},{9,1},{17,25},{25,17},{2,10},{10... | collective-permute-start | bytes 2359304 | tf_op jit(solution)/shard_map/ppermute | solution.py:45
  266.5 120.5 %reduce-scatter.7.cloned.1.call-start = ((), (), s32[]{:S(2)}) async-start(), calls=%async_computation.7 | async-start | bytes 2949120 | tf_op jit(solution)/shard_map/reduce_scatter | solution.py:935
  292.0 22.7 %collective-permute-start.29 = (bf16[1024,1536]{1,0:T(8,128)(2,1)}, bf16[1024,1536]{1,0:T(8,128)(2,1)S(1)}, u32[]{:S(2)}, u32[]{:S(2)}) collective-permute-start(bf16[1024,1536]{1,0:T(8,128)(2,1)} %get-tuple-element.272), channel_id=1, source_target_pairs={{0,8},{8,0},{16,24},{24,16},{1,9},{9,1},{17,25},{25,17},{2,10},{10... | collective-permute-start | bytes 9437192 | tf_op jit(solution)/shard_map/ppermute | solution.py:45
  317.4 15.1 %collective-permute-start.30 = (bf16[128,1536]{1,0:T(8,128)(2,1)S(1)}, bf16[128,1536]{1,0:T(8,128)(2,1)}, u32[]{:S(2)}, u32[]{:S(2)}) collective-permute-start(bf16[128,1536]{1,0:T(8,128)(2,1)S(1)} %get-tuple-element.405), channel_id=1, source_target_pairs={{0,16},{8,24},{16,0},{24,8},{1,17},{9,25},{17,1},{25,9},{2,18},{10... | collective-permute-start | bytes 1179656 | tf_op jit(solution)/shard_map/ppermute | solution.py:45
  336.1 19.6 %collective-permute-start.32 = (bf16[256,1536]{1,0:T(8,128)(2,1)}, bf16[256,1536]{1,0:T(8,128)(2,1)}, u32[]{:S(2)}, u32[]{:S(2)}) collective-permute-start(bf16[256,1536]{1,0:T(8,128)(2,1)} %pad_maximum_fusion.1), channel_id=1, source_target_pairs={{0,16},{8,24},{16,0},{24,8},{1,17},{9,25},{17,1},{25,9},{2,18},{10... | collective-permute-start | bytes 2359304 | tf_op jit(solution)/shard_map/ppermute | solution.py:45
  337.5 19.3 %collective-permute-start.33 = (bf16[256,1536]{1,0:T(8,128)(2,1)}, bf16[256,1536]{1,0:T(8,128)(2,1)S(1)}, u32[]{:S(2)}, u32[]{:S(2)}) collective-permute-start(bf16[256,1536]{1,0:T(8,128)(2,1)} %pad_maximum_fusion.2), channel_id=1, source_target_pairs={{0,1},{1,0},{2,3},{3,2},{4,5},{5,4},{6,7},{7,6},{8,9},{9,8},{10,11... | collective-permute-start | bytes 2359304 | tf_op jit(solution)/shard_map/ppermute | solution.py:49
  338.1 112.7 %reduce-scatter.9.cloned.1.call-start = ((), (), s32[]{:S(2)}) async-start(), calls=%async_computation.8 | async-start | bytes 2949120 | tf_op jit(solution)/shard_map/reduce_scatter | solution.py:935
  362.7 21.2 %collective-permute-start.34 = (bf16[256,1536]{1,0:T(8,128)(2,1)S(1)}, bf16[256,1536]{1,0:T(8,128)(2,1)}, u32[]{:S(2)}, u32[]{:S(2)}) collective-permute-start(bf16[256,1536]{1,0:T(8,128)(2,1)S(1)} %fusion.78.own_ref), channel_id=1, source_target_pairs={{0,1},{1,0},{2,3},{3,2},{4,5},{5,4},{6,7},{7,6},{8,9},{9,8},{10,11... | collective-permute-start | bytes 2359304 | tf_op jit(solution)/shard_map/ppermute | solution.py:49
  363.2 174.6 %reduce-scatter.11.cloned.1.call-start = ((), (), s32[]{:S(2)}) async-start(), calls=%async_computation.9 | async-start | bytes 2949120 | tf_op jit(solution)/shard_map/reduce_scatter | solution.py:935
  371.1 19.9 %collective-permute-start.36 = (bf16[256,1536]{1,0:T(8,128)(2,1)}, bf16[256,1536]{1,0:T(8,128)(2,1)}, u32[]{:S(2)}, u32[]{:S(2)}) collective-permute-start(bf16[256,1536]{1,0:T(8,128)(2,1)} %add_convert_fusion.3), channel_id=1, source_target_pairs={{0,16},{8,24},{16,0},{24,8},{1,17},{9,25},{17,1},{25,9},{2,18},{10... | collective-permute-start | bytes 2359304 | tf_op jit(solution)/shard_map/ppermute | solution.py:45
  403.2 29.4 %collective-permute-start.40 = (bf16[256,1536]{1,0:T(8,128)(2,1)}, bf16[256,1536]{1,0:T(8,128)(2,1)S(1)}, u32[]{:S(2)}, u32[]{:S(2)}) collective-permute-start(bf16[256,1536]{1,0:T(8,128)(2,1)} %get-tuple-element.384), channel_id=1, source_target_pairs={{0,1},{1,0},{2,3},{3,2},{4,5},{5,4},{6,7},{7,6},{8,9},{9,8},{10,11... | collective-permute-start | bytes 2359304 | tf_op jit(solution)/shard_map/ppermute | solution.py:49
  403.5 29.1 %collective-permute-start.39 = (bf16[256,1536]{1,0:T(8,128)(2,1)S(1)}, bf16[256,1536]{1,0:T(8,128)(2,1)S(1)}, u32[]{:S(2)}, u32[]{:S(2)}) collective-permute-start(bf16[256,1536]{1,0:T(8,128)(2,1)S(1)} %get-tuple-element.385), channel_id=1, source_target_pairs={{0,16},{8,24},{16,0},{24,8},{1,17},{9,25},{17,1},{25,9},{2,18},{10... | collective-permute-start | bytes 2359304 | tf_op jit(solution)/shard_map/ppermute | solution.py:45
  407.4 28.5 %collective-permute-start.38 = (bf16[4,96,768]{2,1,0:T(8,128)(2,1)}, bf16[4,96,768]{2,1,0:T(8,128)(2,1)}, u32[]{:S(2)}, u32[]{:S(2)}) collective-permute-start(bf16[4,96,768]{2,1,0:T(8,128)(2,1)} %fusion.23), channel_id=1, source_target_pairs={{0,16},{8,24},{16,0},{24,8},{1,17},{9,25},{17,1},{25,9},{2,18},{10... | collective-permute-start | bytes 1769480 | tf_op jit(solution)/shard_map/ppermute | solution.py:45
  440.7 24.9 %collective-permute-start.41 = (bf16[4,192,768]{2,1,0:T(8,128)(2,1)}, bf16[4,192,768]{2,1,0:T(8,128)(2,1)}, u32[]{:S(2)}, u32[]{:S(2)}) collective-permute-start(bf16[4,192,768]{2,1,0:T(8,128)(2,1)} %get-tuple-element.306), channel_id=1, source_target_pairs={{0,8},{8,0},{16,24},{24,16},{1,9},{9,1},{17,25},{25,17},{2,10},{10... | collective-permute-start | bytes 3538952 | tf_op jit(solution)/shard_map/ppermute | solution.py:45
  444.0 21.6 %collective-permute-start.43 = (bf16[512,256]{1,0:T(8,128)(2,1)}, bf16[512,256]{1,0:T(8,128)(2,1)}, u32[]{:S(2)}, u32[]{:S(2)}) collective-permute-start(bf16[512,256]{1,0:T(8,128)(2,1)} %get-tuple-element.400), channel_id=1, source_target_pairs={{0,4},{2,6},{4,0},{6,2},{1,5},{3,7},{5,1},{7,3},{8,12},{10,14},{12... | collective-permute-start | bytes 786440 | tf_op jit(solution)/shard_map/ppermute | solution.py:54
  444.7 20.9 %collective-permute-start.42 = (bf16[512,256]{1,0:T(8,128)(2,1)}, bf16[512,256]{1,0:T(8,128)(2,1)}, u32[]{:S(2)}, u32[]{:S(2)}) collective-permute-start(bf16[512,256]{1,0:T(8,128)(2,1)} %get-tuple-element.401), channel_id=1, source_target_pairs={{0,6},{2,0},{4,2},{6,4},{1,7},{3,1},{5,3},{7,5},{8,14},{10,8},{12,... | collective-permute-start | bytes 786440 | tf_op jit(solution)/shard_map/ppermute | solution.py:54
  467.7 14.6 %collective-permute-start.45 = (bf16[4,96,768]{2,1,0:T(8,128)(2,1)S(1)}, bf16[4,96,768]{2,1,0:T(8,128)(2,1)S(1)}, u32[]{:S(2)}, u32[]{:S(2)}) collective-permute-start(bf16[4,96,768]{2,1,0:T(8,128)(2,1)S(1)} %fusion.24), channel_id=1, source_target_pairs={{0,16},{8,24},{16,0},{24,8},{1,17},{9,25},{17,1},{25,9},{2,18},{10... | collective-permute-start | bytes 1769480 | tf_op jit(solution)/shard_map/ppermute | solution.py:45
  474.2 26.2 %collective-permute-start.49 = (bf16[256,1536]{1,0:T(8,128)(2,1)S(1)}, bf16[256,1536]{1,0:T(8,128)(2,1)S(1)}, u32[]{:S(2)}, u32[]{:S(2)}) collective-permute-start(bf16[256,1536]{1,0:T(8,128)(2,1)S(1)} %shard_map.293), channel_id=1, source_target_pairs={{0,1},{1,0},{2,3},{3,2},{4,5},{5,4},{6,7},{7,6},{8,9},{9,8},{10,11... | collective-permute-start | bytes 2359304 | tf_op jit(solution)/shard_map/ppermute | solution.py:49
  483.4 19.8 %collective-permute-start.47 = (bf16[96,1536]{1,0:T(8,128)(2,1)S(1)}, bf16[96,1536]{1,0:T(8,128)(2,1)S(1)}, u32[]{:S(2)}, u32[]{:S(2)}) collective-permute-start(bf16[96,1536]{1,0:T(8,128)(2,1)S(1)} %fusion.40), channel_id=1, source_target_pairs={{0,2},{2,4},{4,6},{6,0},{1,3},{3,5},{5,7},{7,1},{8,10},{10,12},{12... | collective-permute-start | bytes 884744 | tf_op jit(solution)/shard_map/ppermute | solution.py:54
  496.7 13.2 %collective-permute-start.58 = (bf16[96,2688]{1,0:T(8,128)(2,1)S(1)}, bf16[96,2688]{1,0:T(8,128)(2,1)S(1)}, u32[]{:S(2)}, u32[]{:S(2)}) collective-permute-start(bf16[96,2688]{1,0:T(8,128)(2,1)S(1)} %get-tuple-element.337), channel_id=1, source_target_pairs={{0,8},{8,0},{16,24},{24,16},{1,9},{9,1},{17,25},{25,17},{2,10},{10... | collective-permute-start | bytes 1548296 | tf_op jit(solution)/shard_map/ppermute | solution.py:45
  496.7 14.5 %collective-permute-start.59 = (bf16[96,2688]{1,0:T(8,128)(2,1)S(1)}, bf16[96,2688]{1,0:T(8,128)(2,1)S(1)}, u32[]{:S(2)}, u32[]{:S(2)}) collective-permute-start(bf16[96,2688]{1,0:T(8,128)(2,1)S(1)} %get-tuple-element.338), channel_id=1, source_target_pairs={{0,16},{8,24},{16,0},{24,8},{1,17},{9,25},{17,1},{25,9},{2,18},{10... | collective-permute-start | bytes 1548296 | tf_op jit(solution)/shard_map/ppermute | solution.py:45
  499.0 22.5 %collective-permute-start.60 = (bf16[96,2688]{1,0:T(8,128)(2,1)S(1)}, bf16[96,2688]{1,0:T(8,128)(2,1)S(1)}, u32[]{:S(2)}, u32[]{:S(2)}) collective-permute-start(bf16[96,2688]{1,0:T(8,128)(2,1)S(1)} %get-tuple-element.339), channel_id=1, source_target_pairs={{0,24},{8,16},{16,8},{24,0},{1,25},{9,17},{17,9},{25,1},{2,26},{10... | collective-permute-start | bytes 1548296 | tf_op jit(solution)/shard_map/ppermute | solution.py:45
  506.1 20.1 %collective-permute-start.52 = (f32[4096]{0:T(1024)S(1)}, f32[4096]{0:T(1024)S(1)}, u32[]{:S(2)}, u32[]{:S(2)}) collective-permute-start(f32[4096]{0:T(1024)S(1)} %pad_maximum_fusion.7), channel_id=1, source_target_pairs={{0,16},{8,24},{16,0},{24,8},{1,17},{9,25},{17,1},{25,9},{2,18},{10... | collective-permute-start | bytes 49160 | tf_op jit(solution)/shard_map/ppermute | solution.py:1044
  507.6 30.2 %collective-permute-start.54 = (bf16[256,1536]{1,0:T(8,128)(2,1)S(1)}, bf16[256,1536]{1,0:T(8,128)(2,1)S(1)}, u32[]{:S(2)}, u32[]{:S(2)}) collective-permute-start(bf16[256,1536]{1,0:T(8,128)(2,1)S(1)} %shard_map.295.own_ref), channel_id=1, source_target_pairs={{0,1},{1,0},{2,3},{3,2},{4,5},{5,4},{6,7},{7,6},{8,9},{9,8},{10,11... | collective-permute-start | bytes 2359304 | tf_op jit(solution)/shard_map/ppermute | solution.py:49
  509.9 17.5 %collective-permute-start.53 = (f32[4096]{0:T(1024)S(1)}, f32[4096]{0:T(1024)S(1)}, u32[]{:S(2)}, u32[]{:S(2)}) collective-permute-start(f32[4096]{0:T(1024)S(1)} %pad_maximum_fusion.7), channel_id=1, source_target_pairs={{0,24},{8,0},{16,8},{24,16},{1,25},{9,1},{17,9},{25,17},{2,26},{10... | collective-permute-start | bytes 49160 | tf_op jit(solution)/shard_map/ppermute | solution.py:1044
  511.2 19.4 %collective-permute-start.51 = (f32[4096]{0:T(1024)S(1)}, f32[4096]{0:T(1024)S(1)}, u32[]{:S(2)}, u32[]{:S(2)}) collective-permute-start(f32[4096]{0:T(1024)S(1)} %pad_maximum_fusion.7), channel_id=1, source_target_pairs={{0,8},{8,16},{16,24},{24,0},{1,9},{9,17},{17,25},{25,1},{2,10},{10... | collective-permute-start | bytes 49160 | tf_op jit(solution)/shard_map/ppermute | solution.py:1044
  522.3 14.9 %collective-permute-start.50 = (bf16[96,1536]{1,0:T(8,128)(2,1)S(1)}, bf16[96,1536]{1,0:T(8,128)(2,1)S(1)}, u32[]{:S(2)}, u32[]{:S(2)}) collective-permute-start(bf16[96,1536]{1,0:T(8,128)(2,1)S(1)} %fusion.33), channel_id=1, source_target_pairs={{0,2},{2,4},{4,6},{6,0},{1,3},{3,5},{5,7},{7,1},{8,10},{10,12},{12... | collective-permute-start | bytes 884744 | tf_op jit(solution)/shard_map/ppermute | solution.py:54
  535.2 19.5 %collective-permute-start.65 = (bf16[256,1536]{1,0:T(8,128)(2,1)S(1)}, bf16[256,1536]{1,0:T(8,128)(2,1)}, u32[]{:S(2)}, u32[]{:S(2)}) collective-permute-start(bf16[256,1536]{1,0:T(8,128)(2,1)S(1)} %shard_map.298.own_ref), channel_id=1, source_target_pairs={{0,1},{1,0},{2,3},{3,2},{4,5},{5,4},{6,7},{7,6},{8,9},{9,8},{10,11... | collective-permute-start | bytes 2359304 | tf_op jit(solution)/shard_map/ppermute | solution.py:49
  543.4 13.2 %collective-permute-start.61 = (bf16[96,1536]{1,0:T(8,128)(2,1)S(1)}, bf16[96,1536]{1,0:T(8,128)(2,1)S(1)}, u32[]{:S(2)}, u32[]{:S(2)}) collective-permute-start(bf16[96,1536]{1,0:T(8,128)(2,1)S(1)} %fusion.37), channel_id=1, source_target_pairs={{0,2},{2,4},{4,6},{6,0},{1,3},{3,5},{5,7},{7,1},{8,10},{10,12},{12... | collective-permute-start | bytes 884744 | tf_op jit(solution)/shard_map/ppermute | solution.py:54
  (136 other events, 1187.0 us)
Sparse Core Ops, SparseCore 0:
  49.0 91.9 all-gather.4
  142.6 126.8 all-gather.2
  271.8 64.5 reduce-scatter.4
  338.6 48.3 reduce-scatter.6
  389.1 47.5 reduce-scatter.8
  465.7 57.7 reduce-scatter.10

commit v5 on v4

--- a/solution.py
+++ b/solution.py
@@ -1054,16 +1054,16 @@
     for s in range(2, n_seq):
         total = z_shift(total.astype(BF16), 1)
         if s == 2:
-            total, sums, out_other, up_share, *arrived = together(
-                total, sums, out_other, up_share, *kv_moved, *pieces
+            total, sums, out_other, up_share, *kv_moved = together(
+                total, sums, out_other, up_share, *kv_moved
             )
-            kv_moved, pieces = arrived[: n_seq - 1], arrived[n_seq - 1 :]
             up_pieces = exchange_units(up_share)
             sums = shift_add(sums, "seq")
         elif s == 3:
-            total, sums, input_other, *up_pieces = together(
-                total, sums, input_other, *up_pieces
+            total, sums, input_other, *arrived = together(
+                total, sums, input_other, *pieces, *up_pieces
             )
+            pieces, up_pieces = arrived[:n_dp], arrived[n_dp:]
         total = place_of(large, s + 1) + total.astype(F32)
     kv_share = functools.reduce(
         lambda a, b: a + b.astype(F32), kv_moved, place_of(kv_rows, 0)

time: 584 us -> 605 us (1.036)
  waiting for transfers between devices: 165 us -> 190 us
  Pallas kernels: 207 us -> 197 us
  starting transfers between devices: 74.2 us -> 82.7 us
    ppermute x38, waiting for transfers between devices: 62.4 us -> 82.4 us  [dp_swap(): return lax.ppermute(value, 'dp', [(i, i ^ flip) for i in range(size)])]
    pallas_call x1, Pallas kernels: 24.4 us -> 13.1 us  [attend_back(): pl.pallas_call(functools.partial(attend_back_kernel, rows, HEAD_DIM ** (-...]
    pallas_call x1, Pallas kernels: 17.5 us -> 9.51 us  [attend(): pl.pallas_call(functools.partial(attend_kernel, rows, HEAD_DIM ** (-0.5)...]
    ppermute x15, starting transfers between devices: 23.9 us -> 31.7 us  [z_shift(): lax.ppermute(value, 'seq', [(i, (i + step) % size) for i in range(size)])]
    pallas_call x4, Pallas kernels: 70.1 us -> 77.9 us  [feed(): pl.pallas_call(functools.partial(feed_kernel, columns // 3, earlier is no...]
    unnamed x220 -> x208, local copies, waits for them, and re-layouts: 29.1 us -> 26.6 us
  transfers between devices with their start and end apart: 76 -> 76, of which waited for: 32 -> 34; matrix products, arithmetic and copies ran while one was open for 14% -> 13% of each run, Pallas kernels for 36% -> 33%
where the time goes in v5:
time: 605 us; the launch traced here: 596 us
  Pallas kernels  197 us (33%)
  waiting for transfers between devices  190 us (31%)
  starting transfers between devices  82.7 us (14%)
  other arithmetic  47.5 us (8%)
  local copies, waits for them, and re-layouts  45.7 us (8%)
  matrix products  16.8 us (3%)
  between operations  16.3 us (3%)
    ppermute x38, waiting for transfers between devices, dp_swap(): return lax.ppermute(value, 'dp', [(i, i ^ flip) for i in range(size)])  82.4 us
    pallas_call x4, Pallas kernels, feed(): pl.pallas_call(functools.partial(feed_kernel, columns // 3, earlier is no...  77.9 us
    ppermute x15, waiting for transfers between devices, z_shift(): lax.ppermute(value, 'seq', [(i, (i + step) % size) for i in range(size)])  71 us
    pallas_call x4, Pallas kernels, unit_gradients(): pl.pallas_call(kernel, grid=(each * len(which),), in_specs=[held] * len(l...  51 us
    ppermute x38, starting transfers between devices, dp_swap(): return lax.ppermute(value, 'dp', [(i, i ^ flip) for i in range(size)])  33 us
    ppermute x15, starting transfers between devices, z_shift(): lax.ppermute(value, 'seq', [(i, (i + step) % size) for i in range(size)])  31.7 us
    unnamed x208, local copies, waits for them, and re-layouts  26.6 us
    ppermute x10, waiting for transfers between devices, y_swap(): return lax.ppermute(value, 'tensor', [(0, 1), (1, 0)])  26.5 us
  transfers between devices with their start and end apart: 76, of which 34 were waited for; matrix products, arithmetic and copies ran while one was open for 13% of the time, Pallas kernels for 33%

profile of v5, /device:TPU:0, one launch (start us, length us, event | category | flops | bytes accessed | tf_op | source)
XLA Modules:
  0.0 595.6 jit_solution(7400452572602745674)
XLA Ops:
  8.3 3.0 collective-permute-start.1
  30.6 4.3 convolution_convert_fusion.1.x_ref
  36.1 5.2 collective-permute-done.5.refs_2_
  48.9 4.8 collective-permute-done.8.refs_6_
  53.7 3.2 collective-permute-done.7.refs_3_
  59.4 6.6 %convolution_convert_fusion.refs_0_ = bf16[512,1536]{1,0:T(8,128)(2,1)} fusion(bf16[1536,1536]{1,0:T(8,128)(2,1)} %copy-done.3, bf16[512,1536]{1,0:T(8,128)(2,1)S(1)} %copy-done.70, bf16[256,1536]{1,0:T(8,128)(2,1)S(1)} %get-tuple-element.392, bf16[256,1536]{1,0:T(8,128)(2,1)S(1)} %get-tuple-element.391, pred[]{:T(512)S(6)} %eq.52), kind=kOutput, calls=%fused_computation.13 | convolution fusion | flops 2420637696 | bytes 9437185 | tf_op jit(solution)/shard_map/dot_general | solution.py:24
  75.8 6.0 %shard_map.275 = (bf16[512,768]{1,0:T(8,128)(2,1)S(1)}, bf16[512,256]{1,0:T(8,128)(2,1)S(1)}, bf16[512,1536]{1,0:T(8,128)(2,1)S(1)}, bf16[16,96,1792]{2,1,0:T(8,128)(2,1)}) custom-call(s32[16]{0:T(128)S(1)} %copy-done.54, bf16[8,96,1792]{2,1,0:T(8,128)(2,1)S(1)} %shard_map.274.mine_ref, bf16[8,96,1792]{2,1,0:T(8,128)(2,1)} %collective-permute-done.10.theirs_ref, ...), custom_call_target="tpu_custom_call" | custom-call | tf_op jit(solution)/shard_map/pallas_call | solution.py:407
  91.7 11.6 %collective-permute-done.13 = bf16[512,256]{1,0:T(8,128)(2,1)S(1)} collective-permute-done((bf16[512,256]{1,0:T(8,128)(2,1)S(1)}, bf16[512,256]{1,0:T(8,128)(2,1)S(1)}, u32[]{:S(2)}, u32[]{:S(2)}) %collective-permute-start.13) | collective-permute-done | bytes 262176 | tf_op jit(solution)/shard_map/ppermute | solution.py:54
  105.6 30.2 %collective-permute-done.12 = bf16[512,256]{1,0:T(8,128)(2,1)S(1)} collective-permute-done((bf16[512,256]{1,0:T(8,128)(2,1)S(1)}, bf16[512,256]{1,0:T(8,128)(2,1)S(1)}, u32[]{:S(2)}, u32[]{:S(2)}) %collective-permute-start.12) | collective-permute-done | bytes 262176 | tf_op jit(solution)/shard_map/ppermute | solution.py:54
  137.4 2.8 shard_map.279
  143.5 9.5 %shard_map.276 = (bf16[512,768]{1,0:T(8,128)(2,1)S(1)}, f32[6,1,512]{2,1,0:T(1,128)S(1)}) custom-call(s32[4]{0:T(128)S(1)} %convert_add_fusion.7.flag_ref, bf16[512,768]{1,0:T(8,128)(2,1)S(1)} %copy-done.18, bf16[2048,128]{1,0:T(8,128)(2,1)S(1)} %get-tuple-element.403.k_ref, bf16[2048,128]{1,0:T(8,128)(2,1)S(1)} %get-tuple-element.402.v_ref, ...), custom_call_target="tpu_custom_call" | custom-call | tf_op jit(solution)/shard_map/pallas_call | solution.py:188
  153.1 3.4 convolution_convert_fusion.2
  158.3 7.4 %collective-permute-start.21 = (bf16[512,1536]{1,0:T(8,128)(2,1)}, bf16[512,1536]{1,0:T(8,128)(2,1)S(1)}, u32[]{:S(2)}, u32[]{:S(2)}) collective-permute-start(bf16[512,1536]{1,0:T(8,128)(2,1)} %convolution_convert_fusion.refs_0_), channel_id=1, source_target_pairs={{0,8},{8,0},{16,24},{24,16},{1,9},{9,1},{17,25},{25,17},{2,10},{10... | collective-permute-start | bytes 4718600 | tf_op jit(solution)/shard_map/ppermute | solution.py:45
  170.4 7.2 %collective-permute-done.18.refs_1_ = bf16[512,1536]{1,0:T(8,128)(2,1)} collective-permute-done((bf16[512,1536]{1,0:T(8,128)(2,1)}, bf16[512,1536]{1,0:T(8,128)(2,1)}, u32[]{:S(2)}, u32[]{:S(2)}) %collective-permute-start.18) | collective-permute-done | bytes 1572896 | tf_op jit(solution)/shard_map/ppermute | solution.py:45
  188.1 12.0 %collective-permute-done.20.refs_1_ = bf16[256,1536]{1,0:T(8,128)(2,1)S(1)} collective-permute-done((bf16[256,1536]{1,0:T(8,128)(2,1)S(1)}, bf16[256,1536]{1,0:T(8,128)(2,1)S(1)}, u32[]{:S(2)}, u32[]{:S(2)}) %collective-permute-start.20) | collective-permute-done | bytes 786464 | tf_op jit(solution)/shard_map/ppermute | solution.py:49
  203.7 9.2 %collective-permute-done.23 = bf16[128,1536]{1,0:T(8,128)(2,1)S(1)} collective-permute-done((bf16[128,1536]{1,0:T(8,128)(2,1)S(1)}, bf16[128,1536]{1,0:T(8,128)(2,1)S(1)}, u32[]{:S(2)}, u32[]{:S(2)}) %collective-permute-start.23) | collective-permute-done | bytes 393248 | tf_op jit(solution)/shard_map/ppermute | solution.py:49
  219.4 12.5 %shard_map.280 = (bf16[2048,1152]{1,0:T(8,128)(2,1)}, bf16[1024,1536]{1,0:T(8,128)(2,1)}, bf16[1024,1536]{1,0:T(8,128)(2,1)}) custom-call(bf16[2048,1536]{1,0:T(8,128)(2,1)} %bitcast.103, bf16[2048,1536]{1,0:T(8,128)(2,1)} %bitcast.110, bf16[1536,1152]{1,0:T(8,128)(2,1)} %all-gather.5.cloned.1.call-done.refs_2_), custom_call_target="tpu_custom_call" | custom-call | tf_op jit(solution)/shard_map/pallas_call | solution.py:586
  231.8 12.5 %shard_map.281 = (bf16[2048,1152]{1,0:T(8,128)(2,1)}, bf16[1024,1536]{1,0:T(8,128)(2,1)}, bf16[1024,1536]{1,0:T(8,128)(2,1)}) custom-call(bf16[2048,1536]{1,0:T(8,128)(2,1)} %bitcast.104, bf16[2048,1536]{1,0:T(8,128)(2,1)} %bitcast.111, bf16[1536,1152]{1,0:T(8,128)(2,1)} %all-gather.5.cloned.1.call-done.refs_2_, ...), custom_call_target="tpu_custom_call", output_to_operand_aliasing={{0}: (3, {})} | custom-call | tf_op jit(solution)/shard_map/pallas_call | solution.py:586
  244.3 16.6 %shard_map.282 = bf16[1536,1152]{1,0:T(8,128)(2,1)} custom-call(bf16[2048,1536]{1,0:T(8,128)(2,1)} %bitcast.105, bf16[2048,1536]{1,0:T(8,128)(2,1)} %bitcast.112, bf16[2048,1152]{1,0:T(8,128)(2,1)} %get-tuple-element.268.p_ref), custom_call_target="tpu_custom_call" | custom-call | tf_op jit(solution)/shard_map/pallas_call | solution.py:629
  261.0 8.3 %all-gather.3.cloned.1.call-done.refs_2_ = bf16[1536,2304]{1,0:T(8,128)(2,1)} async-done(((bf16[384,2304]{1,0:T(8,128)(2,1)}), bf16[1536,2304]{1,0:T(8,128)(2,1)}) %all-gather.3.cloned.1.call-update) | async-done | bytes 7077904 | tf_op jit(solution)/shard_map/all_gather | solution.py:896
  269.3 30.3 %shard_map.283 = (bf16[2048,2304]{1,0:T(8,128)(2,1)}, bf16[1024,1536]{1,0:T(8,128)(2,1)}, bf16[1024,1536]{1,0:T(8,128)(2,1)}) custom-call(bf16[2048,1536]{1,0:T(8,128)(2,1)} %bitcast.106, bf16[2048,1536]{1,0:T(8,128)(2,1)} %bitcast.113, bf16[1536,2304]{1,0:T(8,128)(2,1)} %all-gather.3.cloned.1.call-done.refs_2_, ...), custom_call_target="tpu_custom_call" | custom-call | tf_op jit(solution)/shard_map/pallas_call | solution.py:586
  299.6 22.7 %shard_map.284 = (bf16[2048,2304]{1,0:T(8,128)(2,1)}, bf16[1024,1536]{1,0:T(8,128)(2,1)}, bf16[1024,1536]{1,0:T(8,128)(2,1)}) custom-call(bf16[2048,1536]{1,0:T(8,128)(2,1)} %bitcast.107, bf16[2048,1536]{1,0:T(8,128)(2,1)} %bitcast.114, bf16[1536,2304]{1,0:T(8,128)(2,1)} %all-gather.3.cloned.1.call-done.refs_2_, ...), custom_call_target="tpu_custom_call", output_to_operand_aliasing={{0}: (5, {})} | custom-call | tf_op jit(solution)/shard_map/pallas_call | solution.py:586
  328.0 11.4 %shard_map.285 = bf16[1536,768]{1,0:T(8,128)(2,1)} custom-call(bf16[2048,1536]{1,0:T(8,128)(2,1)} %bitcast.115, bf16[2048,2304]{1,0:T(8,128)(2,1)} %get-tuple-element.288.p_ref), custom_call_target="tpu_custom_call" | custom-call | flops 4831838208 | tf_op jit(solution)/shard_map/pallas_call | solution.py:629
  345.7 11.6 %shard_map.286 = bf16[1536,768]{1,0:T(8,128)(2,1)} custom-call(bf16[2048,1536]{1,0:T(8,128)(2,1)} %bitcast.108, bf16[2048,2304]{1,0:T(8,128)(2,1)} %get-tuple-element.288.p_ref), custom_call_target="tpu_custom_call" | custom-call | flops 4831838208 | tf_op jit(solution)/shard_map/pallas_call | solution.py:629
  357.3 5.9 collective-permute-done.32
  364.3 3.5 multiply_reduce_fusion
  370.9 5.2 collective-permute-done.35
  380.0 11.4 %shard_map.287 = bf16[1536,768]{1,0:T(8,128)(2,1)} custom-call(bf16[2048,1536]{1,0:T(8,128)(2,1)} %bitcast.109, bf16[2048,2304]{1,0:T(8,128)(2,1)} %get-tuple-element.288.p_ref), custom_call_target="tpu_custom_call" | custom-call | flops 4831838208 | tf_op jit(solution)/shard_map/pallas_call | solution.py:629
  392.6 5.9 collective-permute-done.36
  398.5 3.0 copy-done.2
  401.4 3.3 shard_map.288
  407.4 3.5 add_convert_fusion.1
  415.9 13.1 %shard_map.290 = (bf16[512,768]{1,0:T(8,128)(2,1)}, bf16[2048,256]{1,0:T(8,128)(2,1)}) custom-call(s32[4]{0:T(128)} %copy-done.51, bf16[512,768]{1,0:T(8,128)(2,1)} %copy-done.17, bf16[2048,128]{1,0:T(8,128)(2,1)} %copy-done.10, bf16[2048,128]{1,0:T(8,128)(2,1)} %copy-done.9, bf16[512,768]{1,0:T(8,128)(2,1)} %copy-done.26, f32[6,1,512]{2,1,0:T(1,128)} %copy-done.48, ...), custom_call_target="tpu_custom_call" | custom-call | tf_op jit(solution)/shard_map/pallas_call | solution.py:295
  431.7 12.0 %collective-permute-done.38 = bf16[4,96,768]{2,1,0:T(8,128)(2,1)} collective-permute-done((bf16[4,96,768]{2,1,0:T(8,128)(2,1)}, bf16[4,96,768]{2,1,0:T(8,128)(2,1)}, u32[]{:S(2)}, u32[]{:S(2)}) %collective-permute-start.38) | collective-permute-done | bytes 589856 | tf_op jit(solution)/shard_map/ppermute | solution.py:45
  453.2 2.7 collective-permute-start.42
  458.6 4.3 collective-permute-done.44
  462.9 10.3 %collective-permute-done.43 = bf16[512,256]{1,0:T(8,128)(2,1)} collective-permute-done((bf16[512,256]{1,0:T(8,128)(2,1)}, bf16[512,256]{1,0:T(8,128)(2,1)}, u32[]{:S(2)}, u32[]{:S(2)}) %collective-permute-start.43) | collective-permute-done | bytes 262176 | tf_op jit(solution)/shard_map/ppermute | solution.py:54
  483.6 6.5 %collective-permute-done.45 = bf16[4,96,768]{2,1,0:T(8,128)(2,1)S(1)} collective-permute-done((bf16[4,96,768]{2,1,0:T(8,128)(2,1)S(1)}, bf16[4,96,768]{2,1,0:T(8,128)(2,1)S(1)}, u32[]{:S(2)}, u32[]{:S(2)}) %collective-permute-start.45) | collective-permute-done | bytes 589856 | tf_op jit(solution)/shard_map/ppermute | solution.py:45
  491.1 6.2 %collective-permute-start.47 = (bf16[96,1536]{1,0:T(8,128)(2,1)S(1)}, bf16[96,1536]{1,0:T(8,128)(2,1)S(1)}, u32[]{:S(2)}, u32[]{:S(2)}) collective-permute-start(bf16[96,1536]{1,0:T(8,128)(2,1)S(1)} %fusion.40), channel_id=1, source_target_pairs={{0,2},{2,4},{4,6},{6,0},{1,3},{3,5},{5,7},{7,1},{8,10},{10,12},{12... | collective-permute-start | bytes 884744 | tf_op jit(solution)/shard_map/ppermute | solution.py:54
  506.5 5.0 collective-permute-done.47
  518.5 4.0 collective-permute-start.50
  526.4 4.3 collective-permute-start.57
  531.8 2.8 collective-permute-start.55
  534.7 4.8 collective-permute-done.57
  548.7 7.3 %collective-permute-done.64.refs_2_ = bf16[96,2688]{1,0:T(8,128)(2,1)} collective-permute-done((bf16[96,2688]{1,0:T(8,128)(2,1)}, bf16[96,2688]{1,0:T(8,128)(2,1)}, u32[]{:S(2)}, u32[]{:S(2)}) %collective-permute-start.64) | collective-permute-done | bytes 516128 | tf_op jit(solution)/shard_map/ppermute | solution.py:45
  556.1 7.8 %collective-permute-done.65.refs_3_ = bf16[96,2688]{1,0:T(8,128)(2,1)} collective-permute-done((bf16[96,2688]{1,0:T(8,128)(2,1)}, bf16[96,2688]{1,0:T(8,128)(2,1)}, u32[]{:S(2)}, u32[]{:S(2)}) %collective-permute-start.65) | collective-permute-done | bytes 516128 | tf_op jit(solution)/shard_map/ppermute | solution.py:45
  569.6 5.0 collective-permute-done.67.refs_6_
  582.8 4.0 shard_map.301
  (469 shorter events, 185.2 us)
Async XLA Ops:
  7.2 212.2 %all-gather.5.cloned.1.call-start = ((), (), s32[]{:S(2)}) async-start(), calls=%async_computation.5 | async-start | bytes 4423680 | tf_op jit(solution)/shard_map/all_gather | solution.py:864
  8.3 17.2 %collective-permute-start.1 = (bf16[96,1792]{1,0:T(8,128)(2,1)S(1)}, bf16[96,1792]{1,0:T(8,128)(2,1)S(1)}, u32[]{:S(2)}, u32[]{:S(2)}) collective-permute-start(bf16[96,1792]{1,0:T(8,128)(2,1)S(1)} %pad_maximum_fusion.3.refs_0_), channel_id=1, source_target_pairs={{0,16},{8,24},{16,0},{24,8},{1,17},{9,25},{17,1},{25,9},{2,18},{10... | collective-permute-start | bytes 1032200 | tf_op jit(solution)/shard_map/ppermute | solution.py:45
  11.3 14.2 %collective-permute-start = (bf16[96,1792]{1,0:T(8,128)(2,1)S(1)}, bf16[96,1792]{1,0:T(8,128)(2,1)S(1)}, u32[]{:S(2)}, u32[]{:S(2)}) collective-permute-start(bf16[96,1792]{1,0:T(8,128)(2,1)S(1)} %pad_maximum_fusion.3.refs_0_), channel_id=1, source_target_pairs={{0,2},{2,4},{4,6},{6,0},{1,3},{3,5},{5,7},{7,1},{8,10},{10,12},{12... | collective-permute-start | bytes 1032200 | tf_op jit(solution)/shard_map/ppermute | solution.py:54
  25.5 17.0 %collective-permute-start.3 = (bf16[96,1792]{1,0:T(8,128)(2,1)S(1)}, bf16[96,1792]{1,0:T(8,128)(2,1)S(1)}, u32[]{:S(2)}, u32[]{:S(2)}) collective-permute-start(bf16[96,1792]{1,0:T(8,128)(2,1)S(1)} %collective-permute-done.refs_1_), channel_id=1, source_target_pairs={{0,16},{8,24},{16,0},{24,8},{1,17},{9,25},{17,1},{25,9},{2,18},{10... | collective-permute-start | bytes 1032200 | tf_op jit(solution)/shard_map/ppermute | solution.py:45
  26.1 17.2 %collective-permute-start.2 = (bf16[96,1792]{1,0:T(8,128)(2,1)S(1)}, bf16[96,1792]{1,0:T(8,128)(2,1)S(1)}, u32[]{:S(2)}, u32[]{:S(2)}) collective-permute-start(bf16[96,1792]{1,0:T(8,128)(2,1)S(1)} %collective-permute-done.refs_1_), channel_id=1, source_target_pairs={{0,2},{2,4},{4,6},{6,0},{1,3},{3,5},{5,7},{7,1},{8,10},{10,12},{12... | collective-permute-start | bytes 1032200 | tf_op jit(solution)/shard_map/ppermute | solution.py:54
  27.7 13.6 %collective-permute-start.5 = (bf16[96,1152]{1,0:T(8,128)(2,1)S(1)}, bf16[96,1152]{1,0:T(8,128)(2,1)S(1)}, u32[]{:S(2)}, u32[]{:S(2)}) collective-permute-start(bf16[96,1152]{1,0:T(8,128)(2,1)S(1)} %get-tuple-element.209), channel_id=1, source_target_pairs={{0,16},{8,24},{16,0},{24,8},{1,17},{9,25},{17,1},{25,9},{2,18},{10... | collective-permute-start | bytes 663560 | tf_op jit(solution)/shard_map/ppermute | solution.py:45
  48.8 220.5 %all-gather.3.cloned.1.call-start = ((), (), s32[]{:S(2)}) async-start(), calls=%async_computation.4 | async-start | bytes 8847360 | tf_op jit(solution)/shard_map/all_gather | solution.py:896
  83.8 19.6 %collective-permute-start.13 = (bf16[512,256]{1,0:T(8,128)(2,1)S(1)}, bf16[512,256]{1,0:T(8,128)(2,1)S(1)}, u32[]{:S(2)}, u32[]{:S(2)}) collective-permute-start(bf16[512,256]{1,0:T(8,128)(2,1)S(1)} %get-tuple-element.242), channel_id=1, source_target_pairs={{0,6},{2,0},{4,2},{6,4},{1,7},{3,1},{5,3},{7,5},{8,14},{10,8},{12,... | collective-permute-start | bytes 786440 | tf_op jit(solution)/shard_map/ppermute | solution.py:54
  84.3 51.4 %collective-permute-start.12 = (bf16[512,256]{1,0:T(8,128)(2,1)S(1)}, bf16[512,256]{1,0:T(8,128)(2,1)S(1)}, u32[]{:S(2)}, u32[]{:S(2)}) collective-permute-start(bf16[512,256]{1,0:T(8,128)(2,1)S(1)} %get-tuple-element.242), channel_id=1, source_target_pairs={{0,4},{2,6},{4,0},{6,2},{1,5},{3,7},{5,1},{7,3},{8,12},{10,14},{12... | collective-permute-start | bytes 786440 | tf_op jit(solution)/shard_map/ppermute | solution.py:54
  85.0 50.7 %collective-permute-start.11 = (bf16[512,256]{1,0:T(8,128)(2,1)S(1)}, bf16[512,256]{1,0:T(8,128)(2,1)S(1)}, u32[]{:S(2)}, u32[]{:S(2)}) collective-permute-start(bf16[512,256]{1,0:T(8,128)(2,1)S(1)} %get-tuple-element.242), channel_id=1, source_target_pairs={{0,2},{2,4},{4,6},{6,0},{1,3},{3,5},{5,7},{7,1},{8,10},{10,12},{12... | collective-permute-start | bytes 786440 | tf_op jit(solution)/shard_map/ppermute | solution.py:54
  89.6 46.1 %collective-permute-start.14 = (bf16[96,2304]{1,0:T(8,128)(2,1)}, bf16[96,2304]{1,0:T(8,128)(2,1)S(1)}, u32[]{:S(2)}, u32[]{:S(2)}) collective-permute-start(bf16[96,2304]{1,0:T(8,128)(2,1)} %copy-done.57), channel_id=1, source_target_pairs={{0,8},{8,0},{16,24},{24,16},{1,9},{9,1},{17,25},{25,17},{2,10},{10... | collective-permute-start | bytes 1327112 | tf_op jit(solution)/shard_map/ppermute | solution.py:45
  89.7 46.0 %collective-permute-start.15 = (bf16[96,2304]{1,0:T(8,128)(2,1)}, bf16[96,2304]{1,0:T(8,128)(2,1)S(1)}, u32[]{:S(2)}, u32[]{:S(2)}) collective-permute-start(bf16[96,2304]{1,0:T(8,128)(2,1)} %copy-done.56), channel_id=1, source_target_pairs={{0,16},{8,24},{16,0},{24,8},{1,17},{9,25},{17,1},{25,9},{2,18},{10... | collective-permute-start | bytes 1327112 | tf_op jit(solution)/shard_map/ppermute | solution.py:45
  103.4 32.4 %collective-permute-start.16 = (bf16[96,2304]{1,0:T(8,128)(2,1)}, bf16[96,2304]{1,0:T(8,128)(2,1)S(1)}, u32[]{:S(2)}, u32[]{:S(2)}) collective-permute-start(bf16[96,2304]{1,0:T(8,128)(2,1)} %copy-done.55), channel_id=1, source_target_pairs={{0,24},{8,16},{16,8},{24,0},{1,25},{9,17},{17,9},{25,1},{2,26},{10... | collective-permute-start | bytes 1327112 | tf_op jit(solution)/shard_map/ppermute | solution.py:45
  140.3 217.1 %reduce-scatter.5.cloned.1.call-start = ((), (), s32[]{:S(2)}) async-start(), calls=%async_computation.6 | async-start | bytes 4423680 | tf_op jit(solution)/shard_map/reduce_scatter | solution.py:927
  140.7 36.9 %collective-permute-start.18 = (bf16[512,1536]{1,0:T(8,128)(2,1)}, bf16[512,1536]{1,0:T(8,128)(2,1)}, u32[]{:S(2)}, u32[]{:S(2)}) collective-permute-start(bf16[512,1536]{1,0:T(8,128)(2,1)} %convolution_convert_fusion.refs_0_), channel_id=1, source_target_pairs={{0,16},{8,24},{16,0},{24,8},{1,17},{9,25},{17,1},{25,9},{2,18},{10... | collective-permute-start | bytes 4718600 | tf_op jit(solution)/shard_map/ppermute | solution.py:45
  156.5 13.9 %collective-permute-start.17 = (bf16[256,1536]{1,0:T(8,128)(2,1)}, bf16[256,1536]{1,0:T(8,128)(2,1)S(1)}, u32[]{:S(2)}, u32[]{:S(2)}) collective-permute-start(bf16[256,1536]{1,0:T(8,128)(2,1)} %convolution_convert_fusion.2), channel_id=1, source_target_pairs={{0,1},{1,0},{2,3},{3,2},{4,5},{5,4},{6,7},{7,6},{8,9},{9,8},{10,11... | collective-permute-start | bytes 2359304 | tf_op jit(solution)/shard_map/ppermute | solution.py:49
  158.3 24.5 %collective-permute-start.21 = (bf16[512,1536]{1,0:T(8,128)(2,1)}, bf16[512,1536]{1,0:T(8,128)(2,1)S(1)}, u32[]{:S(2)}, u32[]{:S(2)}) collective-permute-start(bf16[512,1536]{1,0:T(8,128)(2,1)} %convolution_convert_fusion.refs_0_), channel_id=1, source_target_pairs={{0,8},{8,0},{16,24},{24,16},{1,9},{9,1},{17,25},{25,17},{2,10},{10... | collective-permute-start | bytes 4718600 | tf_op jit(solution)/shard_map/ppermute | solution.py:45
  180.0 20.0 %collective-permute-start.20 = (bf16[256,1536]{1,0:T(8,128)(2,1)S(1)}, bf16[256,1536]{1,0:T(8,128)(2,1)S(1)}, u32[]{:S(2)}, u32[]{:S(2)}) collective-permute-start(bf16[256,1536]{1,0:T(8,128)(2,1)S(1)} %multiply_convert_fusion.refs_0_), channel_id=1, source_target_pairs={{0,1},{1,0},{2,3},{3,2},{4,5},{5,4},{6,7},{7,6},{8,9},{9,8},{10,11... | collective-permute-start | bytes 2359304 | tf_op jit(solution)/shard_map/ppermute | solution.py:49
  181.6 19.7 %collective-permute-start.19 = (bf16[256,1536]{1,0:T(8,128)(2,1)S(1)}, bf16[256,1536]{1,0:T(8,128)(2,1)S(1)}, u32[]{:S(2)}, u32[]{:S(2)}) collective-permute-start(bf16[256,1536]{1,0:T(8,128)(2,1)S(1)} %multiply_convert_fusion.refs_0_), channel_id=1, source_target_pairs={{0,16},{8,24},{16,0},{24,8},{1,17},{9,25},{17,1},{25,9},{2,18},{10... | collective-permute-start | bytes 2359304 | tf_op jit(solution)/shard_map/ppermute | solution.py:45
  182.9 20.8 %collective-permute-start.25 = (bf16[256,1536]{1,0:T(8,128)(2,1)S(1)}, bf16[256,1536]{1,0:T(8,128)(2,1)S(1)}, u32[]{:S(2)}, u32[]{:S(2)}) collective-permute-start(bf16[256,1536]{1,0:T(8,128)(2,1)S(1)} %multiply_convert_fusion.refs_0_), channel_id=1, source_target_pairs={{0,8},{8,0},{16,24},{24,16},{1,9},{9,1},{17,25},{25,17},{2,10},{10... | collective-permute-start | bytes 2359304 | tf_op jit(solution)/shard_map/ppermute | solution.py:45
  261.0 131.6 %reduce-scatter.7.cloned.1.call-start = ((), (), s32[]{:S(2)}) async-start(), calls=%async_computation.7 | async-start | bytes 2949120 | tf_op jit(solution)/shard_map/reduce_scatter | solution.py:935
  299.6 22.7 %collective-permute-start.29 = (bf16[1024,1536]{1,0:T(8,128)(2,1)}, bf16[1024,1536]{1,0:T(8,128)(2,1)S(1)}, u32[]{:S(2)}, u32[]{:S(2)}) collective-permute-start(bf16[1024,1536]{1,0:T(8,128)(2,1)} %get-tuple-element.272), channel_id=1, source_target_pairs={{0,8},{8,0},{16,24},{24,16},{1,9},{9,1},{17,25},{25,17},{2,10},{10... | collective-permute-start | bytes 9437192 | tf_op jit(solution)/shard_map/ppermute | solution.py:45
  325.0 15.1 %collective-permute-start.30 = (bf16[128,1536]{1,0:T(8,128)(2,1)S(1)}, bf16[128,1536]{1,0:T(8,128)(2,1)}, u32[]{:S(2)}, u32[]{:S(2)}) collective-permute-start(bf16[128,1536]{1,0:T(8,128)(2,1)S(1)} %get-tuple-element.405), channel_id=1, source_target_pairs={{0,16},{8,24},{16,0},{24,8},{1,17},{9,25},{17,1},{25,9},{2,18},{10... | collective-permute-start | bytes 1179656 | tf_op jit(solution)/shard_map/ppermute | solution.py:45
  343.6 19.6 %collective-permute-start.32 = (bf16[256,1536]{1,0:T(8,128)(2,1)}, bf16[256,1536]{1,0:T(8,128)(2,1)}, u32[]{:S(2)}, u32[]{:S(2)}) collective-permute-start(bf16[256,1536]{1,0:T(8,128)(2,1)} %pad_maximum_fusion.1), channel_id=1, source_target_pairs={{0,16},{8,24},{16,0},{24,8},{1,17},{9,25},{17,1},{25,9},{2,18},{10... | collective-permute-start | bytes 2359304 | tf_op jit(solution)/shard_map/ppermute | solution.py:45
  345.1 19.2 %collective-permute-start.33 = (bf16[256,1536]{1,0:T(8,128)(2,1)}, bf16[256,1536]{1,0:T(8,128)(2,1)S(1)}, u32[]{:S(2)}, u32[]{:S(2)}) collective-permute-start(bf16[256,1536]{1,0:T(8,128)(2,1)} %pad_maximum_fusion.2), channel_id=1, source_target_pairs={{0,1},{1,0},{2,3},{3,2},{4,5},{5,4},{6,7},{7,6},{8,9},{9,8},{10,11... | collective-permute-start | bytes 2359304 | tf_op jit(solution)/shard_map/ppermute | solution.py:49
  345.7 112.9 %reduce-scatter.9.cloned.1.call-start = ((), (), s32[]{:S(2)}) async-start(), calls=%async_computation.8 | async-start | bytes 2949120 | tf_op jit(solution)/shard_map/reduce_scatter | solution.py:935
  370.1 21.3 %collective-permute-start.34 = (bf16[256,1536]{1,0:T(8,128)(2,1)S(1)}, bf16[256,1536]{1,0:T(8,128)(2,1)}, u32[]{:S(2)}, u32[]{:S(2)}) collective-permute-start(bf16[256,1536]{1,0:T(8,128)(2,1)S(1)} %fusion.78.own_ref), channel_id=1, source_target_pairs={{0,1},{1,0},{2,3},{3,2},{4,5},{5,4},{6,7},{7,6},{8,9},{9,8},{10,11... | collective-permute-start | bytes 2359304 | tf_op jit(solution)/shard_map/ppermute | solution.py:49
  370.8 172.3 %reduce-scatter.11.cloned.1.call-start = ((), (), s32[]{:S(2)}) async-start(), calls=%async_computation.9 | async-start | bytes 2949120 | tf_op jit(solution)/shard_map/reduce_scatter | solution.py:935
  378.6 19.9 %collective-permute-start.36 = (bf16[256,1536]{1,0:T(8,128)(2,1)}, bf16[256,1536]{1,0:T(8,128)(2,1)}, u32[]{:S(2)}, u32[]{:S(2)}) collective-permute-start(bf16[256,1536]{1,0:T(8,128)(2,1)} %add_convert_fusion.3), channel_id=1, source_target_pairs={{0,16},{8,24},{16,0},{24,8},{1,17},{9,25},{17,1},{25,9},{2,18},{10... | collective-permute-start | bytes 2359304 | tf_op jit(solution)/shard_map/ppermute | solution.py:45
  410.9 20.2 %collective-permute-start.40 = (bf16[256,1536]{1,0:T(8,128)(2,1)}, bf16[256,1536]{1,0:T(8,128)(2,1)S(1)}, u32[]{:S(2)}, u32[]{:S(2)}) collective-permute-start(bf16[256,1536]{1,0:T(8,128)(2,1)} %get-tuple-element.384), channel_id=1, source_target_pairs={{0,1},{1,0},{2,3},{3,2},{4,5},{5,4},{6,7},{7,6},{8,9},{9,8},{10,11... | collective-permute-start | bytes 2359304 | tf_op jit(solution)/shard_map/ppermute | solution.py:49
  411.3 20.4 %collective-permute-start.39 = (bf16[256,1536]{1,0:T(8,128)(2,1)S(1)}, bf16[256,1536]{1,0:T(8,128)(2,1)S(1)}, u32[]{:S(2)}, u32[]{:S(2)}) collective-permute-start(bf16[256,1536]{1,0:T(8,128)(2,1)S(1)} %get-tuple-element.385), channel_id=1, source_target_pairs={{0,16},{8,24},{16,0},{24,8},{1,17},{9,25},{17,1},{25,9},{2,18},{10... | collective-permute-start | bytes 2359304 | tf_op jit(solution)/shard_map/ppermute | solution.py:45
  415.2 28.4 %collective-permute-start.38 = (bf16[4,96,768]{2,1,0:T(8,128)(2,1)}, bf16[4,96,768]{2,1,0:T(8,128)(2,1)}, u32[]{:S(2)}, u32[]{:S(2)}) collective-permute-start(bf16[4,96,768]{2,1,0:T(8,128)(2,1)} %fusion.23), channel_id=1, source_target_pairs={{0,16},{8,24},{16,0},{24,8},{1,17},{9,25},{17,1},{25,9},{2,18},{10... | collective-permute-start | bytes 1769480 | tf_op jit(solution)/shard_map/ppermute | solution.py:45
  448.4 24.9 %collective-permute-start.41 = (bf16[4,192,768]{2,1,0:T(8,128)(2,1)}, bf16[4,192,768]{2,1,0:T(8,128)(2,1)}, u32[]{:S(2)}, u32[]{:S(2)}) collective-permute-start(bf16[4,192,768]{2,1,0:T(8,128)(2,1)} %get-tuple-element.306), channel_id=1, source_target_pairs={{0,8},{8,0},{16,24},{24,16},{1,9},{9,1},{17,25},{25,17},{2,10},{10... | collective-permute-start | bytes 3538952 | tf_op jit(solution)/shard_map/ppermute | solution.py:45
  451.7 21.6 %collective-permute-start.43 = (bf16[512,256]{1,0:T(8,128)(2,1)}, bf16[512,256]{1,0:T(8,128)(2,1)}, u32[]{:S(2)}, u32[]{:S(2)}) collective-permute-start(bf16[512,256]{1,0:T(8,128)(2,1)} %get-tuple-element.400), channel_id=1, source_target_pairs={{0,4},{2,6},{4,0},{6,2},{1,5},{3,7},{5,1},{7,3},{8,12},{10,14},{12... | collective-permute-start | bytes 786440 | tf_op jit(solution)/shard_map/ppermute | solution.py:54
  453.2 20.0 %collective-permute-start.42 = (bf16[512,256]{1,0:T(8,128)(2,1)}, bf16[512,256]{1,0:T(8,128)(2,1)}, u32[]{:S(2)}, u32[]{:S(2)}) collective-permute-start(bf16[512,256]{1,0:T(8,128)(2,1)} %get-tuple-element.401), channel_id=1, source_target_pairs={{0,6},{2,0},{4,2},{6,4},{1,7},{3,1},{5,3},{7,5},{8,14},{10,8},{12,... | collective-permute-start | bytes 786440 | tf_op jit(solution)/shard_map/ppermute | solution.py:54
  475.4 14.6 %collective-permute-start.45 = (bf16[4,96,768]{2,1,0:T(8,128)(2,1)S(1)}, bf16[4,96,768]{2,1,0:T(8,128)(2,1)S(1)}, u32[]{:S(2)}, u32[]{:S(2)}) collective-permute-start(bf16[4,96,768]{2,1,0:T(8,128)(2,1)S(1)} %fusion.24), channel_id=1, source_target_pairs={{0,16},{8,24},{16,0},{24,8},{1,17},{9,25},{17,1},{25,9},{2,18},{10... | collective-permute-start | bytes 1769480 | tf_op jit(solution)/shard_map/ppermute | solution.py:45
  481.9 24.6 %collective-permute-start.49 = (bf16[256,1536]{1,0:T(8,128)(2,1)S(1)}, bf16[256,1536]{1,0:T(8,128)(2,1)S(1)}, u32[]{:S(2)}, u32[]{:S(2)}) collective-permute-start(bf16[256,1536]{1,0:T(8,128)(2,1)S(1)} %shard_map.293), channel_id=1, source_target_pairs={{0,1},{1,0},{2,3},{3,2},{4,5},{5,4},{6,7},{7,6},{8,9},{9,8},{10,11... | collective-permute-start | bytes 2359304 | tf_op jit(solution)/shard_map/ppermute | solution.py:49
  491.1 20.4 %collective-permute-start.47 = (bf16[96,1536]{1,0:T(8,128)(2,1)S(1)}, bf16[96,1536]{1,0:T(8,128)(2,1)S(1)}, u32[]{:S(2)}, u32[]{:S(2)}) collective-permute-start(bf16[96,1536]{1,0:T(8,128)(2,1)S(1)} %fusion.40), channel_id=1, source_target_pairs={{0,2},{2,4},{4,6},{6,0},{1,3},{3,5},{5,7},{7,1},{8,10},{10,12},{12... | collective-permute-start | bytes 884744 | tf_op jit(solution)/shard_map/ppermute | solution.py:54
  512.1 14.3 %collective-permute-start.52 = (f32[4096]{0:T(1024)S(1)}, f32[4096]{0:T(1024)S(1)}, u32[]{:S(2)}, u32[]{:S(2)}) collective-permute-start(f32[4096]{0:T(1024)S(1)} %pad_maximum_fusion.7), channel_id=1, source_target_pairs={{0,16},{8,24},{16,0},{24,8},{1,17},{9,25},{17,1},{25,9},{2,18},{10... | collective-permute-start | bytes 49160 | tf_op jit(solution)/shard_map/ppermute | solution.py:1044
  513.7 17.0 %collective-permute-start.53 = (f32[4096]{0:T(1024)S(1)}, f32[4096]{0:T(1024)S(1)}, u32[]{:S(2)}, u32[]{:S(2)}) collective-permute-start(f32[4096]{0:T(1024)S(1)} %pad_maximum_fusion.7), channel_id=1, source_target_pairs={{0,24},{8,0},{16,8},{24,16},{1,25},{9,1},{17,9},{25,17},{2,26},{10... | collective-permute-start | bytes 49160 | tf_op jit(solution)/shard_map/ppermute | solution.py:1044
  513.7 18.1 %collective-permute-start.51 = (f32[4096]{0:T(1024)S(1)}, f32[4096]{0:T(1024)S(1)}, u32[]{:S(2)}, u32[]{:S(2)}) collective-permute-start(f32[4096]{0:T(1024)S(1)} %pad_maximum_fusion.7), channel_id=1, source_target_pairs={{0,8},{8,16},{16,24},{24,0},{1,9},{9,17},{17,25},{25,1},{2,10},{10... | collective-permute-start | bytes 49160 | tf_op jit(solution)/shard_map/ppermute | solution.py:1044
  514.2 28.8 %collective-permute-start.54 = (bf16[256,1536]{1,0:T(8,128)(2,1)S(1)}, bf16[256,1536]{1,0:T(8,128)(2,1)S(1)}, u32[]{:S(2)}, u32[]{:S(2)}) collective-permute-start(bf16[256,1536]{1,0:T(8,128)(2,1)S(1)} %shard_map.295.own_ref), channel_id=1, source_target_pairs={{0,1},{1,0},{2,3},{3,2},{4,5},{5,4},{6,7},{7,6},{8,9},{9,8},{10,11... | collective-permute-start | bytes 2359304 | tf_op jit(solution)/shard_map/ppermute | solution.py:49
  518.5 23.6 %collective-permute-start.50 = (bf16[96,1536]{1,0:T(8,128)(2,1)S(1)}, bf16[96,1536]{1,0:T(8,128)(2,1)S(1)}, u32[]{:S(2)}, u32[]{:S(2)}) collective-permute-start(bf16[96,1536]{1,0:T(8,128)(2,1)S(1)} %fusion.33), channel_id=1, source_target_pairs={{0,2},{2,4},{4,6},{6,0},{1,3},{3,5},{5,7},{7,1},{8,10},{10,12},{12... | collective-permute-start | bytes 884744 | tf_op jit(solution)/shard_map/ppermute | solution.py:54
  541.0 15.0 %collective-permute-start.64 = (bf16[96,2688]{1,0:T(8,128)(2,1)}, bf16[96,2688]{1,0:T(8,128)(2,1)}, u32[]{:S(2)}, u32[]{:S(2)}) collective-permute-start(bf16[96,2688]{1,0:T(8,128)(2,1)} %get-tuple-element.341), channel_id=1, source_target_pairs={{0,16},{8,24},{16,0},{24,8},{1,17},{9,25},{17,1},{25,9},{2,18},{10... | collective-permute-start | bytes 1548296 | tf_op jit(solution)/shard_map/ppermute | solution.py:45
  542.1 21.8 %collective-permute-start.65 = (bf16[96,2688]{1,0:T(8,128)(2,1)}, bf16[96,2688]{1,0:T(8,128)(2,1)}, u32[]{:S(2)}, u32[]{:S(2)}) collective-permute-start(bf16[96,2688]{1,0:T(8,128)(2,1)} %get-tuple-element.342), channel_id=1, source_target_pairs={{0,24},{8,16},{16,8},{24,0},{1,25},{9,17},{17,9},{25,1},{2,26},{10... | collective-permute-start | bytes 1548296 | tf_op jit(solution)/shard_map/ppermute | solution.py:45
  542.2 27.5 %collective-permute-start.62 = (bf16[256,1536]{1,0:T(8,128)(2,1)S(1)}, bf16[256,1536]{1,0:T(8,128)(2,1)}, u32[]{:S(2)}, u32[]{:S(2)}) collective-permute-start(bf16[256,1536]{1,0:T(8,128)(2,1)S(1)} %shard_map.297.own_ref), channel_id=1, source_target_pairs={{0,1},{1,0},{2,3},{3,2},{4,5},{5,4},{6,7},{7,6},{8,9},{9,8},{10,11... | collective-permute-start | bytes 2359304 | tf_op jit(solution)/shard_map/ppermute | solution.py:49
  543.1 24.5 %collective-permute-start.61 = (f32[4096]{0:T(1024)S(1)}, f32[4096]{0:T(1024)S(1)}, u32[]{:S(2)}, u32[]{:S(2)}) collective-permute-start(f32[4096]{0:T(1024)S(1)} %add_add_fusion.1), channel_id=1, source_target_pairs={{0,6},{2,0},{4,2},{6,4},{1,7},{3,1},{5,3},{7,5},{8,14},{10,8},{12,... | collective-permute-start | bytes 49160 | tf_op jit(solution)/shard_map/ppermute | solution.py:1044
  548.3 19.6 %collective-permute-start.60 = (f32[4096]{0:T(1024)S(1)}, f32[4096]{0:T(1024)S(1)}, u32[]{:S(2)}, u32[]{:S(2)}) collective-permute-start(f32[4096]{0:T(1024)S(1)} %add_add_fusion.1), channel_id=1, source_target_pairs={{0,4},{2,6},{4,0},{6,2},{1,5},{3,7},{5,1},{7,3},{8,12},{10,14},{12... | collective-permute-start | bytes 49160 | tf_op jit(solution)/shard_map/ppermute | solution.py:1044
  (130 other events, 1207.4 us)
Sparse Core Ops, SparseCore 0:
  49.0 91.9 all-gather.4
  142.5 126.7 all-gather.2
  271.6 64.5 reduce-scatter.4
  345.8 46.7 reduce-scatter.6
  394.8 47.5 reduce-scatter.8
  473.4 60.4 reduce-scatter.10
